TPU v7x, 32 devices: a whole 2x2x4 slice. The times are simulated.
32 devices in a mesh: side: 2 (over y), dev: 16 (over z, x, core).
Axes of the slice: x: 2, y: 2, z: 4, core: 2. Of those that a mesh axis runs over, the one named last changes fastest.
Arguments:
- queries: bfloat16 [512, 8192], P('dev', 'side'), may hold values from -6 to 6
- cache_keys: bfloat16 [512, 256, 512], P('dev', None, 'side'), may hold values from -6 to 6
- cache_values: bfloat16 [512, 256, 512], P('dev', None, 'side'), may hold values from -6 to 6
- new_key: bfloat16 [512, 512], P('dev', 'side'), may hold values from -15 to 15
- new_value: bfloat16 [512, 512], P('dev', 'side'), may hold values from -6 to 6
- cache_lengths: int32 [512], P('dev'), may hold values from 2 to 256, as said below
- hidden: bfloat16 [512, 4096], P('dev'), may hold values from -6 to 6
- norm_gain: bfloat16 [4096], replicated, may hold values from 0.099609375 to 1.8984375
- expert_ids: int32 [512, 8], P('dev'), may hold values from 0 to 15, all different within a row; in each aligned block of 32 rows (0 to 31, 32 to 63, ...) at most 32 rows name the same one
- router_probs: float32 [512, 8], P('dev'), may hold values from 0.02 to 1
- w_gate: bfloat16 [16, 4096, 1536], P('dev', None, 'side'), may hold values from -0.09375 to 0.09375
- w_up: bfloat16 [16, 4096, 1536], P('dev', None, 'side'), may hold values from -0.09375 to 0.09375
- w_down: bfloat16 [16, 1536, 4096], P('dev', 'side'), may hold values from -0.15625 to 0.15625
Outputs:
- context: bfloat16 [512, 8192], P('dev', 'side')
- moe_out: bfloat16 [512, 4096], P('dev')
Inputs may be any that keep to these rules, and one draw needn't show every extreme that they name: `expert_ids`: in each aligned block of 32 rows (the rows of one dev index) no expert is named more than 32 times, a bound that some block reaches. `cache_lengths`: every aligned block of 32 tokens holds a token with 256 valid positions.
All inputs are finite; a program needn't handle non-finite values.
Results may differ from a plain program's by a relative error of at most 0.012.
Values may be sent and summed in bfloat16 or wider, within the bound.
No kernel may reach another device: no remote copies, remote signals or barrier semaphores. Data moves between devices by JAX's collectives and lax.ppermute only.
A program may use at most 128 MiB of HBM per device.

v0:
```python
import jax
import jax.numpy as jnp
from jax import lax
from jax.sharding import PartitionSpec as P

HEADS = 64
KV_HEADS = 4
HEAD_DIM = 128


def route_onehot(block_ids, expert_count, capacity):
    flat_ids = block_ids.reshape(-1)
    expert_hot = (flat_ids[:, None] == jnp.arange(expert_count, dtype=jnp.int32)[None, :]).astype(
        jnp.int32
    )
    earlier = jnp.cumsum(expert_hot, axis=0) - expert_hot
    slot_rank = jnp.sum(earlier * expert_hot, axis=1)
    slot_hot = (slot_rank[:, None] == jnp.arange(capacity, dtype=jnp.int32)[None, :]).astype(
        jnp.float32
    )
    route_hot = expert_hot.astype(jnp.float32)[:, :, None] * slot_hot[:, None, :]
    return route_hot.reshape(block_ids.shape[0], block_ids.shape[1], expert_count, capacity)


def attend_local(queries, cache_keys, cache_values, new_key, new_value, cache_lengths):
    row_count = queries.shape[0]
    cache_len = cache_keys.shape[1]
    groups = cache_keys.shape[2] // HEAD_DIM
    per_group = HEADS // KV_HEADS
    score_scale = HEAD_DIM ** (-0.5)
    query_heads = queries.reshape(row_count, groups, per_group, HEAD_DIM)
    key_heads = cache_keys.reshape(row_count, cache_len, groups, HEAD_DIM)
    value_heads = cache_values.reshape(row_count, cache_len, groups, HEAD_DIM)
    scores = (
        jnp.einsum("tgqd,tlgd->tgql", query_heads, key_heads, preferred_element_type=jnp.float32)
        * score_scale
    )
    own_key = new_key.reshape(row_count, groups, HEAD_DIM)
    own_score = (
        jnp.einsum("tgqd,tgd->tgq", query_heads, own_key, preferred_element_type=jnp.float32)
        * score_scale
    )
    visible = jnp.arange(cache_len, dtype=jnp.int32)[None, :] < cache_lengths[:, None]
    scores = jnp.where(visible[:, None, None, :], scores, -1e30)
    top_score = jnp.maximum(jnp.max(scores, axis=3), own_score)
    exp_scores = jnp.exp(scores - top_score[..., None])
    own_exp = jnp.exp(own_score - top_score)
    denominator = jnp.sum(exp_scores, axis=3) + own_exp
    attn_weights = (exp_scores / denominator[..., None]).astype(jnp.bfloat16)
    own_prob = (own_exp / denominator).astype(jnp.bfloat16)
    combined = jnp.einsum(
        "tgql,tlgd->tgqd", attn_weights, value_heads, preferred_element_type=jnp.float32
    )
    own_value = new_value.reshape(row_count, groups, 1, HEAD_DIM).astype(jnp.float32)
    combined = combined + own_prob.astype(jnp.float32)[..., None] * own_value
    return combined.reshape(row_count, groups * per_group * HEAD_DIM).astype(jnp.bfloat16)


def per_device(
    queries,
    cache_keys,
    cache_values,
    new_key,
    new_value,
    cache_lengths,
    hidden,
    norm_gain,
    expert_ids,
    router_probs,
    w_gate,
    w_up,
    w_down,
):
    context = attend_local(queries, cache_keys, cache_values, new_key, new_value, cache_lengths)
    row_count = hidden.shape[0]
    top_count = expert_ids.shape[1]
    devices = lax.axis_size("dev")
    experts = w_gate.shape[0] * devices
    capacity = max(2, 2 * row_count * top_count // experts)
    gate_share = router_probs / jnp.sum(router_probs, axis=1, keepdims=True)
    hidden_wide = hidden.astype(jnp.float32)
    inverse = lax.rsqrt(jnp.mean(hidden_wide * hidden_wide, axis=1, keepdims=True) + 1e-06)
    normed = (hidden_wide * inverse * norm_gain.astype(jnp.float32)[None, :]).astype(jnp.bfloat16)
    route_hot = route_onehot(expert_ids, experts, capacity)
    slot_hot = jnp.sum(route_hot, axis=1)
    slot_gate = jnp.sum(route_hot * gate_share[:, :, None, None], axis=1)
    buffer = jnp.einsum(
        "rec,rd->ecd", slot_hot.astype(jnp.bfloat16), normed, preferred_element_type=jnp.float32
    ).astype(jnp.bfloat16)
    row_block = lax.all_to_all(buffer, "dev", split_axis=0, concat_axis=0, tiled=True)
    gate_act = jnp.einsum("scd,df->scf", row_block, w_gate[0], preferred_element_type=jnp.float32)
    up_act = jnp.einsum("scd,df->scf", row_block, w_up[0], preferred_element_type=jnp.float32)
    activation = (jax.nn.silu(gate_act) * up_act).astype(jnp.bfloat16)
    partial_out = jnp.einsum(
        "scf,fd->scd", activation, w_down[0], preferred_element_type=jnp.float32
    ).astype(jnp.bfloat16)
    back = lax.all_to_all(partial_out, "dev", split_axis=0, concat_axis=0, tiled=True)
    local_mix = jnp.einsum(
        "rec,ecd->rd", slot_gate, back.astype(jnp.float32), precision=lax.Precision.HIGHEST
    )
    combined = lax.psum(local_mix, "side")
    return (context, combined.astype(jnp.bfloat16))


def solution(mesh):
    in_specs = (
        P("dev", "side"),
        P("dev", None, "side"),
        P("dev", None, "side"),
        P("dev", "side"),
        P("dev", "side"),
        P("dev"),
        P("dev", None),
        P(),
        P("dev", None),
        P("dev", None),
        P("dev", None, "side"),
        P("dev", None, "side"),
        P("dev", "side", None),
    )
    out_specs = (P("dev", "side"), P("dev", None))
    return jax.shard_map(
        per_device, mesh=mesh, in_specs=in_specs, out_specs=out_specs, check_vma=False
    )
```

profile of v0, /device:TPU:10, one launch (start us, length us, event | category | flops | bytes accessed | tf_op | source)
XLA Modules:
  0.0 251.7 jit_solution(1724913784163249886)
XLA Ops:
  0.6 0.8 copy.28
  1.4 0.1 eq.61
  1.5 0.1 eq.57
  1.6 0.1 convert_convert_fusion
  1.7 1.1 fusion.34
  2.8 0.7 reduce_sum.56
  3.5 0.7 broadcast_divide_fusion
  4.2 0.1 copy.32
  4.3 0.6 reduce-window.6
  4.9 0.2 slice_reduce_fusion
  5.1 0.1 fusion.48
  5.2 0.1 eq.65
  5.3 0.7 convert_element_type.92
  6.0 0.1 fusion.45
  6.1 1.1 fusion.15
  7.2 0.0 slice-start
  7.2 2.4 convolution_convert_fusion
  9.6 0.0 slice-start.1
  9.6 98.3 %all_to_all.10 = bf16[16,32,4096]{2,1,0:T(8,128)(2,1)S(1)} all-to-all(bf16[16,32,4096]{2,1,0:T(8,128)(2,1)S(1)} %convolution_convert_fusion), channel_id=1, replica_groups=mesh['side'=2,'dev'=16] {'dev'}, dimensions={0} | all-to-all | bytes 8388608 | tf_op jit(solution)/shard_map/all_to_all | solution.py:90
  107.9 0.0 copy-start
  107.9 2.0 copy-done
  109.8 0.0 slice-done
  109.8 0.0 slice-done.1
  109.8 3.4 %fusion.4 = f32[16,32,768]{2,1,0:T(8,128)S(1)} fusion(bf16[16,32,4096]{2,1,0:T(8,128)(2,1)S(1)} %all_to_all.10, bf16[1,4096,768]{2,1,0:T(8,128)(2,1)S(1)} %bitcast.90), kind=kOutput, calls=%fused_computation.4 | convolution fusion | flops 3221225472 | bytes 12058624 | tf_op jit(solution)/shard_map/scd,df->scf/dot_general | solution.py:91
  113.3 16.5 %fusion.6 = bf16[16,32,4096]{2,1,0:T(8,128)(2,1)} fusion(bf16[1,768,4096]{2,1,0:T(8,128)(2,1)} %param.25, f32[16,32,768]{2,1,0:T(8,128)S(1)} %fusion.4, bf16[16,32,4096]{2,1,0:T(8,128)(2,1)} %copy-done, bf16[1,4096,768]{2,1,0:T(8,128)(2,1)} %param.24), kind=kOutput, calls=%fused_computation.6 | convolution fusion | flops 6446907392 | bytes 22544384 | tf_op jit(solution)/shard_map/scf,fd->scd/dot_general | solution.py:94
  129.8 0.0 copy-start.2
  129.8 0.0 copy-start.3
  129.8 0.0 copy-start.1
  129.8 0.0 copy-start.4
  129.8 5.6 %all-to-all-start.1 = ((bf16[16,32,4096]{2,1,0:T(8,128)(2,1)}), bf16[16,32,4096]{2,1,0:T(8,128)(2,1)}, u32[]{:S(2)}, u32[]{:S(2)}) async-start(bf16[16,32,4096]{2,1,0:T(8,128)(2,1)} %fusion.6), calls=%async_computation.1 | async-start | bytes 8388608 | tf_op jit(solution)/shard_map/all_to_all | solution.py:97
  135.4 0.0 copy-done.2
  135.5 0.0 copy-done.3
  135.5 0.0 copy-start.5
  135.5 0.0 copy-done.1
  135.6 0.0 copy-done.4
  135.6 0.1 iota_compare_fusion.2
  135.7 0.2 fusion.54
  135.9 3.7 %fusion.53 = (f32[32,2,16]{2,1,0:T(2,128)S(1)}, f32[32,2,16,256]{3,2,1,0:T(8,128)S(1)}) fusion(bf16[32,2,16,128]{3,2,1,0:T(8,128)(2,1)S(1)} %bitcast.83, pred[32,256]{1,0:T(8,128)(4,1)S(1)} %iota_compare_fusion.2, bf16[32,256,256]{2,1,0:T(8,128)(2,1)} %param.14), kind=kOutput, calls=%fused_computation.62 | convolution fusion | flops 67894272 | bytes 5517312 | tf_op jit(solution)/shard_map/tgqd,tlgd->tgql/dot_general | solution.py:35
  139.7 0.4 fusion.32
  140.1 0.1 fusion.50
  140.2 0.0 copy-done.5
  140.2 1.0 fusion.29
  141.1 0.8 copy.66
  141.9 85.8 %all-to-all-done.1 = bf16[16,32,4096]{2,1,0:T(8,128)(2,1)} async-done(((bf16[16,32,4096]{2,1,0:T(8,128)(2,1)}), bf16[16,32,4096]{2,1,0:T(8,128)(2,1)}, u32[]{:S(2)}, u32[]{:S(2)}) %all-to-all-start.1) | async-done | bytes 4194336 | tf_op jit(solution)/shard_map/all_to_all | solution.py:97
  227.8 5.3 %convolution_bitcast_fusion = f32[32,4096]{1,0:T(8,128)S(1)} fusion(bf16[16,32,4096]{2,1,0:T(8,128)(2,1)} %all-to-all-done.1, f32[32,16,32]{2,1,0:T(8,128)S(1)} %get-tuple-element.2), kind=kOutput, calls=%fused_computation.8 | convolution fusion | flops 805306368 | bytes 4784128 | tf_op jit(solution)/shard_map/rec,ecd->rd/dot_general | solution.py:98
  233.0 18.6 %all-reduce.1 = bf16[32,4096]{1,0:T(8,128)(2,1)} all-reduce(f32[32,4096]{1,0:T(8,128)S(1)} %convolution_bitcast_fusion), channel_id=1, replica_groups=mesh['side'=2,'dev'=16] {'side'}, use_global_device_ids=true, to_apply=%region_9.10 | all-reduce | flops 131072 | bytes 786432 | tf_op jit(solution)/shard_map/psum | solution.py:101
  (9 shorter events, 0.2 us)
Async XLA Ops:
  7.2 102.7 %slice-start = ((s8[6291456]{0:T(1024)(128)(4,1)}), s8[4194304]{0:T(1024)(128)(4,1)S(1)}, s32[]{:S(2)}) async-start(s8[6291456]{0:T(1024)(128)(4,1)} %bitcast.89), calls=%async_computation.2 | async-start | bytes 8388608
  9.6 100.3 %slice-start.1 = ((s8[6291456]{0:T(1024)(128)(4,1)}), s8[2097152]{0:T(1024)(128)(4,1)S(1)}, s32[]{:S(2)}) async-start(s8[6291456]{0:T(1024)(128)(4,1)} %bitcast.89), calls=%async_computation.3 | async-start | bytes 4194304
  107.9 2.0 copy-start
  129.8 5.6 %copy-start.2 = (bf16[32,256]{1,0:T(8,128)(2,1)S(1)}, bf16[32,256]{1,0:T(8,128)(2,1)}, u32[]{:S(2)}) copy-start(bf16[32,256]{1,0:T(8,128)(2,1)} %param.16) | copy-start | bytes 49156
  129.8 5.6 %copy-start.3 = (bf16[32,256]{1,0:T(8,128)(2,1)S(1)}, bf16[32,256]{1,0:T(8,128)(2,1)}, u32[]{:S(2)}) copy-start(bf16[32,256]{1,0:T(8,128)(2,1)} %param.17) | copy-start | bytes 49156
  129.8 5.7 %copy-start.1 = (bf16[32,4096]{1,0:T(8,128)(2,1)S(1)}, bf16[32,4096]{1,0:T(8,128)(2,1)}, u32[]{:S(2)}) copy-start(bf16[32,4096]{1,0:T(8,128)(2,1)} %param.13) | copy-start | bytes 786436
  129.8 5.7 %copy-start.4 = (s32[32]{0:T(128)S(1)}, s32[32]{0:T(128)}, u32[]{:S(2)}) copy-start(s32[32]{0:T(128)} %param.18) | copy-start | bytes 388
  129.8 97.9 %all-to-all-start.1 = ((bf16[16,32,4096]{2,1,0:T(8,128)(2,1)}), bf16[16,32,4096]{2,1,0:T(8,128)(2,1)}, u32[]{:S(2)}, u32[]{:S(2)}) async-start(bf16[16,32,4096]{2,1,0:T(8,128)(2,1)} %fusion.6), calls=%async_computation.1 | async-start | bytes 8388608 | tf_op jit(solution)/shard_map/all_to_all | solution.py:97
  135.5 4.7 %copy-start.5 = (bf16[32,256,256]{2,1,0:T(8,128)(2,1)S(1)}, bf16[32,256,256]{2,1,0:T(8,128)(2,1)}, u32[]{:S(2)}) copy-start(bf16[32,256,256]{2,1,0:T(8,128)(2,1)} %param.15) | copy-start | bytes 12582916
where the time goes:
time: 252 us
  blocking collectives  117 us (46%)
  waiting for transfers between devices  85.8 us (34%)
  matrix products  32.5 us (13%)
  other arithmetic  5.81 us (2%)
  starting transfers between devices  5.61 us (2%)
  local copies, waits for them, and re-layouts  4.18 us (2%)
    all_to_all x1, blocking collectives, per_device(): lax.all_to_all(buffer, 'dev', split_axis=0, concat_axis=0, tiled=True)  98.3 us
    all_to_all x1, waiting for transfers between devices, per_device(): lax.all_to_all(partial_out, 'dev', split_axis=0, concat_axis=0, tiled=True)  85.8 us
    psum x1, blocking collectives, per_device(): combined = lax.psum(local_mix, 'side')  18.6 us
    dot_general x1, matrix products, per_device(): jnp.einsum('scf,fd->scd', activation, w_down[0], preferred_element_type=j...  16.5 us
    all_to_all x1, starting transfers between devices, per_device(): lax.all_to_all(partial_out, 'dev', split_axis=0, concat_axis=0, tiled=True)  5.61 us
    dot_general x1, matrix products, per_device(): jnp.einsum('rec,ecd->rd', slot_gate, back.astype(jnp.float32), precision=...  5.27 us
  transfers between devices with their start and end apart: 1, of which 1 were waited for; matrix products, arithmetic and copies ran while one was open for 3% of the time, Pallas kernels for 0%

commit v1 on v0

v1 whole, which is shorter than its diff:
```python
import jax
import jax.numpy as jnp
from jax import lax
from jax.experimental import pallas as pl
from jax.experimental.pallas import tpu as pltpu
from jax.sharding import PartitionSpec as P

HEADS = 64
KV_HEADS = 4
HEAD_DIM = 128


def attend_local(queries, cache_keys, cache_values, new_key, new_value, cache_lengths):
    row_count = queries.shape[0]
    cache_len = cache_keys.shape[1]
    groups = cache_keys.shape[2] // HEAD_DIM
    per_group = HEADS // KV_HEADS
    score_scale = HEAD_DIM ** (-0.5)
    query_heads = queries.reshape(row_count, groups, per_group, HEAD_DIM)
    key_heads = cache_keys.reshape(row_count, cache_len, groups, HEAD_DIM)
    value_heads = cache_values.reshape(row_count, cache_len, groups, HEAD_DIM)
    scores = (
        jnp.einsum("tgqd,tlgd->tgql", query_heads, key_heads, preferred_element_type=jnp.float32)
        * score_scale
    )
    own_key = new_key.reshape(row_count, groups, HEAD_DIM)
    own_score = (
        jnp.einsum("tgqd,tgd->tgq", query_heads, own_key, preferred_element_type=jnp.float32)
        * score_scale
    )
    visible = jnp.arange(cache_len, dtype=jnp.int32)[None, :] < cache_lengths[:, None]
    scores = jnp.where(visible[:, None, None, :], scores, -1e30)
    top_score = jnp.maximum(jnp.max(scores, axis=3), own_score)
    exp_scores = jnp.exp(scores - top_score[..., None])
    own_exp = jnp.exp(own_score - top_score)
    denominator = jnp.sum(exp_scores, axis=3) + own_exp
    attn_weights = (exp_scores / denominator[..., None]).astype(jnp.bfloat16)
    own_prob = (own_exp / denominator).astype(jnp.bfloat16)
    combined = jnp.einsum(
        "tgql,tlgd->tgqd", attn_weights, value_heads, preferred_element_type=jnp.float32
    )
    own_value = new_value.reshape(row_count, groups, 1, HEAD_DIM).astype(jnp.float32)
    combined = combined + own_prob.astype(jnp.float32)[..., None] * own_value
    return combined.reshape(row_count, groups * per_group * HEAD_DIM).astype(jnp.bfloat16)


def norm_kernel(side_ref, hidden_ref, gain_ref, ids_ref, probs_ref, rows_ref, half_ref):
    features = hidden_ref.shape[1]
    row_count = hidden_ref.shape[0]
    lanes = rows_ref.shape[1] - features
    wide = hidden_ref[...].astype(jnp.float32)
    inverse = lax.rsqrt(jnp.mean(wide * wide, axis=1, keepdims=True) + 1e-06)
    normed = wide * inverse * gain_ref[...].astype(jnp.float32)
    probs = probs_ref[...]
    share = probs / jnp.sum(probs, axis=1, keepdims=True)
    ids = ids_ref[...]
    lane = lax.broadcasted_iota(jnp.int32, (row_count, lanes), 1)
    half_lanes = lanes // 2
    expert_of = jnp.where(lane < half_lanes, lane, lane - half_lanes)
    gates = jnp.zeros((row_count, lanes), jnp.float32)
    for k in range(ids.shape[1]):
        gates = gates + jnp.where(expert_of == ids[:, k : k + 1], share[:, k : k + 1], 0.0)
    coarse = gates.astype(jnp.bfloat16).astype(jnp.float32)
    gates = jnp.where(lane < half_lanes, coarse, gates - coarse)
    whole = jnp.concatenate([normed, gates], axis=1)
    half = row_count // 2
    first = side_ref[0] == 0
    mine = jnp.where(first, whole[:half], whole[half:]).astype(jnp.bfloat16)
    other = jnp.where(first, whole[half:], whole[:half]).astype(jnp.bfloat16)
    rows_ref[:half] = mine
    rows_ref[half:] = other
    half_ref[...] = mine


def normed_rows(hidden, norm_gain, expert_ids, router_probs, experts):
    row_count, features = hidden.shape
    lanes = 128 * (-(-2 * experts // 128))
    side = lax.axis_index("side").astype(jnp.int32).reshape(1)
    width = features + lanes
    vmem = pl.BlockSpec(memory_space=pltpu.VMEM)
    return pl.pallas_call(
        norm_kernel,
        in_specs=[pl.BlockSpec(memory_space=pltpu.SMEM), vmem, vmem, vmem, vmem],
        out_specs=(vmem, vmem),
        out_shape=(
            jax.ShapeDtypeStruct((row_count, width), jnp.bfloat16),
            jax.ShapeDtypeStruct((row_count // 2, width), jnp.bfloat16),
        ),
        name="norm_and_gates",
    )(side, hidden, norm_gain.reshape(1, features), expert_ids, router_probs)


def expert_kernel(
    expert_ref, own_ref, other_ref, gate_ref, up_ref, down_ref, own_out, other_out, total
):
    step = pl.program_id(0)
    features = gate_ref.shape[1]
    rows = own_ref.shape[0]
    x = jnp.concatenate([own_ref[:, :features], other_ref[:, :features]], axis=0)
    tail = jnp.concatenate([own_ref[:, features:], other_ref[:, features:]], axis=0)
    lanes = tail.shape[1]
    lane = lax.broadcasted_iota(jnp.int32, tail.shape, 1)
    mine = (lane == expert_ref[0]) | (lane == expert_ref[0] + lanes // 2)
    share = jnp.sum(jnp.where(mine, tail.astype(jnp.float32), 0.0), axis=1, keepdims=True)
    gate_act = jnp.dot(x, gate_ref[0], preferred_element_type=jnp.float32)
    up_act = jnp.dot(x, up_ref[0], preferred_element_type=jnp.float32)
    activation = (jax.nn.silu(gate_act) * up_act * share).astype(jnp.bfloat16)
    part = jnp.dot(activation, down_ref[0], preferred_element_type=jnp.float32)

    @pl.when(step == 0)
    def _():
        total[...] = part

    @pl.when(step > 0)
    def _():
        total[...] += part

    @pl.when(step == pl.num_programs(0) - 1)
    def _():
        own_out[...] = total[:rows].astype(jnp.bfloat16)
        other_out[...] = total[rows:].astype(jnp.bfloat16)


def expert_rows(own, other, w_gate, w_up, w_down):
    rows, width = own.shape
    _, features, hidden_units = w_gate.shape
    chunk = 256
    expert = lax.axis_index("dev").astype(jnp.int32).reshape(1)
    whole = pl.BlockSpec((rows, width), lambda j: (0, 0))
    out = pl.BlockSpec((rows, features), lambda j: (0, 0))
    return pl.pallas_call(
        expert_kernel,
        grid=(hidden_units // chunk,),
        in_specs=[
            pl.BlockSpec(memory_space=pltpu.SMEM),
            whole,
            whole,
            pl.BlockSpec((1, features, chunk), lambda j: (0, 0, j)),
            pl.BlockSpec((1, features, chunk), lambda j: (0, 0, j)),
            pl.BlockSpec((1, chunk, features), lambda j: (0, j, 0)),
        ],
        out_specs=(out, out),
        out_shape=(jax.ShapeDtypeStruct((rows, features), jnp.bfloat16),) * 2,
        scratch_shapes=[pltpu.VMEM((2 * rows, features), jnp.float32)],
        compiler_params=pltpu.CompilerParams(
            dimension_semantics=("arbitrary",), vmem_limit_bytes=50 * 1024 * 1024
        ),
        name="expert_rows",
    )(expert, own, other, w_gate, w_up, w_down)


def add(*parts):
    total = parts[0].astype(jnp.float32)
    for part in parts[1:]:
        total = total + part.astype(jnp.float32)
    return total


def add_rounded(*parts):
    return add(*parts).astype(jnp.bfloat16)


def per_device(
    queries,
    cache_keys,
    cache_values,
    new_key,
    new_value,
    cache_lengths,
    hidden,
    norm_gain,
    expert_ids,
    router_probs,
    w_gate,
    w_up,
    w_down,
):
    devices = lax.axis_size("dev")
    planes = devices // 4
    experts = w_gate.shape[0] * devices

    def over(bit):
        return lambda a: lax.ppermute(a, "dev", [(d, d ^ bit) for d in range(devices)])

    core, across = over(1), over(2)
    sides = lambda a: lax.ppermute(a, "side", [(0, 1), (1, 0)])

    own_rows, own_half = normed_rows(hidden, norm_gain, expert_ids, router_probs, experts)
    half = own_half.shape[0]
    arrived = {i: over(4 * i)(own_half) for i in range(1, planes)}
    context = attend_local(queries, cache_keys, cache_values, new_key, new_value, cache_lengths)
    blocks = {0: [own_rows, across(own_rows)]}
    for i in range(1, planes):
        mine = arrived[i]
        beside, facing = across(mine), sides(mine)
        diagonal = sides(beside) if i % 4 != 3 else across(facing)
        blocks[i] = [mine, facing, beside, diagonal]

    reduced = {}
    for first in range(0, planes, 2):
        group = [first, first + 1]
        stack = jnp.concatenate(blocks[first] + blocks[first + 1], axis=0)
        own_out, other_out = expert_rows(stack, core(stack), w_gate, w_up, w_down)
        merged = add_rounded(own_out, core(other_out))
        for place, i in enumerate(group):
            four = merged[place * 4 * half : (place + 1) * 4 * half]
            if i % 4 in (0, 3):
                pair = add_rounded(four[: 2 * half], across(four[2 * half :]))
                parts = (pair[:half], sides(pair[half:]))
            else:
                mine, facing, beside, diagonal = (four[j * half : (j + 1) * half] for j in range(4))
                got = sides(jnp.concatenate([facing, diagonal], axis=0))
                mine = add(mine, got[:half])
                parts = (mine, across(add_rounded(beside, got[half:])))
            if i == 0:
                reduced[i] = add(*parts)
            else:
                reduced[i] = over(4 * i)(add_rounded(*parts))
    total = add_rounded(*(reduced[i] for i in range(planes)))
    partner = sides(total)
    first = lax.axis_index("side") == 0
    moe_out = jnp.concatenate(
        [jnp.where(first, total, partner), jnp.where(first, partner, total)], axis=0
    )
    return (context, moe_out)


def solution(mesh):
    in_specs = (
        P("dev", "side"),
        P("dev", None, "side"),
        P("dev", None, "side"),
        P("dev", "side"),
        P("dev", "side"),
        P("dev"),
        P("dev", None),
        P(),
        P("dev", None),
        P("dev", None),
        P("dev", None, "side"),
        P("dev", None, "side"),
        P("dev", "side", None),
    )
    out_specs = (P("dev", "side"), P("dev", None))
    return jax.shard_map(
        per_device, mesh=mesh, in_specs=in_specs, out_specs=out_specs, check_vma=False
    )
```

time: 252 us -> 108 us (0.43)
  the two profiles are of different devices: /device:TPU:10 before, /device:TPU:0 now
where the time goes in v1:
time: 108 us; the launch traced here: 107 us
  starting transfers between devices  35.2 us (33%)
  waiting for transfers between devices  30.2 us (28%)
  Pallas kernels  25.6 us (24%)
  local copies, waits for them, and re-layouts  7.22 us (7%)
  matrix products  4.67 us (4%)
  other arithmetic  3.51 us (3%)
    pallas_call x2, Pallas kernels, expert_rows(): pl.pallas_call(expert_kernel, grid=(hidden_units // chunk,), in_specs=[pl...  23.6 us
    ppermute x19, starting transfers between devices, over(): lax.ppermute(a, 'dev', [(d, d ^ bit) for d in range(devices)])  22.8 us
    ppermute x19, waiting for transfers between devices, over(): lax.ppermute(a, 'dev', [(d, d ^ bit) for d in range(devices)])  21.2 us
    ppermute x10, starting transfers between devices, per_device(): sides = lambda a: lax.ppermute(a, 'side', [(0, 1), (1, 0)])  12.4 us
    ppermute x10, waiting for transfers between devices, per_device(): sides = lambda a: lax.ppermute(a, 'side', [(0, 1), (1, 0)])  8.99 us
    unnamed x28, local copies, waits for them, and re-layouts  5.75 us
    dot_general x1, matrix products, attend_local(): jnp.einsum('tgqd,tlgd->tgql', query_heads, key_heads, preferred_element_t...  3.5 us
  transfers between devices with their start and end apart: 29, of which 12 were waited for; matrix products, arithmetic and copies ran while one was open for 9% of the time, Pallas kernels for 22%

profile of v1, /device:TPU:0, one launch (start us, length us, event | category | flops | bytes accessed | tf_op | source)
XLA Modules:
  0.0 107.3 jit_solution(11440900331689040465)
XLA Ops:
  0.6 1.4 %copy.17.ids_ref = s32[32,8]{1,0:T(8,128)} copy(s32[32,8]{0,1:T(8,128)} %param.21) | data formatting | bytes 2048 | tf_op args[8]
  2.0 1.4 %copy.18.probs_ref = f32[32,8]{1,0:T(8,128)} copy(f32[32,8]{0,1:T(8,128)} %param.22) | data formatting | bytes 2048 | tf_op args[9]
  3.4 1.3 %reshape.64.gain_ref = bf16[1,4096]{1,0:T(2,128)(2,1)} reshape(bf16[4096]{0:T(1024)(128)(2,1)} %param.20) | data formatting | bytes 16384 | tf_op jit(solution)/shard_map/reshape | solution.py:90
  4.7 2.0 %norm_and_gates.1 = (bf16[32,4224]{1,0:T(8,128)(2,1)}, bf16[16,4224]{1,0:T(8,128)(2,1)}) custom-call(s32[1]{0:T(128)} %bitcast.3.side_ref, bf16[32,4096]{1,0:T(8,128)(2,1)} %hidden_ref.1, bf16[1,4096]{1,0:T(2,128)(2,1)} %reshape.64.gain_ref, s32[32,8]{1,0:T(8,128)} %copy.17.ids_ref, f32[32,8]{1,0:T(8,128)} %copy.18.probs_ref), custom_call_target="tpu_custom_call" | custom-call | tf_op jit(solution)/shard_map/norm_and_gates/pallas_call | solution.py:81
  6.7 3.0 %collective-permute-start.1 = (bf16[16,4224]{1,0:T(8,128)(2,1)}, bf16[16,4224]{1,0:T(8,128)(2,1)S(1)}, u32[]{:S(2)}, u32[]{:S(2)}) collective-permute-start(bf16[16,4224]{1,0:T(8,128)(2,1)} %get-tuple-element.9), channel_id=1, source_target_pairs={{0,4},{1,5},{2,6},{3,7},{4,0},{5,1},{6,2},{7,3},{8,12},{9,13},{10,... | collective-permute-start | bytes 405512 | tf_op jit(solution)/shard_map/ppermute | solution.py:183
  9.7 2.6 %collective-permute-start.12 = (bf16[16,4224]{1,0:T(8,128)(2,1)}, bf16[16,4224]{1,0:T(8,128)(2,1)S(1)}, u32[]{:S(2)}, u32[]{:S(2)}) collective-permute-start(bf16[16,4224]{1,0:T(8,128)(2,1)} %get-tuple-element.9), channel_id=1, source_target_pairs={{0,8},{1,9},{2,10},{3,11},{4,12},{5,13},{6,14},{7,15},{8,0},{9,1},... | collective-permute-start | bytes 405512 | tf_op jit(solution)/shard_map/ppermute | solution.py:183
  12.3 1.7 %collective-permute-start = (bf16[32,4224]{1,0:T(8,128)(2,1)}, bf16[32,4224]{1,0:T(8,128)(2,1)S(1)}, u32[]{:S(2)}, u32[]{:S(2)}) collective-permute-start(bf16[32,4224]{1,0:T(8,128)(2,1)} %get-tuple-element.8), channel_id=1, source_target_pairs={{0,2},{1,3},{2,0},{3,1},{4,6},{5,7},{6,4},{7,5},{8,10},{9,11},{10,... | collective-permute-start | bytes 811016 | tf_op jit(solution)/shard_map/ppermute | solution.py:183
  14.0 1.0 constant_dynamic-update-slice_fusion.5
  15.1 1.7 %collective-permute-start.2 = (bf16[16,4224]{1,0:T(8,128)(2,1)S(1)}, bf16[16,4224]{1,0:T(8,128)(2,1)S(1)}, u32[]{:S(2)}, u32[]{:S(2)}) collective-permute-start(bf16[16,4224]{1,0:T(8,128)(2,1)S(1)} %collective-permute-done.1), channel_id=1, source_target_pairs={{0,16},{16,0},{1,17},{17,1},{2,18},{18,2},{3,19},{19,3},{4,20},{20... | collective-permute-start | bytes 405512 | tf_op jit(solution)/shard_map/ppermute | solution.py:186
  16.9 1.5 %collective-permute-start.3 = (bf16[16,4224]{1,0:T(8,128)(2,1)S(1)}, bf16[16,4224]{1,0:T(8,128)(2,1)S(1)}, u32[]{:S(2)}, u32[]{:S(2)}) collective-permute-start(bf16[16,4224]{1,0:T(8,128)(2,1)S(1)} %collective-permute-done.1), channel_id=1, source_target_pairs={{0,2},{1,3},{2,0},{3,1},{4,6},{5,7},{6,4},{7,5},{8,10},{9,11},{10,... | collective-permute-start | bytes 405512 | tf_op jit(solution)/shard_map/ppermute | solution.py:183
  18.4 4.7 %collective-permute-done.12 = bf16[16,4224]{1,0:T(8,128)(2,1)S(1)} collective-permute-done((bf16[16,4224]{1,0:T(8,128)(2,1)}, bf16[16,4224]{1,0:T(8,128)(2,1)S(1)}, u32[]{:S(2)}, u32[]{:S(2)}) %collective-permute-start.12) | collective-permute-done | bytes 135200 | tf_op jit(solution)/shard_map/ppermute | solution.py:183
  23.1 1.6 %collective-permute-start.13 = (bf16[16,4224]{1,0:T(8,128)(2,1)S(1)}, bf16[16,4224]{1,0:T(8,128)(2,1)S(1)}, u32[]{:S(2)}, u32[]{:S(2)}) collective-permute-start(bf16[16,4224]{1,0:T(8,128)(2,1)S(1)} %collective-permute-done.12), channel_id=1, source_target_pairs={{0,16},{16,0},{1,17},{17,1},{2,18},{18,2},{3,19},{19,3},{4,20},{20... | collective-permute-start | bytes 405512 | tf_op jit(solution)/shard_map/ppermute | solution.py:186
  24.7 1.5 %collective-permute-start.14 = (bf16[16,4224]{1,0:T(8,128)(2,1)S(1)}, bf16[16,4224]{1,0:T(8,128)(2,1)S(1)}, u32[]{:S(2)}, u32[]{:S(2)}) collective-permute-start(bf16[16,4224]{1,0:T(8,128)(2,1)S(1)} %collective-permute-done.12), channel_id=1, source_target_pairs={{0,2},{1,3},{2,0},{3,1},{4,6},{5,7},{6,4},{7,5},{8,10},{9,11},{10,... | collective-permute-start | bytes 405512 | tf_op jit(solution)/shard_map/ppermute | solution.py:183
  26.2 0.5 collective-permute-start.17
  26.8 0.6 collective-permute-start.18
  27.4 1.5 %collective-permute-start.4 = (bf16[16,4224]{1,0:T(8,128)(2,1)S(1)}, bf16[16,4224]{1,0:T(8,128)(2,1)S(1)}, u32[]{:S(2)}, u32[]{:S(2)}) collective-permute-start(bf16[16,4224]{1,0:T(8,128)(2,1)S(1)} %collective-permute-done.3), channel_id=1, source_target_pairs={{0,16},{16,0},{1,17},{17,1},{2,18},{18,2},{3,19},{19,3},{4,20},{20... | collective-permute-start | bytes 405512 | tf_op jit(solution)/shard_map/ppermute | solution.py:186
  28.9 2.2 %collective-permute-done.14 = bf16[16,4224]{1,0:T(8,128)(2,1)S(1)} collective-permute-done((bf16[16,4224]{1,0:T(8,128)(2,1)S(1)}, bf16[16,4224]{1,0:T(8,128)(2,1)S(1)}, u32[]{:S(2)}, u32[]{:S(2)}) %collective-permute-start.14) | collective-permute-done | bytes 135200 | tf_op jit(solution)/shard_map/ppermute | solution.py:183
  31.2 0.5 collective-permute-done.17
  31.7 1.6 %collective-permute-start.19 = (bf16[16,4224]{1,0:T(8,128)(2,1)S(1)}, bf16[16,4224]{1,0:T(8,128)(2,1)S(1)}, u32[]{:S(2)}, u32[]{:S(2)}) collective-permute-start(bf16[16,4224]{1,0:T(8,128)(2,1)S(1)} %collective-permute-done.17), channel_id=1, source_target_pairs={{0,2},{1,3},{2,0},{3,1},{4,6},{5,7},{6,4},{7,5},{8,10},{9,11},{10,... | collective-permute-start | bytes 405512 | tf_op jit(solution)/shard_map/ppermute | solution.py:183
  33.4 2.8 %collective-permute-done.15 = bf16[16,4224]{1,0:T(8,128)(2,1)S(1)} collective-permute-done((bf16[16,4224]{1,0:T(8,128)(2,1)S(1)}, bf16[16,4224]{1,0:T(8,128)(2,1)S(1)}, u32[]{:S(2)}, u32[]{:S(2)}) %collective-permute-start.15) | collective-permute-done | bytes 135200 | tf_op jit(solution)/shard_map/ppermute | solution.py:186
  36.2 0.5 collective-permute-done.19
  36.8 1.0 copy-done
  37.8 12.3 %expert_rows.2 = (bf16[128,4096]{1,0:T(8,128)(2,1)S(1)}, bf16[128,4096]{1,0:T(8,128)(2,1)}) custom-call(s32[1]{0:T(128)} %bitcast.2.expert_ref, bf16[128,4224]{1,0:T(8,128)(2,1)S(1)} %constant_dynamic-update-slice_fusion.own_ref, bf16[128,4224]{1,0:T(8,128)(2,1)} %copy-done, bf16[1,4096,768]{2,1,0:T(8,128)(2,1)} %gate_ref.3, bf16[1,4096,768]{2,1,0:T(8,128)(2,1)} %up_ref.3, ...), custom_call_target="tpu_custom_call" | custom-call | tf_op jit(solution)/shard_map/expert_rows/pallas_call | solution.py:131
  50.1 0.5 collective-permute-start.6
  51.0 3.5 %fusion.25 = (f32[32,2,16]{2,1,0:T(2,128)S(1)}, f32[32,2,16,256]{3,2,1,0:T(8,128)S(1)}) fusion(bf16[32,2,16,128]{3,2,1,0:T(8,128)(2,1)S(1)} %bitcast.40, pred[32,256]{1,0:T(8,128)(4,1)S(1)} %iota_compare_fusion, bf16[32,256,256]{2,1,0:T(8,128)(2,1)} %param.14), kind=kOutput, calls=%fused_computation.53 | convolution fusion | flops 67894272 | bytes 5517312 | tf_op jit(solution)/shard_map/tgqd,tlgd->tgql/dot_general | solution.py:23
  55.0 11.3 %expert_rows.3 = (bf16[128,4096]{1,0:T(8,128)(2,1)S(1)}, bf16[128,4096]{1,0:T(8,128)(2,1)S(1)}) custom-call(s32[1]{0:T(128)} %bitcast.2.expert_ref, bf16[128,4224]{1,0:T(8,128)(2,1)S(1)} %constant_dynamic-update-slice_fusion.6.own_ref, bf16[128,4224]{1,0:T(8,128)(2,1)} %collective-permute-done.20.other_ref, bf16[1,4096,768]{2,1,0:T(8,128)(2,1)} %gate_ref.3, ...), custom_call_target="tpu_custom_call" | custom-call | tf_op jit(solution)/shard_map/expert_rows/pallas_call | solution.py:131
  66.5 1.5 %add_convert_fusion.1 = bf16[128,4096]{1,0:T(8,128)(2,1)S(1)} fusion(bf16[128,4096]{1,0:T(8,128)(2,1)} %collective-permute-done.6, bf16[128,4096]{1,0:T(8,128)(2,1)S(1)} %get-tuple-element.10), kind=kLoop, calls=%fused_computation.7 | loop fusion | flops 2097152 | bytes 3145728 | tf_op jit(solution)/shard_map/convert_element_type | solution.py:160
  68.0 1.1 %collective-permute-done.21 = bf16[128,4096]{1,0:T(8,128)(2,1)S(1)} collective-permute-done((bf16[128,4096]{1,0:T(8,128)(2,1)S(1)}, bf16[128,4096]{1,0:T(8,128)(2,1)S(1)}, u32[]{:S(2)}, u32[]{:S(2)}) %collective-permute-start.21) | collective-permute-done | bytes 1048608 | tf_op jit(solution)/shard_map/ppermute | solution.py:183
  69.4 1.6 %collective-permute-start.7 = (bf16[32,4096]{1,0:T(8,128)(2,1)S(1)}, bf16[32,4096]{1,0:T(8,128)(2,1)S(1)}, u32[]{:S(2)}, u32[]{:S(2)}) collective-permute-start(bf16[32,4096]{1,0:T(8,128)(2,1)S(1)} %slice.97), channel_id=1, source_target_pairs={{0,2},{1,3},{2,0},{3,1},{4,6},{5,7},{6,4},{7,5},{8,10},{9,11},{10,... | collective-permute-start | bytes 786440 | tf_op jit(solution)/shard_map/ppermute | solution.py:183
  71.1 1.6 %collective-permute-start.9 = (bf16[32,4096]{1,0:T(8,128)(2,1)S(1)}, bf16[32,4096]{1,0:T(8,128)(2,1)S(1)}, u32[]{:S(2)}, u32[]{:S(2)}) collective-permute-start(bf16[32,4096]{1,0:T(8,128)(2,1)S(1)} %pad_maximum_fusion), channel_id=1, source_target_pairs={{0,16},{16,0},{1,17},{17,1},{2,18},{18,2},{3,19},{19,3},{4,20},{20... | collective-permute-start | bytes 786440 | tf_op jit(solution)/shard_map/ppermute | solution.py:186
  72.7 0.6 collective-permute-start.22
  73.2 0.5 collective-permute-start.25
  73.7 4.9 %collective-permute-done.7 = bf16[32,4096]{1,0:T(8,128)(2,1)S(1)} collective-permute-done((bf16[32,4096]{1,0:T(8,128)(2,1)S(1)}, bf16[32,4096]{1,0:T(8,128)(2,1)S(1)}, u32[]{:S(2)}, u32[]{:S(2)}) %collective-permute-start.7) | collective-permute-done | bytes 262176 | tf_op jit(solution)/shard_map/ppermute | solution.py:183
  78.7 1.7 %collective-permute-start.8 = (bf16[16,4096]{1,0:T(8,128)(2,1)S(1)}, bf16[16,4096]{1,0:T(8,128)(2,1)S(1)}, u32[]{:S(2)}, u32[]{:S(2)}) collective-permute-start(bf16[16,4096]{1,0:T(8,128)(2,1)S(1)} %slice.99), channel_id=1, source_target_pairs={{0,16},{16,0},{1,17},{17,1},{2,18},{18,2},{3,19},{19,3},{4,20},{20... | collective-permute-start | bytes 393224 | tf_op jit(solution)/shard_map/ppermute | solution.py:186
  80.4 1.6 %collective-permute-start.10 = (bf16[16,4096]{1,0:T(8,128)(2,1)S(1)}, bf16[16,4096]{1,0:T(8,128)(2,1)S(1)}, u32[]{:S(2)}, u32[]{:S(2)}) collective-permute-start(bf16[16,4096]{1,0:T(8,128)(2,1)S(1)} %add_convert_fusion.9), channel_id=1, source_target_pairs={{0,2},{1,3},{2,0},{3,1},{4,6},{5,7},{6,4},{7,5},{8,10},{9,11},{10,... | collective-permute-start | bytes 393224 | tf_op jit(solution)/shard_map/ppermute | solution.py:183
  82.0 4.0 %collective-permute-done.22 = bf16[32,4096]{1,0:T(8,128)(2,1)S(1)} collective-permute-done((bf16[32,4096]{1,0:T(8,128)(2,1)S(1)}, bf16[32,4096]{1,0:T(8,128)(2,1)S(1)}, u32[]{:S(2)}, u32[]{:S(2)}) %collective-permute-start.22) | collective-permute-done | bytes 262176 | tf_op jit(solution)/shard_map/ppermute | solution.py:186
  86.0 0.5 collective-permute-start.23
  86.6 1.7 %collective-permute-start.26 = (bf16[16,4096]{1,0:T(8,128)(2,1)S(1)}, bf16[16,4096]{1,0:T(8,128)(2,1)S(1)}, u32[]{:S(2)}, u32[]{:S(2)}) collective-permute-start(bf16[16,4096]{1,0:T(8,128)(2,1)S(1)} %slice.115), channel_id=1, source_target_pairs={{0,16},{16,0},{1,17},{17,1},{2,18},{18,2},{3,19},{19,3},{4,20},{20... | collective-permute-start | bytes 393224 | tf_op jit(solution)/shard_map/ppermute | solution.py:186
  88.3 1.5 %collective-permute-start.11 = (bf16[16,4096]{1,0:T(8,128)(2,1)S(1)}, bf16[16,4096]{1,0:T(8,128)(2,1)S(1)}, u32[]{:S(2)}, u32[]{:S(2)}) collective-permute-start(bf16[16,4096]{1,0:T(8,128)(2,1)S(1)} %add_convert_fusion.8), channel_id=1, source_target_pairs={{0,4},{1,5},{2,6},{3,7},{4,0},{5,1},{6,2},{7,3},{8,12},{9,13},{10,... | collective-permute-start | bytes 393224 | tf_op jit(solution)/shard_map/ppermute | solution.py:183
  89.8 1.2 %collective-permute-done.23 = bf16[16,4096]{1,0:T(8,128)(2,1)S(1)} collective-permute-done((bf16[16,4096]{1,0:T(8,128)(2,1)S(1)}, bf16[16,4096]{1,0:T(8,128)(2,1)S(1)}, u32[]{:S(2)}, u32[]{:S(2)}) %collective-permute-start.23) | collective-permute-done | bytes 131104 | tf_op jit(solution)/shard_map/ppermute | solution.py:183
  91.1 2.0 %collective-permute-start.24 = (bf16[16,4096]{1,0:T(8,128)(2,1)S(1)}, bf16[16,4096]{1,0:T(8,128)(2,1)S(1)}, u32[]{:S(2)}, u32[]{:S(2)}) collective-permute-start(bf16[16,4096]{1,0:T(8,128)(2,1)S(1)} %add_convert_fusion.6), channel_id=1, source_target_pairs={{0,8},{1,9},{2,10},{3,11},{4,12},{5,13},{6,14},{7,15},{8,0},{9,1},... | collective-permute-start | bytes 393224 | tf_op jit(solution)/shard_map/ppermute | solution.py:183
  93.1 2.0 %collective-permute-start.27 = (bf16[16,4096]{1,0:T(8,128)(2,1)S(1)}, bf16[16,4096]{1,0:T(8,128)(2,1)S(1)}, u32[]{:S(2)}, u32[]{:S(2)}) collective-permute-start(bf16[16,4096]{1,0:T(8,128)(2,1)S(1)} %add_convert_fusion.5), channel_id=1, source_target_pairs={{0,12},{1,13},{2,14},{3,15},{4,8},{5,9},{6,10},{7,11},{8,4},{9,5},... | collective-permute-start | bytes 393224 | tf_op jit(solution)/shard_map/ppermute | solution.py:183
  95.1 6.4 %collective-permute-done.24 = bf16[16,4096]{1,0:T(8,128)(2,1)S(1)} collective-permute-done((bf16[16,4096]{1,0:T(8,128)(2,1)S(1)}, bf16[16,4096]{1,0:T(8,128)(2,1)S(1)}, u32[]{:S(2)}, u32[]{:S(2)}) %collective-permute-start.24) | collective-permute-done | bytes 131104 | tf_op jit(solution)/shard_map/ppermute | solution.py:183
  101.5 1.6 %collective-permute-start.28 = (bf16[16,4096]{1,0:T(8,128)(2,1)S(1)}, bf16[16,4096]{1,0:T(8,128)(2,1)S(1)}, u32[]{:S(2)}, u32[]{:S(2)}) collective-permute-start(bf16[16,4096]{1,0:T(8,128)(2,1)S(1)} %add_convert_fusion.4), channel_id=1, source_target_pairs={{0,16},{16,0},{1,17},{17,1},{2,18},{18,2},{3,19},{19,3},{4,20},{20... | collective-permute-start | bytes 393224 | tf_op jit(solution)/shard_map/ppermute | solution.py:186
  103.1 0.9 fusion.15
  104.1 0.8 copy.44
  104.9 1.7 %collective-permute-done.28 = bf16[16,4096]{1,0:T(8,128)(2,1)S(1)} collective-permute-done((bf16[16,4096]{1,0:T(8,128)(2,1)S(1)}, bf16[16,4096]{1,0:T(8,128)(2,1)S(1)}, u32[]{:S(2)}, u32[]{:S(2)}) %collective-permute-start.28) | collective-permute-done | bytes 131104 | tf_op jit(solution)/shard_map/ppermute | solution.py:186
  106.6 0.7 pad_maximum_fusion.2
  (73 shorter events, 2.4 us)
Async XLA Ops:
  6.7 8.5 %collective-permute-start.1 = (bf16[16,4224]{1,0:T(8,128)(2,1)}, bf16[16,4224]{1,0:T(8,128)(2,1)S(1)}, u32[]{:S(2)}, u32[]{:S(2)}) collective-permute-start(bf16[16,4224]{1,0:T(8,128)(2,1)} %get-tuple-element.9), channel_id=1, source_target_pairs={{0,4},{1,5},{2,6},{3,7},{4,0},{5,1},{6,2},{7,3},{8,12},{9,13},{10,... | collective-permute-start | bytes 405512 | tf_op jit(solution)/shard_map/ppermute | solution.py:183
  9.7 13.4 %collective-permute-start.12 = (bf16[16,4224]{1,0:T(8,128)(2,1)}, bf16[16,4224]{1,0:T(8,128)(2,1)S(1)}, u32[]{:S(2)}, u32[]{:S(2)}) collective-permute-start(bf16[16,4224]{1,0:T(8,128)(2,1)} %get-tuple-element.9), channel_id=1, source_target_pairs={{0,8},{1,9},{2,10},{3,11},{4,12},{5,13},{6,14},{7,15},{8,0},{9,1},... | collective-permute-start | bytes 405512 | tf_op jit(solution)/shard_map/ppermute | solution.py:183
  12.3 12.4 %collective-permute-start.16 = (bf16[16,4224]{1,0:T(8,128)(2,1)}, bf16[16,4224]{1,0:T(8,128)(2,1)S(1)}, u32[]{:S(2)}, u32[]{:S(2)}) collective-permute-start(bf16[16,4224]{1,0:T(8,128)(2,1)} %get-tuple-element.9), channel_id=1, source_target_pairs={{0,12},{1,13},{2,14},{3,15},{4,8},{5,9},{6,10},{7,11},{8,4},{9,5},... | collective-permute-start | bytes 405512 | tf_op jit(solution)/shard_map/ppermute | solution.py:183
  12.3 13.9 %collective-permute-start = (bf16[32,4224]{1,0:T(8,128)(2,1)}, bf16[32,4224]{1,0:T(8,128)(2,1)S(1)}, u32[]{:S(2)}, u32[]{:S(2)}) collective-permute-start(bf16[32,4224]{1,0:T(8,128)(2,1)} %get-tuple-element.8), channel_id=1, source_target_pairs={{0,2},{1,3},{2,0},{3,1},{4,6},{5,7},{6,4},{7,5},{8,10},{9,11},{10,... | collective-permute-start | bytes 811016 | tf_op jit(solution)/shard_map/ppermute | solution.py:183
  15.1 11.6 %collective-permute-start.2 = (bf16[16,4224]{1,0:T(8,128)(2,1)S(1)}, bf16[16,4224]{1,0:T(8,128)(2,1)S(1)}, u32[]{:S(2)}, u32[]{:S(2)}) collective-permute-start(bf16[16,4224]{1,0:T(8,128)(2,1)S(1)} %collective-permute-done.1), channel_id=1, source_target_pairs={{0,16},{16,0},{1,17},{17,1},{2,18},{18,2},{3,19},{19,3},{4,20},{20... | collective-permute-start | bytes 405512 | tf_op jit(solution)/shard_map/ppermute | solution.py:186
  16.9 10.5 %collective-permute-start.3 = (bf16[16,4224]{1,0:T(8,128)(2,1)S(1)}, bf16[16,4224]{1,0:T(8,128)(2,1)S(1)}, u32[]{:S(2)}, u32[]{:S(2)}) collective-permute-start(bf16[16,4224]{1,0:T(8,128)(2,1)S(1)} %collective-permute-done.1), channel_id=1, source_target_pairs={{0,2},{1,3},{2,0},{3,1},{4,6},{5,7},{6,4},{7,5},{8,10},{9,11},{10,... | collective-permute-start | bytes 405512 | tf_op jit(solution)/shard_map/ppermute | solution.py:183
  23.1 8.0 %collective-permute-start.13 = (bf16[16,4224]{1,0:T(8,128)(2,1)S(1)}, bf16[16,4224]{1,0:T(8,128)(2,1)S(1)}, u32[]{:S(2)}, u32[]{:S(2)}) collective-permute-start(bf16[16,4224]{1,0:T(8,128)(2,1)S(1)} %collective-permute-done.12), channel_id=1, source_target_pairs={{0,16},{16,0},{1,17},{17,1},{2,18},{18,2},{3,19},{19,3},{4,20},{20... | collective-permute-start | bytes 405512 | tf_op jit(solution)/shard_map/ppermute | solution.py:186
  24.7 6.4 %collective-permute-start.14 = (bf16[16,4224]{1,0:T(8,128)(2,1)S(1)}, bf16[16,4224]{1,0:T(8,128)(2,1)S(1)}, u32[]{:S(2)}, u32[]{:S(2)}) collective-permute-start(bf16[16,4224]{1,0:T(8,128)(2,1)S(1)} %collective-permute-done.12), channel_id=1, source_target_pairs={{0,2},{1,3},{2,0},{3,1},{4,6},{5,7},{6,4},{7,5},{8,10},{9,11},{10,... | collective-permute-start | bytes 405512 | tf_op jit(solution)/shard_map/ppermute | solution.py:183
  26.2 5.5 %collective-permute-start.17 = (bf16[16,4224]{1,0:T(8,128)(2,1)S(1)}, bf16[16,4224]{1,0:T(8,128)(2,1)S(1)}, u32[]{:S(2)}, u32[]{:S(2)}) collective-permute-start(bf16[16,4224]{1,0:T(8,128)(2,1)S(1)} %collective-permute-done.16), channel_id=1, source_target_pairs={{0,16},{16,0},{1,17},{17,1},{2,18},{18,2},{3,19},{19,3},{4,20},{20... | collective-permute-start | bytes 405512 | tf_op jit(solution)/shard_map/ppermute | solution.py:186
  26.8 9.5 %collective-permute-start.18 = (bf16[16,4224]{1,0:T(8,128)(2,1)S(1)}, bf16[16,4224]{1,0:T(8,128)(2,1)S(1)}, u32[]{:S(2)}, u32[]{:S(2)}) collective-permute-start(bf16[16,4224]{1,0:T(8,128)(2,1)S(1)} %collective-permute-done.16), channel_id=1, source_target_pairs={{0,2},{1,3},{2,0},{3,1},{4,6},{5,7},{6,4},{7,5},{8,10},{9,11},{10,... | collective-permute-start | bytes 405512 | tf_op jit(solution)/shard_map/ppermute | solution.py:183
  27.4 5.9 %collective-permute-start.4 = (bf16[16,4224]{1,0:T(8,128)(2,1)S(1)}, bf16[16,4224]{1,0:T(8,128)(2,1)S(1)}, u32[]{:S(2)}, u32[]{:S(2)}) collective-permute-start(bf16[16,4224]{1,0:T(8,128)(2,1)S(1)} %collective-permute-done.3), channel_id=1, source_target_pairs={{0,16},{16,0},{1,17},{17,1},{2,18},{18,2},{3,19},{19,3},{4,20},{20... | collective-permute-start | bytes 405512 | tf_op jit(solution)/shard_map/ppermute | solution.py:186
  31.1 5.0 %collective-permute-start.15 = (bf16[16,4224]{1,0:T(8,128)(2,1)S(1)}, bf16[16,4224]{1,0:T(8,128)(2,1)S(1)}, u32[]{:S(2)}, u32[]{:S(2)}) collective-permute-start(bf16[16,4224]{1,0:T(8,128)(2,1)S(1)} %collective-permute-done.14), channel_id=1, source_target_pairs={{0,16},{16,0},{1,17},{17,1},{2,18},{18,2},{3,19},{19,3},{4,20},{20... | collective-permute-start | bytes 405512 | tf_op jit(solution)/shard_map/ppermute | solution.py:186
  31.7 5.0 %collective-permute-start.19 = (bf16[16,4224]{1,0:T(8,128)(2,1)S(1)}, bf16[16,4224]{1,0:T(8,128)(2,1)S(1)}, u32[]{:S(2)}, u32[]{:S(2)}) collective-permute-start(bf16[16,4224]{1,0:T(8,128)(2,1)S(1)} %collective-permute-done.17), channel_id=1, source_target_pairs={{0,2},{1,3},{2,0},{3,1},{4,6},{5,7},{6,4},{7,5},{8,10},{9,11},{10,... | collective-permute-start | bytes 405512 | tf_op jit(solution)/shard_map/ppermute | solution.py:183
  33.3 3.5 %collective-permute-start.5 = (bf16[128,4224]{1,0:T(8,128)(2,1)S(1)}, bf16[128,4224]{1,0:T(8,128)(2,1)S(1)}, u32[]{:S(2)}, u32[]{:S(2)}) collective-permute-start(bf16[128,4224]{1,0:T(8,128)(2,1)S(1)} %constant_dynamic-update-slice_fusion.own_ref), channel_id=1, source_target_pairs={{0,1},{1,0},{2,3},{3,2},{4,5},{5,4},{6,7},{7,6},{8,9},{9,8},{10,11... | collective-permute-start | bytes 3244040 | tf_op jit(solution)/shard_map/ppermute | solution.py:183
  36.7 18.3 %collective-permute-start.20 = (bf16[128,4224]{1,0:T(8,128)(2,1)S(1)}, bf16[128,4224]{1,0:T(8,128)(2,1)}, u32[]{:S(2)}, u32[]{:S(2)}) collective-permute-start(bf16[128,4224]{1,0:T(8,128)(2,1)S(1)} %constant_dynamic-update-slice_fusion.6.own_ref), channel_id=1, source_target_pairs={{0,1},{1,0},{2,3},{3,2},{4,5},{5,4},{6,7},{7,6},{8,9},{9,8},{10,11... | collective-permute-start | bytes 3244040 | tf_op jit(solution)/shard_map/ppermute | solution.py:183
  36.8 1.0 copy-start
  37.8 12.8 %copy-start.4 = (s32[32]{0:T(128)S(1)}, s32[32]{0:T(128)}, u32[]{:S(2)}) copy-start(s32[32]{0:T(128)} %param.18) | copy-start | bytes 388
  37.8 12.9 %copy-start.1 = (bf16[32,4096]{1,0:T(8,128)(2,1)S(1)}, bf16[32,4096]{1,0:T(8,128)(2,1)}, u32[]{:S(2)}) copy-start(bf16[32,4096]{1,0:T(8,128)(2,1)} %param.13) | copy-start | bytes 786436
  37.8 12.9 %copy-start.2 = (bf16[32,256]{1,0:T(8,128)(2,1)S(1)}, bf16[32,256]{1,0:T(8,128)(2,1)}, u32[]{:S(2)}) copy-start(bf16[32,256]{1,0:T(8,128)(2,1)} %param.16) | copy-start | bytes 49156
  37.8 13.0 %copy-start.3 = (bf16[32,256]{1,0:T(8,128)(2,1)S(1)}, bf16[32,256]{1,0:T(8,128)(2,1)}, u32[]{:S(2)}) copy-start(bf16[32,256]{1,0:T(8,128)(2,1)} %param.17) | copy-start | bytes 49156
  50.1 16.3 %collective-permute-start.6 = (bf16[128,4096]{1,0:T(8,128)(2,1)}, bf16[128,4096]{1,0:T(8,128)(2,1)}, u32[]{:S(2)}, u32[]{:S(2)}) collective-permute-start(bf16[128,4096]{1,0:T(8,128)(2,1)} %get-tuple-element.11), channel_id=1, source_target_pairs={{0,1},{1,0},{2,3},{3,2},{4,5},{5,4},{6,7},{7,6},{8,9},{9,8},{10,11... | collective-permute-start | bytes 3145736 | tf_op jit(solution)/shard_map/ppermute | solution.py:183
  66.4 2.7 %collective-permute-start.21 = (bf16[128,4096]{1,0:T(8,128)(2,1)S(1)}, bf16[128,4096]{1,0:T(8,128)(2,1)S(1)}, u32[]{:S(2)}, u32[]{:S(2)}) collective-permute-start(bf16[128,4096]{1,0:T(8,128)(2,1)S(1)} %get-tuple-element.13), channel_id=1, source_target_pairs={{0,1},{1,0},{2,3},{3,2},{4,5},{5,4},{6,7},{7,6},{8,9},{9,8},{10,11... | collective-permute-start | bytes 3145736 | tf_op jit(solution)/shard_map/ppermute | solution.py:183
  69.4 9.2 %collective-permute-start.7 = (bf16[32,4096]{1,0:T(8,128)(2,1)S(1)}, bf16[32,4096]{1,0:T(8,128)(2,1)S(1)}, u32[]{:S(2)}, u32[]{:S(2)}) collective-permute-start(bf16[32,4096]{1,0:T(8,128)(2,1)S(1)} %slice.97), channel_id=1, source_target_pairs={{0,2},{1,3},{2,0},{3,1},{4,6},{5,7},{6,4},{7,5},{8,10},{9,11},{10,... | collective-permute-start | bytes 786440 | tf_op jit(solution)/shard_map/ppermute | solution.py:183
  71.1 9.3 %collective-permute-start.9 = (bf16[32,4096]{1,0:T(8,128)(2,1)S(1)}, bf16[32,4096]{1,0:T(8,128)(2,1)S(1)}, u32[]{:S(2)}, u32[]{:S(2)}) collective-permute-start(bf16[32,4096]{1,0:T(8,128)(2,1)S(1)} %pad_maximum_fusion), channel_id=1, source_target_pairs={{0,16},{16,0},{1,17},{17,1},{2,18},{18,2},{3,19},{19,3},{4,20},{20... | collective-permute-start | bytes 786440 | tf_op jit(solution)/shard_map/ppermute | solution.py:186
  72.7 13.3 %collective-permute-start.22 = (bf16[32,4096]{1,0:T(8,128)(2,1)S(1)}, bf16[32,4096]{1,0:T(8,128)(2,1)S(1)}, u32[]{:S(2)}, u32[]{:S(2)}) collective-permute-start(bf16[32,4096]{1,0:T(8,128)(2,1)S(1)} %pad_maximum_fusion.1), channel_id=1, source_target_pairs={{0,16},{16,0},{1,17},{17,1},{2,18},{18,2},{3,19},{19,3},{4,20},{20... | collective-permute-start | bytes 786440 | tf_op jit(solution)/shard_map/ppermute | solution.py:186
  73.2 13.3 %collective-permute-start.25 = (bf16[32,4096]{1,0:T(8,128)(2,1)S(1)}, bf16[32,4096]{1,0:T(8,128)(2,1)S(1)}, u32[]{:S(2)}, u32[]{:S(2)}) collective-permute-start(bf16[32,4096]{1,0:T(8,128)(2,1)S(1)} %slice.113), channel_id=1, source_target_pairs={{0,2},{1,3},{2,0},{3,1},{4,6},{5,7},{6,4},{7,5},{8,10},{9,11},{10,... | collective-permute-start | bytes 786440 | tf_op jit(solution)/shard_map/ppermute | solution.py:183
  78.7 16.4 %collective-permute-start.8 = (bf16[16,4096]{1,0:T(8,128)(2,1)S(1)}, bf16[16,4096]{1,0:T(8,128)(2,1)S(1)}, u32[]{:S(2)}, u32[]{:S(2)}) collective-permute-start(bf16[16,4096]{1,0:T(8,128)(2,1)S(1)} %slice.99), channel_id=1, source_target_pairs={{0,16},{16,0},{1,17},{17,1},{2,18},{18,2},{3,19},{19,3},{4,20},{20... | collective-permute-start | bytes 393224 | tf_op jit(solution)/shard_map/ppermute | solution.py:186
  80.4 22.8 %copy-start.5 = (bf16[32,256,256]{2,1,0:T(8,128)(2,1)S(1)}, bf16[32,256,256]{2,1,0:T(8,128)(2,1)}, u32[]{:S(2)}) copy-start(bf16[32,256,256]{2,1,0:T(8,128)(2,1)} %param.15) | copy-start | bytes 12582916
  80.4 7.8 %collective-permute-start.10 = (bf16[16,4096]{1,0:T(8,128)(2,1)S(1)}, bf16[16,4096]{1,0:T(8,128)(2,1)S(1)}, u32[]{:S(2)}, u32[]{:S(2)}) collective-permute-start(bf16[16,4096]{1,0:T(8,128)(2,1)S(1)} %add_convert_fusion.9), channel_id=1, source_target_pairs={{0,2},{1,3},{2,0},{3,1},{4,6},{5,7},{6,4},{7,5},{8,10},{9,11},{10,... | collective-permute-start | bytes 393224 | tf_op jit(solution)/shard_map/ppermute | solution.py:183
  86.0 5.0 %collective-permute-start.23 = (bf16[16,4096]{1,0:T(8,128)(2,1)S(1)}, bf16[16,4096]{1,0:T(8,128)(2,1)S(1)}, u32[]{:S(2)}, u32[]{:S(2)}) collective-permute-start(bf16[16,4096]{1,0:T(8,128)(2,1)S(1)} %add_convert_fusion.7), channel_id=1, source_target_pairs={{0,2},{1,3},{2,0},{3,1},{4,6},{5,7},{6,4},{7,5},{8,10},{9,11},{10,... | collective-permute-start | bytes 393224 | tf_op jit(solution)/shard_map/ppermute | solution.py:183
  86.6 6.4 %collective-permute-start.26 = (bf16[16,4096]{1,0:T(8,128)(2,1)S(1)}, bf16[16,4096]{1,0:T(8,128)(2,1)S(1)}, u32[]{:S(2)}, u32[]{:S(2)}) collective-permute-start(bf16[16,4096]{1,0:T(8,128)(2,1)S(1)} %slice.115), channel_id=1, source_target_pairs={{0,16},{16,0},{1,17},{17,1},{2,18},{18,2},{3,19},{19,3},{4,20},{20... | collective-permute-start | bytes 393224 | tf_op jit(solution)/shard_map/ppermute | solution.py:186
  88.3 6.8 %collective-permute-start.11 = (bf16[16,4096]{1,0:T(8,128)(2,1)S(1)}, bf16[16,4096]{1,0:T(8,128)(2,1)S(1)}, u32[]{:S(2)}, u32[]{:S(2)}) collective-permute-start(bf16[16,4096]{1,0:T(8,128)(2,1)S(1)} %add_convert_fusion.8), channel_id=1, source_target_pairs={{0,4},{1,5},{2,6},{3,7},{4,0},{5,1},{6,2},{7,3},{8,12},{9,13},{10,... | collective-permute-start | bytes 393224 | tf_op jit(solution)/shard_map/ppermute | solution.py:183
  91.1 10.4 %collective-permute-start.24 = (bf16[16,4096]{1,0:T(8,128)(2,1)S(1)}, bf16[16,4096]{1,0:T(8,128)(2,1)S(1)}, u32[]{:S(2)}, u32[]{:S(2)}) collective-permute-start(bf16[16,4096]{1,0:T(8,128)(2,1)S(1)} %add_convert_fusion.6), channel_id=1, source_target_pairs={{0,8},{1,9},{2,10},{3,11},{4,12},{5,13},{6,14},{7,15},{8,0},{9,1},... | collective-permute-start | bytes 393224 | tf_op jit(solution)/shard_map/ppermute | solution.py:183
  93.1 8.4 %collective-permute-start.27 = (bf16[16,4096]{1,0:T(8,128)(2,1)S(1)}, bf16[16,4096]{1,0:T(8,128)(2,1)S(1)}, u32[]{:S(2)}, u32[]{:S(2)}) collective-permute-start(bf16[16,4096]{1,0:T(8,128)(2,1)S(1)} %add_convert_fusion.5), channel_id=1, source_target_pairs={{0,12},{1,13},{2,14},{3,15},{4,8},{5,9},{6,10},{7,11},{8,4},{9,5},... | collective-permute-start | bytes 393224 | tf_op jit(solution)/shard_map/ppermute | solution.py:183
  101.5 5.0 %collective-permute-start.28 = (bf16[16,4096]{1,0:T(8,128)(2,1)S(1)}, bf16[16,4096]{1,0:T(8,128)(2,1)S(1)}, u32[]{:S(2)}, u32[]{:S(2)}) collective-permute-start(bf16[16,4096]{1,0:T(8,128)(2,1)S(1)} %add_convert_fusion.4), channel_id=1, source_target_pairs={{0,16},{16,0},{1,17},{17,1},{2,18},{18,2},{3,19},{19,3},{4,20},{20... | collective-permute-start | bytes 393224 | tf_op jit(solution)/shard_map/ppermute | solution.py:186

commit v2 on v1

v2 whole, which is shorter than its diff:
```python
import functools

import jax
import jax.numpy as jnp
from jax import lax
from jax.experimental import pallas as pl
from jax.experimental.pallas import tpu as pltpu
from jax.sharding import PartitionSpec as P

HEADS = 64
KV_HEADS = 4
HEAD_DIM = 128


def in_hbm(*arrays):
    return [pltpu.with_memory_space_constraint(a, pltpu.HBM) for a in arrays]


def attend_kernel(
    lengths_ref,
    query_src,
    key_src,
    value_src,
    new_key_src,
    new_value_src,
    *rest,
    chunk,
    together,
):
    weight_srcs, context_ref, weight_refs = rest[:3], rest[3], rest[4:7]
    queries, keys, values, new_key, new_value, by_token, mixed, sems = rest[7:]
    row_count, cache_len, width = keys.shape
    groups = width // HEAD_DIM
    per_group = HEADS // KV_HEADS
    heads = groups * per_group
    score_scale = HEAD_DIM ** (-0.5)
    small = [
        pltpu.make_async_copy(source, target, sems.at[0, j])
        for j, (source, target) in enumerate(
            ((query_src, queries), (new_key_src, new_key), (new_value_src, new_value))
        )
    ]
    cached = [
        [
            pltpu.make_async_copy(
                source.at[pl.ds(low, chunk)], target.at[pl.ds(low, chunk)], sems.at[1 + j, place]
            )
            for j, (source, target) in enumerate(((key_src, keys), (value_src, values)))
        ]
        for place, low in enumerate(range(0, row_count, chunk))
    ]
    weights = [
        pltpu.make_async_copy(source, target, sems.at[3, j])
        for j, (source, target) in enumerate(zip(weight_srcs, weight_refs))
    ]
    for copy in small + sum(cached, []) + weights:
        copy.start()
    for copy in small:
        copy.wait()
    for head in range(heads):
        columns = slice(head * HEAD_DIM, (head + 1) * HEAD_DIM)
        by_token[pl.ds(head, row_count, stride=heads), :] = queries[:, columns].astype(jnp.float32)
    group_of = lax.broadcasted_iota(jnp.int32, (heads, HEAD_DIM), 0) // per_group
    position = lax.broadcasted_iota(jnp.int32, (heads, cache_len), 1)
    own_keys = new_key[...].astype(jnp.float32)
    own_values = new_value[...].astype(jnp.float32)
    for place, low in enumerate(range(0, row_count, chunk)):
        for copy in cached[place]:
            copy.wait()
        for first in range(low, low + chunk, together):
            tokens = range(first, first + together)
            spread, scores, own_score = [], [], []
            for token in tokens:
                query = by_token[token * heads : (token + 1) * heads, :]
                spread = jnp.concatenate(
                    [jnp.where(group_of == g, query, 0.0) for g in range(groups)], axis=1
                )
                score = lax.dot_general(
                    spread.astype(jnp.bfloat16),
                    keys[token],
                    (((1,), (1,)), ((), ())),
                    preferred_element_type=jnp.float32,
                )
                scores.append(
                    jnp.where(position < lengths_ref[token], score * score_scale, -1e30)
                )
                own_score.append(
                    jnp.sum(spread * own_keys[token : token + 1], axis=1, keepdims=True)
                )
            scores = jnp.concatenate(scores, axis=0)
            own_score = jnp.concatenate(own_score, axis=0) * score_scale
            top_score = jnp.maximum(jnp.max(scores, axis=1, keepdims=True), own_score)
            exp_scores = jnp.exp(scores - top_score)
            own_exp = jnp.exp(own_score - top_score)
            inverse = 1.0 / (jnp.sum(exp_scores, axis=1, keepdims=True) + own_exp)
            attn_weights = (exp_scores * inverse).astype(jnp.bfloat16)
            own_prob = (own_exp * inverse).astype(jnp.bfloat16).astype(jnp.float32)
            for place_of, token in enumerate(tokens):
                rows = slice(place_of * heads, (place_of + 1) * heads)
                combined = jnp.dot(
                    attn_weights[rows], values[token], preferred_element_type=jnp.float32
                )
                combined = combined + own_prob[rows] * own_values[token : token + 1]
                picked = combined[:, :HEAD_DIM]
                for g in range(1, groups):
                    columns = slice(g * HEAD_DIM, (g + 1) * HEAD_DIM)
                    picked = jnp.where(group_of == g, combined[:, columns], picked)
                mixed[token * heads : (token + 1) * heads, :] = picked
    for head in range(heads):
        columns = slice(head * HEAD_DIM, (head + 1) * HEAD_DIM)
        context_ref[:, columns] = mixed[pl.ds(head, row_count, stride=heads), :].astype(
            jnp.bfloat16
        )
    for copy in weights:
        copy.wait()


def attend_and_stage(
    queries, cache_keys, cache_values, new_key, new_value, cache_lengths, weights
):
    row_count, width = queries.shape
    heads = width // HEAD_DIM
    vmem, hbm = pl.BlockSpec(memory_space=pltpu.VMEM), pl.BlockSpec(memory_space=pltpu.HBM)
    held = (queries, cache_keys, cache_values, new_key, new_value)
    chunk = 8
    out = pl.pallas_call(
        functools.partial(attend_kernel, chunk=chunk, together=4),
        in_specs=[pl.BlockSpec(memory_space=pltpu.SMEM)] + [hbm] * 8,
        out_specs=[vmem] * 4,
        out_shape=[jax.ShapeDtypeStruct(queries.shape, queries.dtype)]
        + [pltpu.VMEM(w.shape, w.dtype) for w in weights],
        scratch_shapes=[pltpu.VMEM(a.shape, a.dtype) for a in held]
        + [pltpu.VMEM((row_count * heads, HEAD_DIM), jnp.float32)] * 2
        + [pltpu.SemaphoreType.DMA((4, max(4, row_count // chunk)))],
        compiler_params=pltpu.CompilerParams(vmem_limit_bytes=16 * 1024 * 1024),
        name="attend_and_stage",
    )(cache_lengths, *in_hbm(*held, *weights))
    return out[0], out[1:]


def norm_kernel(side_ref, *refs):
    sources, (rows_ref, half_ref), held, sems = refs[:4], refs[4:6], refs[6:10], refs[10]
    copies = [
        pltpu.make_async_copy(source, target, sems.at[j])
        for j, (source, target) in enumerate(zip(sources, held))
    ]
    for copy in copies:
        copy.start()
    for copy in copies:
        copy.wait()
    hidden_ref, gain_ref, ids_ref, probs_ref = held
    features = hidden_ref.shape[1]
    row_count = hidden_ref.shape[0]
    lanes = rows_ref.shape[1] - features
    wide = hidden_ref[...].astype(jnp.float32)
    inverse = lax.rsqrt(jnp.mean(wide * wide, axis=1, keepdims=True) + 1e-06)
    normed = wide * inverse * gain_ref[...].astype(jnp.float32).reshape(1, features)
    probs = probs_ref[...]
    share = probs / jnp.sum(probs, axis=0, keepdims=True)
    ids = ids_ref[...]
    place = lax.broadcasted_iota(jnp.int32, (lanes, row_count), 0)
    half_lanes = lanes // 2
    expert_of = jnp.where(place < half_lanes, place, place - half_lanes)
    gates = jnp.zeros((lanes, row_count), jnp.float32)
    for k in range(ids.shape[0]):
        gates = gates + jnp.where(expert_of == ids[k : k + 1], share[k : k + 1], 0.0)
    coarse = gates.astype(jnp.bfloat16).astype(jnp.float32)
    gates = jnp.where(place < half_lanes, coarse, gates - coarse).T
    half = row_count // 2
    first = side_ref[0] == 0

    def store(columns, values):
        values = values.astype(jnp.bfloat16)
        mine = jnp.where(first, values[:half], values[half:])
        rows_ref[:half, columns] = mine
        rows_ref[half:, columns] = jnp.where(first, values[half:], values[:half])
        half_ref[:, columns] = mine

    store(slice(0, features), normed)
    store(slice(features, features + lanes), gates)


def normed_rows(hidden, norm_gain, expert_ids, router_probs, experts):
    row_count, features = hidden.shape
    lanes = 128 * (-(-2 * experts // 128))
    side = lax.axis_index("side").astype(jnp.int32).reshape(1)
    width = features + lanes
    vmem, hbm = pl.BlockSpec(memory_space=pltpu.VMEM), pl.BlockSpec(memory_space=pltpu.HBM)
    held = (hidden, norm_gain, expert_ids.T, router_probs.T)
    return pl.pallas_call(
        norm_kernel,
        in_specs=[pl.BlockSpec(memory_space=pltpu.SMEM)] + [hbm] * 4,
        out_specs=(vmem, vmem),
        out_shape=(
            jax.ShapeDtypeStruct((row_count, width), jnp.bfloat16),
            jax.ShapeDtypeStruct((row_count // 2, width), jnp.bfloat16),
        ),
        scratch_shapes=[pltpu.VMEM(a.shape, a.dtype) for a in held]
        + [pltpu.SemaphoreType.DMA((4,))],
        compiler_params=pltpu.CompilerParams(vmem_limit_bytes=8 * 1024 * 1024),
        name="norm_and_gates",
    )(side, *in_hbm(*held))


def expert_kernel(
    expert_ref,
    early_own_ref,
    early_other_ref,
    late_own_ref,
    late_other_ref,
    gate_ref,
    up_ref,
    down_ref,
    own_out,
    other_out,
    activation,
):
    features = gate_ref.shape[1]
    rows = own_out.shape[0]
    sources = (early_own_ref, late_own_ref, early_other_ref, late_other_ref)
    x = jnp.concatenate([ref[:, :features] for ref in sources], axis=0)
    tail = jnp.concatenate([ref[:, features:] for ref in sources], axis=0)
    lanes = tail.shape[1]
    lane = lax.broadcasted_iota(jnp.int32, tail.shape, 1)
    mine = (lane == expert_ref[0]) | (lane == expert_ref[0] + lanes // 2)
    share = jnp.sum(jnp.where(mine, tail.astype(jnp.float32), 0.0), axis=1, keepdims=True)
    for low in range(0, gate_ref.shape[2], 256):
        units = slice(low, low + 256)
        gate_act = jnp.dot(x, gate_ref[0, :, units], preferred_element_type=jnp.float32)
        up_act = jnp.dot(x, up_ref[0, :, units], preferred_element_type=jnp.float32)
        activation[:, units] = (jax.nn.silu(gate_act) * up_act * share).astype(jnp.bfloat16)
    hidden_units = activation[...]
    for low in range(0, features, 1024):
        columns = slice(low, low + 1024)
        part = jnp.dot(
            hidden_units, down_ref[0, :, columns], preferred_element_type=jnp.float32
        ).astype(jnp.bfloat16)
        own_out[:, columns] = part[:rows]
        other_out[:, columns] = part[rows:]


def expert_rows(early_own, early_other, late_own, late_other, weights):
    rows = early_own.shape[0] + late_own.shape[0]
    _, features, hidden_units = weights[0].shape
    expert = lax.axis_index("dev").astype(jnp.int32).reshape(1)
    vmem = pl.BlockSpec(memory_space=pltpu.VMEM)
    return pl.pallas_call(
        expert_kernel,
        in_specs=[pl.BlockSpec(memory_space=pltpu.SMEM)] + [vmem] * 7,
        out_specs=(vmem, vmem),
        out_shape=(jax.ShapeDtypeStruct((rows, features), jnp.bfloat16),) * 2,
        scratch_shapes=[pltpu.VMEM((2 * rows, hidden_units), jnp.bfloat16)],
        compiler_params=pltpu.CompilerParams(vmem_limit_bytes=24 * 1024 * 1024),
        name="expert_rows",
    )(
        expert,
        early_own,
        early_other,
        late_own,
        late_other,
        *(pltpu.with_memory_space_constraint(w, pltpu.VMEM) for w in weights),
    )


def add(*parts):
    total = parts[0].astype(jnp.float32)
    for part in parts[1:]:
        total = total + part.astype(jnp.float32)
    return total


def add_rounded(*parts):
    return add(*parts).astype(jnp.bfloat16)


def per_device(
    queries,
    cache_keys,
    cache_values,
    new_key,
    new_value,
    cache_lengths,
    hidden,
    norm_gain,
    expert_ids,
    router_probs,
    w_gate,
    w_up,
    w_down,
):
    devices = lax.axis_size("dev")
    planes = devices // 4
    experts = w_gate.shape[0] * devices

    def over(bit):
        return lambda a: lax.ppermute(a, "dev", [(d, d ^ bit) for d in range(devices)])

    core, across = over(1), over(2)
    sides = lambda a: lax.ppermute(a, "side", [(0, 1), (1, 0)])

    own_rows, own_half = normed_rows(hidden, norm_gain, expert_ids, router_probs, experts)
    half = own_half.shape[0]
    arrived = {i: over(4 * i)(own_half) for i in range(1, planes)}
    beside_own = across(own_rows)
    context, weights = attend_and_stage(
        queries,
        cache_keys,
        cache_values,
        new_key,
        new_value,
        cache_lengths,
        (w_gate, w_up, w_down),
    )
    far = range(2, planes)
    context, weights, waited = lax.optimization_barrier(
        (context, weights, [arrived[i] for i in far])
    )
    arrived.update(zip(far, waited))

    blocks = {}
    for first in range(planes - 2, -1, -2):
        early, late = [], []
        for i in (first, first + 1):
            if i == 0:
                early += [own_rows, beside_own]
                continue
            mine = arrived[i]
            beside, facing = across(mine), sides(mine)
            early += [mine, facing, beside]
            late.append(sides(beside) if i % 4 != 3 else across(facing))
        early, late = jnp.concatenate(early, axis=0), jnp.concatenate(late, axis=0)
        blocks[first] = (early, core(early), late, core(late))

    reduced = {}
    for first in range(planes - 2, -1, -2):
        own_out, other_out = expert_rows(*blocks[first], weights)
        merged = add_rounded(own_out, core(other_out))
        rows = [merged[j * half : (j + 1) * half] for j in range(8)]
        rows = (rows[:4], rows[4:]) if first == 0 else (rows[:3] + rows[6:7], rows[3:6] + rows[7:])
        for i, (mine, facing, beside, diagonal) in zip((first, first + 1), rows):
            if i % 4 in (0, 3):
                got = across(jnp.concatenate([beside, diagonal], axis=0))
                parts = (add(mine, got[:half]), sides(add_rounded(facing, got[half:])))
            else:
                got = sides(jnp.concatenate([facing, diagonal], axis=0))
                parts = (add(mine, got[:half]), across(add_rounded(beside, got[half:])))
            if i == 0:
                reduced[i] = add(*parts)
            else:
                reduced[i] = over(4 * i)(add_rounded(*parts))
    total = add_rounded(*(reduced[i] for i in range(planes)))
    partner = sides(total)
    first = lax.axis_index("side") == 0
    moe_out = jnp.concatenate(
        [jnp.where(first, total, partner), jnp.where(first, partner, total)], axis=0
    )
    return (context, moe_out)


def solution(mesh):
    in_specs = (
        P("dev", "side"),
        P("dev", None, "side"),
        P("dev", None, "side"),
        P("dev", "side"),
        P("dev", "side"),
        P("dev"),
        P("dev", None),
        P(),
        P("dev", None),
        P("dev", None),
        P("dev", None, "side"),
        P("dev", None, "side"),
        P("dev", "side", None),
    )
    out_specs = (P("dev", "side"), P("dev", None))
    return jax.shard_map(
        per_device, mesh=mesh, in_specs=in_specs, out_specs=out_specs, check_vma=False
    )
```

time: 108 us -> 95.8 us (0.89)
  local copies, waits for them, and re-layouts: 7.22 us -> 0.93 us
  waiting for transfers between devices: 30.2 us -> 36 us
  matrix products: 4.67 us -> 0 us
  Pallas kernels: 25.6 us -> 21.7 us
  other arithmetic: 3.51 us -> 1.68 us
    ppermute x10, waiting for transfers between devices: 8.99 us -> 19.1 us  [per_device(): sides = lambda a: lax.ppermute(a, 'side', [(0, 1), (1, 0)])]
    unnamed x28 -> x12, local copies, waits for them, and re-layouts: 5.75 us -> 0.81 us
    dot_general x3 -> x0, matrix products: 4.67 us -> none  [the longest x1 3.5 us: attend_local(): jnp.einsum('tgqd,tlgd->tgql', query_heads, key_heads, preferred_element_t...]
    ppermute x19 -> x21, waiting for transfers between devices: 21.2 us -> 17 us  [over(): lax.ppermute(a, 'dev', [(d, d ^ bit) for d in range(devices)])]
    pallas_call x2 -> x3, Pallas kernels: 23.6 us -> 20.5 us  [the longest x1 10.3 us: attend_and_stage(): pl.pallas_call(functools.partial(attend_kernel, chunk=chunk, together=4),...]
    ppermute x10, starting transfers between devices: 12.4 us -> 10.7 us  [per_device(): sides = lambda a: lax.ppermute(a, 'side', [(0, 1), (1, 0)])]
    reshape x2 -> x0, local copies, waits for them, and re-layouts: 1.32 us -> none  [the longest x1 1.31 us: normed_rows(): norm_gain.reshape(1, features)]
    convert_element_type x10 -> x8, other arithmetic: 2.14 us -> 0.88 us  [add_rounded(): return add(*parts).astype(jnp.bfloat16)]
  transfers between devices with their start and end apart: 29 -> 31, of which waited for: 12 -> 14; matrix products, arithmetic and copies ran while one was open for 9% -> 1% of each run, Pallas kernels for 22% -> 21%
where the time goes in v2:
time: 95.8 us; the launch traced here: 95.6 us
  waiting for transfers between devices  36 us (38%)
  starting transfers between devices  34.4 us (36%)
  Pallas kernels  21.7 us (23%)
  other arithmetic  1.68 us (2%)
    ppermute x21, starting transfers between devices, over(): lax.ppermute(a, 'dev', [(d, d ^ bit) for d in range(devices)])  23.7 us
    ppermute x10, waiting for transfers between devices, per_device(): sides = lambda a: lax.ppermute(a, 'side', [(0, 1), (1, 0)])  19.1 us
    ppermute x21, waiting for transfers between devices, over(): lax.ppermute(a, 'dev', [(d, d ^ bit) for d in range(devices)])  17 us
    ppermute x10, starting transfers between devices, per_device(): sides = lambda a: lax.ppermute(a, 'side', [(0, 1), (1, 0)])  10.7 us
    pallas_call x1, Pallas kernels, attend_and_stage(): pl.pallas_call(functools.partial(attend_kernel, chunk=chunk, together=4),...  10.3 us
    pallas_call x2, Pallas kernels, expert_rows(): pl.pallas_call(expert_kernel, in_specs=[pl.BlockSpec(memory_space=pltpu.S...  10.2 us
  transfers between devices with their start and end apart: 31, of which 14 were waited for; matrix products, arithmetic and copies ran while one was open for 1% of the time, Pallas kernels for 21%

profile of v2, /device:TPU:0, one launch (start us, length us, event | category | flops | bytes accessed | tf_op | source)
XLA Modules:
  0.0 95.6 jit_solution(1324331076365746993)
XLA Ops:
  0.6 1.2 %norm_and_gates.1 = (bf16[32,4224]{1,0:T(8,128)(2,1)S(1)}, bf16[16,4224]{1,0:T(8,128)(2,1)S(1)}) custom-call(s32[1]{0:T(128)} %bitcast.side_ref, bf16[32,4096]{1,0:T(8,128)(2,1)} %refs_0_.1, bf16[4096]{0:T(1024)(128)(2,1)} %refs_1_.1, s32[8,32]{1,0:T(8,128)} %bitcast.4, f32[8,32]{1,0:T(8,128)} %bitcast.5), custom_call_target="tpu_custom_call" | custom-call | tf_op jit(solution)/shard_map/norm_and_gates/pallas_call | solution.py:190
  1.9 4.1 %collective-permute-start = (bf16[16,4224]{1,0:T(8,128)(2,1)S(1)}, bf16[16,4224]{1,0:T(8,128)(2,1)S(1)}, u32[]{:S(2)}, u32[]{:S(2)}) collective-permute-start(bf16[16,4224]{1,0:T(8,128)(2,1)S(1)} %get-tuple-element.22), channel_id=1, source_target_pairs={{0,8},{1,9},{2,10},{3,11},{4,12},{5,13},{6,14},{7,15},{8,0},{9,1},... | collective-permute-start | bytes 405512 | tf_op jit(solution)/shard_map/ppermute | solution.py:296
  6.0 1.3 %collective-permute-start.1 = (bf16[16,4224]{1,0:T(8,128)(2,1)S(1)}, bf16[16,4224]{1,0:T(8,128)(2,1)S(1)}, u32[]{:S(2)}, u32[]{:S(2)}) collective-permute-start(bf16[16,4224]{1,0:T(8,128)(2,1)S(1)} %get-tuple-element.22), channel_id=1, source_target_pairs={{0,12},{1,13},{2,14},{3,15},{4,8},{5,9},{6,10},{7,11},{8,4},{9,5},... | collective-permute-start | bytes 405512 | tf_op jit(solution)/shard_map/ppermute | solution.py:296
  7.3 0.2 collective-permute-start.3
  7.6 1.5 %collective-permute-start.2 = (bf16[32,4224]{1,0:T(8,128)(2,1)S(1)}, bf16[32,4224]{1,0:T(8,128)(2,1)S(1)}, u32[]{:S(2)}, u32[]{:S(2)}) collective-permute-start(bf16[32,4224]{1,0:T(8,128)(2,1)S(1)} %get-tuple-element.24), channel_id=1, source_target_pairs={{0,2},{1,3},{2,0},{3,1},{4,6},{5,7},{6,4},{7,5},{8,10},{9,11},{10,... | collective-permute-start | bytes 811016 | tf_op jit(solution)/shard_map/ppermute | solution.py:296
  9.1 0.6 copy-done
  9.7 10.3 %attend_and_stage.1 = (bf16[32,4096]{1,0:T(8,128)(2,1)}, bf16[1,4096,768]{2,1,0:T(8,128)(2,1)S(1)}, bf16[1,4096,768]{2,1,0:T(8,128)(2,1)S(1)}, bf16[1,768,4096]{2,1,0:T(8,128)(2,1)S(1)}) custom-call(s32[32]{0:T(128)S(1)} %copy-done, bf16[32,4096]{1,0:T(8,128)(2,1)} %query_src.1, bf16[32,256,256]{2,1,0:T(8,128)(2,1)} %key_src.1, ...), custom_call_target="tpu_custom_call" | custom-call | tf_op jit(solution)/shard_map/attend_and_stage/pallas_call | solution.py:126
  20.1 1.6 %collective-permute-start.15 = (bf16[16,4224]{1,0:T(8,128)(2,1)S(1)}, bf16[16,4224]{1,0:T(8,128)(2,1)S(1)}, u32[]{:S(2)}, u32[]{:S(2)}) collective-permute-start(bf16[16,4224]{1,0:T(8,128)(2,1)S(1)} %collective-permute-done), channel_id=1, source_target_pairs={{0,16},{16,0},{1,17},{17,1},{2,18},{18,2},{3,19},{19,3},{4,20},{20... | collective-permute-start | bytes 405512 | tf_op jit(solution)/shard_map/ppermute | solution.py:299
  21.7 0.6 collective-permute-start.16
  22.3 0.5 collective-permute-start.17
  22.8 1.5 %collective-permute-start.18 = (bf16[16,4224]{1,0:T(8,128)(2,1)S(1)}, bf16[16,4224]{1,0:T(8,128)(2,1)S(1)}, u32[]{:S(2)}, u32[]{:S(2)}) collective-permute-start(bf16[16,4224]{1,0:T(8,128)(2,1)S(1)} %collective-permute-done.1), channel_id=1, source_target_pairs={{0,2},{1,3},{2,0},{3,1},{4,6},{5,7},{6,4},{7,5},{8,10},{9,11},{10,... | collective-permute-start | bytes 405512 | tf_op jit(solution)/shard_map/ppermute | solution.py:296
  24.3 2.2 %collective-permute-done.15 = bf16[16,4224]{1,0:T(8,128)(2,1)S(1)} collective-permute-done((bf16[16,4224]{1,0:T(8,128)(2,1)S(1)}, bf16[16,4224]{1,0:T(8,128)(2,1)S(1)}, u32[]{:S(2)}, u32[]{:S(2)}) %collective-permute-start.15) | collective-permute-done | bytes 135200 | tf_op jit(solution)/shard_map/ppermute | solution.py:299
  26.5 1.5 %collective-permute-start.4 = (bf16[16,4224]{1,0:T(8,128)(2,1)S(1)}, bf16[16,4224]{1,0:T(8,128)(2,1)S(1)}, u32[]{:S(2)}, u32[]{:S(2)}) collective-permute-start(bf16[16,4224]{1,0:T(8,128)(2,1)S(1)} %collective-permute-done.3), channel_id=1, source_target_pairs={{0,16},{16,0},{1,17},{17,1},{2,18},{18,2},{3,19},{19,3},{4,20},{20... | collective-permute-start | bytes 405512 | tf_op jit(solution)/shard_map/ppermute | solution.py:299
  28.1 0.6 collective-permute-start.5
  28.7 0.4 collective-permute-done.17
  29.1 1.2 %collective-permute-done.18 = bf16[16,4224]{1,0:T(8,128)(2,1)S(1)} collective-permute-done((bf16[16,4224]{1,0:T(8,128)(2,1)S(1)}, bf16[16,4224]{1,0:T(8,128)(2,1)S(1)}, u32[]{:S(2)}, u32[]{:S(2)}) %collective-permute-start.18) | collective-permute-done | bytes 135200 | tf_op jit(solution)/shard_map/ppermute | solution.py:296
  30.4 0.6 collective-permute-start.20
  31.0 1.3 %collective-permute-start.21 = (bf16[16,4224]{1,0:T(8,128)(2,1)S(1)}, bf16[16,4224]{1,0:T(8,128)(2,1)S(1)}, u32[]{:S(2)}, u32[]{:S(2)}) collective-permute-start(bf16[16,4224]{1,0:T(8,128)(2,1)S(1)} %collective-permute-done.17), channel_id=1, source_target_pairs={{0,2},{1,3},{2,0},{3,1},{4,6},{5,7},{6,4},{7,5},{8,10},{9,11},{10,... | collective-permute-start | bytes 405512 | tf_op jit(solution)/shard_map/ppermute | solution.py:296
  32.4 4.0 %collective-permute-done.20 = bf16[16,4224]{1,0:T(8,128)(2,1)S(1)} collective-permute-done((bf16[16,4224]{1,0:T(8,128)(2,1)S(1)}, bf16[16,4224]{1,0:T(8,128)(2,1)S(1)}, u32[]{:S(2)}, u32[]{:S(2)}) %collective-permute-start.20) | collective-permute-done | bytes 135200 | tf_op jit(solution)/shard_map/ppermute | solution.py:299
  36.4 0.3 collective-permute-done.21
  36.8 1.5 %collective-permute-done.22.late_other_ref = bf16[32,4224]{1,0:T(8,128)(2,1)S(1)} collective-permute-done((bf16[32,4224]{1,0:T(8,128)(2,1)S(1)}, bf16[32,4224]{1,0:T(8,128)(2,1)S(1)}, u32[]{:S(2)}, u32[]{:S(2)}) %collective-permute-start.22) | collective-permute-done | bytes 270368 | tf_op jit(solution)/shard_map/ppermute | solution.py:296
  38.3 5.1 %expert_rows.3 = (bf16[128,4096]{1,0:T(8,128)(2,1)S(1)}, bf16[128,4096]{1,0:T(8,128)(2,1)S(1)}) custom-call(s32[1]{0:T(128)} %bitcast.3.expert_ref, bf16[96,4224]{1,0:T(8,128)(2,1)S(1)} %constant_dynamic-update-slice_fusion.5.early_own_ref, bf16[96,4224]{1,0:T(8,128)(2,1)S(1)} %collective-permute-done.19.early_other_ref, ...), custom_call_target="tpu_custom_call" | custom-call | tf_op jit(solution)/shard_map/expert_rows/pallas_call | solution.py:247
  43.6 0.4 collective-permute-start.6
  44.0 1.5 %collective-permute-start.7 = (bf16[16,4224]{1,0:T(8,128)(2,1)S(1)}, bf16[16,4224]{1,0:T(8,128)(2,1)S(1)}, u32[]{:S(2)}, u32[]{:S(2)}) collective-permute-start(bf16[16,4224]{1,0:T(8,128)(2,1)S(1)} %collective-permute-done.5), channel_id=1, source_target_pairs={{0,16},{16,0},{1,17},{17,1},{2,18},{18,2},{3,19},{19,3},{4,20},{20... | collective-permute-start | bytes 405512 | tf_op jit(solution)/shard_map/ppermute | solution.py:299
  45.5 4.2 %collective-permute-done.7.late_own_ref = bf16[16,4224]{1,0:T(8,128)(2,1)S(1)} collective-permute-done((bf16[16,4224]{1,0:T(8,128)(2,1)S(1)}, bf16[16,4224]{1,0:T(8,128)(2,1)S(1)}, u32[]{:S(2)}, u32[]{:S(2)}) %collective-permute-start.7) | collective-permute-done | bytes 135200 | tf_op jit(solution)/shard_map/ppermute | solution.py:299
  49.7 1.4 %collective-permute-done.8.late_other_ref = bf16[16,4224]{1,0:T(8,128)(2,1)S(1)} collective-permute-done((bf16[16,4224]{1,0:T(8,128)(2,1)S(1)}, bf16[16,4224]{1,0:T(8,128)(2,1)S(1)}, u32[]{:S(2)}, u32[]{:S(2)}) %collective-permute-start.8) | collective-permute-done | bytes 135200 | tf_op jit(solution)/shard_map/ppermute | solution.py:296
  51.0 5.1 %expert_rows.2 = (bf16[128,4096]{1,0:T(8,128)(2,1)S(1)}, bf16[128,4096]{1,0:T(8,128)(2,1)S(1)}) custom-call(s32[1]{0:T(128)} %bitcast.3.expert_ref, bf16[112,4224]{1,0:T(8,128)(2,1)S(1)} %constant_dynamic-update-slice_fusion.early_own_ref, bf16[112,4224]{1,0:T(8,128)(2,1)S(1)} %collective-permute-done.6.early_other_ref, ...), custom_call_target="tpu_custom_call" | custom-call | tf_op jit(solution)/shard_map/expert_rows/pallas_call | solution.py:247
  56.1 0.2 collective-permute-start.9
  56.3 0.3 add_convert_fusion
  56.7 1.5 %collective-permute-start.24 = (bf16[32,4096]{1,0:T(8,128)(2,1)S(1)}, bf16[32,4096]{1,0:T(8,128)(2,1)S(1)}, u32[]{:S(2)}, u32[]{:S(2)}) collective-permute-start(bf16[32,4096]{1,0:T(8,128)(2,1)S(1)} %pad_maximum_fusion.1), channel_id=1, source_target_pairs={{0,16},{16,0},{1,17},{17,1},{2,18},{18,2},{3,19},{19,3},{4,20},{20... | collective-permute-start | bytes 786440 | tf_op jit(solution)/shard_map/ppermute | solution.py:299
  58.3 0.6 collective-permute-start.27
  58.9 0.2 add_convert_fusion.1
  59.2 1.6 %collective-permute-start.10 = (bf16[32,4096]{1,0:T(8,128)(2,1)S(1)}, bf16[32,4096]{1,0:T(8,128)(2,1)S(1)}, u32[]{:S(2)}, u32[]{:S(2)}) collective-permute-start(bf16[32,4096]{1,0:T(8,128)(2,1)S(1)} %concatenate.32), channel_id=1, source_target_pairs={{0,2},{1,3},{2,0},{3,1},{4,6},{5,7},{6,4},{7,5},{8,10},{9,11},{10,... | collective-permute-start | bytes 786440 | tf_op jit(solution)/shard_map/ppermute | solution.py:296
  60.7 4.6 %collective-permute-done.24 = bf16[32,4096]{1,0:T(8,128)(2,1)S(1)} collective-permute-done((bf16[32,4096]{1,0:T(8,128)(2,1)S(1)}, bf16[32,4096]{1,0:T(8,128)(2,1)S(1)}, u32[]{:S(2)}, u32[]{:S(2)}) %collective-permute-start.24) | collective-permute-done | bytes 262176 | tf_op jit(solution)/shard_map/ppermute | solution.py:299
  65.4 1.4 %collective-permute-start.25 = (bf16[16,4096]{1,0:T(8,128)(2,1)S(1)}, bf16[16,4096]{1,0:T(8,128)(2,1)S(1)}, u32[]{:S(2)}, u32[]{:S(2)}) collective-permute-start(bf16[16,4096]{1,0:T(8,128)(2,1)S(1)} %add_convert_fusion.6), channel_id=1, source_target_pairs={{0,2},{1,3},{2,0},{3,1},{4,6},{5,7},{6,4},{7,5},{8,10},{9,11},{10,... | collective-permute-start | bytes 393224 | tf_op jit(solution)/shard_map/ppermute | solution.py:296
  66.7 0.8 collective-permute-start.12
  67.5 7.5 %collective-permute-done.25 = bf16[16,4096]{1,0:T(8,128)(2,1)S(1)} collective-permute-done((bf16[16,4096]{1,0:T(8,128)(2,1)S(1)}, bf16[16,4096]{1,0:T(8,128)(2,1)S(1)}, u32[]{:S(2)}, u32[]{:S(2)}) %collective-permute-start.25) | collective-permute-done | bytes 131104 | tf_op jit(solution)/shard_map/ppermute | solution.py:296
  75.1 0.6 collective-permute-start.28
  75.7 2.8 %collective-permute-start.26 = (bf16[16,4096]{1,0:T(8,128)(2,1)S(1)}, bf16[16,4096]{1,0:T(8,128)(2,1)S(1)}, u32[]{:S(2)}, u32[]{:S(2)}) collective-permute-start(bf16[16,4096]{1,0:T(8,128)(2,1)S(1)} %get-tuple-element.38), channel_id=1, source_target_pairs={{0,8},{1,9},{2,10},{3,11},{4,12},{5,13},{6,14},{7,15},{8,0},{9,1},... | collective-permute-start | bytes 393224 | tf_op jit(solution)/shard_map/ppermute | solution.py:296
  78.6 1.3 %collective-permute-start.13 = (bf16[16,4096]{1,0:T(8,128)(2,1)S(1)}, bf16[16,4096]{1,0:T(8,128)(2,1)S(1)}, u32[]{:S(2)}, u32[]{:S(2)}) collective-permute-start(bf16[16,4096]{1,0:T(8,128)(2,1)S(1)} %get-tuple-element.35), channel_id=1, source_target_pairs={{0,2},{1,3},{2,0},{3,1},{4,6},{5,7},{6,4},{7,5},{8,10},{9,11},{10,... | collective-permute-start | bytes 393224 | tf_op jit(solution)/shard_map/ppermute | solution.py:296
  79.9 0.7 collective-permute-start.11
  80.7 2.8 %collective-permute-start.29 = (bf16[16,4096]{1,0:T(8,128)(2,1)S(1)}, bf16[16,4096]{1,0:T(8,128)(2,1)S(1)}, u32[]{:S(2)}, u32[]{:S(2)}) collective-permute-start(bf16[16,4096]{1,0:T(8,128)(2,1)S(1)} %add_convert_fusion.3), channel_id=1, source_target_pairs={{0,12},{1,13},{2,14},{3,15},{4,8},{5,9},{6,10},{7,11},{8,4},{9,5},... | collective-permute-start | bytes 393224 | tf_op jit(solution)/shard_map/ppermute | solution.py:296
  83.6 1.1 %collective-permute-start.14 = (bf16[16,4096]{1,0:T(8,128)(2,1)S(1)}, bf16[16,4096]{1,0:T(8,128)(2,1)S(1)}, u32[]{:S(2)}, u32[]{:S(2)}) collective-permute-start(bf16[16,4096]{1,0:T(8,128)(2,1)S(1)} %add_convert_fusion.7), channel_id=1, source_target_pairs={{0,4},{1,5},{2,6},{3,7},{4,0},{5,1},{6,2},{7,3},{8,12},{9,13},{10,... | collective-permute-start | bytes 393224 | tf_op jit(solution)/shard_map/ppermute | solution.py:296
  84.8 3.0 %collective-permute-done.26 = bf16[16,4096]{1,0:T(8,128)(2,1)S(1)} collective-permute-done((bf16[16,4096]{1,0:T(8,128)(2,1)S(1)}, bf16[16,4096]{1,0:T(8,128)(2,1)S(1)}, u32[]{:S(2)}, u32[]{:S(2)}) %collective-permute-start.26) | collective-permute-done | bytes 131104 | tf_op jit(solution)/shard_map/ppermute | solution.py:296
  87.8 2.0 %collective-permute-done.14 = bf16[16,4096]{1,0:T(8,128)(2,1)S(1)} collective-permute-done((bf16[16,4096]{1,0:T(8,128)(2,1)S(1)}, bf16[16,4096]{1,0:T(8,128)(2,1)S(1)}, u32[]{:S(2)}, u32[]{:S(2)}) %collective-permute-start.14) | collective-permute-done | bytes 131104 | tf_op jit(solution)/shard_map/ppermute | solution.py:296
  89.9 1.4 %collective-permute-start.30 = (bf16[16,4096]{1,0:T(8,128)(2,1)S(1)}, bf16[16,4096]{1,0:T(8,128)(2,1)S(1)}, u32[]{:S(2)}, u32[]{:S(2)}) collective-permute-start(bf16[16,4096]{1,0:T(8,128)(2,1)S(1)} %add_convert_fusion.2), channel_id=1, source_target_pairs={{0,16},{16,0},{1,17},{17,1},{2,18},{18,2},{3,19},{19,3},{4,20},{20... | collective-permute-start | bytes 393224 | tf_op jit(solution)/shard_map/ppermute | solution.py:299
  91.2 3.7 %collective-permute-done.30 = bf16[16,4096]{1,0:T(8,128)(2,1)S(1)} collective-permute-done((bf16[16,4096]{1,0:T(8,128)(2,1)S(1)}, bf16[16,4096]{1,0:T(8,128)(2,1)S(1)}, u32[]{:S(2)}, u32[]{:S(2)}) %collective-permute-start.30) | collective-permute-done | bytes 131104 | tf_op jit(solution)/shard_map/ppermute | solution.py:299
  94.9 0.7 pad_maximum_fusion.3
  (49 shorter events, 1.3 us)
Async XLA Ops:
  1.9 18.2 %collective-permute-start = (bf16[16,4224]{1,0:T(8,128)(2,1)S(1)}, bf16[16,4224]{1,0:T(8,128)(2,1)S(1)}, u32[]{:S(2)}, u32[]{:S(2)}) collective-permute-start(bf16[16,4224]{1,0:T(8,128)(2,1)S(1)} %get-tuple-element.22), channel_id=1, source_target_pairs={{0,8},{1,9},{2,10},{3,11},{4,12},{5,13},{6,14},{7,15},{8,0},{9,1},... | collective-permute-start | bytes 405512 | tf_op jit(solution)/shard_map/ppermute | solution.py:296
  6.0 14.1 %collective-permute-start.1 = (bf16[16,4224]{1,0:T(8,128)(2,1)S(1)}, bf16[16,4224]{1,0:T(8,128)(2,1)S(1)}, u32[]{:S(2)}, u32[]{:S(2)}) collective-permute-start(bf16[16,4224]{1,0:T(8,128)(2,1)S(1)} %get-tuple-element.22), channel_id=1, source_target_pairs={{0,12},{1,13},{2,14},{3,15},{4,8},{5,9},{6,10},{7,11},{8,4},{9,5},... | collective-permute-start | bytes 405512 | tf_op jit(solution)/shard_map/ppermute | solution.py:296
  7.3 15.5 %collective-permute-start.3 = (bf16[16,4224]{1,0:T(8,128)(2,1)S(1)}, bf16[16,4224]{1,0:T(8,128)(2,1)S(1)}, u32[]{:S(2)}, u32[]{:S(2)}) collective-permute-start(bf16[16,4224]{1,0:T(8,128)(2,1)S(1)} %get-tuple-element.22), channel_id=1, source_target_pairs={{0,4},{1,5},{2,6},{3,7},{4,0},{5,1},{6,2},{7,3},{8,12},{9,13},{10,... | collective-permute-start | bytes 405512 | tf_op jit(solution)/shard_map/ppermute | solution.py:296
  7.6 23.5 %collective-permute-start.2 = (bf16[32,4224]{1,0:T(8,128)(2,1)S(1)}, bf16[32,4224]{1,0:T(8,128)(2,1)S(1)}, u32[]{:S(2)}, u32[]{:S(2)}) collective-permute-start(bf16[32,4224]{1,0:T(8,128)(2,1)S(1)} %get-tuple-element.24), channel_id=1, source_target_pairs={{0,2},{1,3},{2,0},{3,1},{4,6},{5,7},{6,4},{7,5},{8,10},{9,11},{10,... | collective-permute-start | bytes 811016 | tf_op jit(solution)/shard_map/ppermute | solution.py:296
  9.1 0.7 copy-start
  20.1 6.4 %collective-permute-start.15 = (bf16[16,4224]{1,0:T(8,128)(2,1)S(1)}, bf16[16,4224]{1,0:T(8,128)(2,1)S(1)}, u32[]{:S(2)}, u32[]{:S(2)}) collective-permute-start(bf16[16,4224]{1,0:T(8,128)(2,1)S(1)} %collective-permute-done), channel_id=1, source_target_pairs={{0,16},{16,0},{1,17},{17,1},{2,18},{18,2},{3,19},{19,3},{4,20},{20... | collective-permute-start | bytes 405512 | tf_op jit(solution)/shard_map/ppermute | solution.py:299
  21.7 6.4 %collective-permute-start.16 = (bf16[16,4224]{1,0:T(8,128)(2,1)S(1)}, bf16[16,4224]{1,0:T(8,128)(2,1)S(1)}, u32[]{:S(2)}, u32[]{:S(2)}) collective-permute-start(bf16[16,4224]{1,0:T(8,128)(2,1)S(1)} %collective-permute-done), channel_id=1, source_target_pairs={{0,2},{1,3},{2,0},{3,1},{4,6},{5,7},{6,4},{7,5},{8,10},{9,11},{10,... | collective-permute-start | bytes 405512 | tf_op jit(solution)/shard_map/ppermute | solution.py:296
  22.3 6.8 %collective-permute-start.17 = (bf16[16,4224]{1,0:T(8,128)(2,1)S(1)}, bf16[16,4224]{1,0:T(8,128)(2,1)S(1)}, u32[]{:S(2)}, u32[]{:S(2)}) collective-permute-start(bf16[16,4224]{1,0:T(8,128)(2,1)S(1)} %collective-permute-done.1), channel_id=1, source_target_pairs={{0,16},{16,0},{1,17},{17,1},{2,18},{18,2},{3,19},{19,3},{4,20},{20... | collective-permute-start | bytes 405512 | tf_op jit(solution)/shard_map/ppermute | solution.py:299
  22.8 7.5 %collective-permute-start.18 = (bf16[16,4224]{1,0:T(8,128)(2,1)S(1)}, bf16[16,4224]{1,0:T(8,128)(2,1)S(1)}, u32[]{:S(2)}, u32[]{:S(2)}) collective-permute-start(bf16[16,4224]{1,0:T(8,128)(2,1)S(1)} %collective-permute-done.1), channel_id=1, source_target_pairs={{0,2},{1,3},{2,0},{3,1},{4,6},{5,7},{6,4},{7,5},{8,10},{9,11},{10,... | collective-permute-start | bytes 405512 | tf_op jit(solution)/shard_map/ppermute | solution.py:296
  26.5 10.2 %collective-permute-start.4 = (bf16[16,4224]{1,0:T(8,128)(2,1)S(1)}, bf16[16,4224]{1,0:T(8,128)(2,1)S(1)}, u32[]{:S(2)}, u32[]{:S(2)}) collective-permute-start(bf16[16,4224]{1,0:T(8,128)(2,1)S(1)} %collective-permute-done.3), channel_id=1, source_target_pairs={{0,16},{16,0},{1,17},{17,1},{2,18},{18,2},{3,19},{19,3},{4,20},{20... | collective-permute-start | bytes 405512 | tf_op jit(solution)/shard_map/ppermute | solution.py:299
  28.1 15.5 %collective-permute-start.5 = (bf16[16,4224]{1,0:T(8,128)(2,1)S(1)}, bf16[16,4224]{1,0:T(8,128)(2,1)S(1)}, u32[]{:S(2)}, u32[]{:S(2)}) collective-permute-start(bf16[16,4224]{1,0:T(8,128)(2,1)S(1)} %collective-permute-done.3), channel_id=1, source_target_pairs={{0,2},{1,3},{2,0},{3,1},{4,6},{5,7},{6,4},{7,5},{8,10},{9,11},{10,... | collective-permute-start | bytes 405512 | tf_op jit(solution)/shard_map/ppermute | solution.py:296
  30.3 8.0 %collective-permute-start.19 = (bf16[96,4224]{1,0:T(8,128)(2,1)S(1)}, bf16[96,4224]{1,0:T(8,128)(2,1)S(1)}, u32[]{:S(2)}, u32[]{:S(2)}) collective-permute-start(bf16[96,4224]{1,0:T(8,128)(2,1)S(1)} %constant_dynamic-update-slice_fusion.5.early_own_ref), channel_id=1, source_target_pairs={{0,1},{1,0},{2,3},{3,2},{4,5},{5,4},{6,7},{7,6},{8,9},{9,8},{10,11... | collective-permute-start | bytes 2433032 | tf_op jit(solution)/shard_map/ppermute | solution.py:296
  30.4 6.0 %collective-permute-start.20 = (bf16[16,4224]{1,0:T(8,128)(2,1)S(1)}, bf16[16,4224]{1,0:T(8,128)(2,1)S(1)}, u32[]{:S(2)}, u32[]{:S(2)}) collective-permute-start(bf16[16,4224]{1,0:T(8,128)(2,1)S(1)} %collective-permute-done.16), channel_id=1, source_target_pairs={{0,16},{16,0},{1,17},{17,1},{2,18},{18,2},{3,19},{19,3},{4,20},{20... | collective-permute-start | bytes 405512 | tf_op jit(solution)/shard_map/ppermute | solution.py:299
  31.0 5.7 %collective-permute-start.21 = (bf16[16,4224]{1,0:T(8,128)(2,1)S(1)}, bf16[16,4224]{1,0:T(8,128)(2,1)S(1)}, u32[]{:S(2)}, u32[]{:S(2)}) collective-permute-start(bf16[16,4224]{1,0:T(8,128)(2,1)S(1)} %collective-permute-done.17), channel_id=1, source_target_pairs={{0,2},{1,3},{2,0},{3,1},{4,6},{5,7},{6,4},{7,5},{8,10},{9,11},{10,... | collective-permute-start | bytes 405512 | tf_op jit(solution)/shard_map/ppermute | solution.py:296
  36.7 1.6 %collective-permute-start.22 = (bf16[32,4224]{1,0:T(8,128)(2,1)S(1)}, bf16[32,4224]{1,0:T(8,128)(2,1)S(1)}, u32[]{:S(2)}, u32[]{:S(2)}) collective-permute-start(bf16[32,4224]{1,0:T(8,128)(2,1)S(1)} %constant_dynamic-update-slice_fusion.11.late_own_ref), channel_id=1, source_target_pairs={{0,1},{1,0},{2,3},{3,2},{4,5},{5,4},{6,7},{7,6},{8,9},{9,8},{10,11... | collective-permute-start | bytes 811016 | tf_op jit(solution)/shard_map/ppermute | solution.py:296
  43.4 13.0 %collective-permute-start.23 = (bf16[128,4096]{1,0:T(8,128)(2,1)S(1)}, bf16[128,4096]{1,0:T(8,128)(2,1)S(1)}, u32[]{:S(2)}, u32[]{:S(2)}) collective-permute-start(bf16[128,4096]{1,0:T(8,128)(2,1)S(1)} %get-tuple-element.33), channel_id=1, source_target_pairs={{0,1},{1,0},{2,3},{3,2},{4,5},{5,4},{6,7},{7,6},{8,9},{9,8},{10,11... | collective-permute-start | bytes 3145736 | tf_op jit(solution)/shard_map/ppermute | solution.py:296
  43.6 7.4 %collective-permute-start.6 = (bf16[112,4224]{1,0:T(8,128)(2,1)S(1)}, bf16[112,4224]{1,0:T(8,128)(2,1)S(1)}, u32[]{:S(2)}, u32[]{:S(2)}) collective-permute-start(bf16[112,4224]{1,0:T(8,128)(2,1)S(1)} %constant_dynamic-update-slice_fusion.early_own_ref), channel_id=1, source_target_pairs={{0,1},{1,0},{2,3},{3,2},{4,5},{5,4},{6,7},{7,6},{8,9},{9,8},{10,11... | collective-permute-start | bytes 2838536 | tf_op jit(solution)/shard_map/ppermute | solution.py:296
  44.0 5.6 %collective-permute-start.7 = (bf16[16,4224]{1,0:T(8,128)(2,1)S(1)}, bf16[16,4224]{1,0:T(8,128)(2,1)S(1)}, u32[]{:S(2)}, u32[]{:S(2)}) collective-permute-start(bf16[16,4224]{1,0:T(8,128)(2,1)S(1)} %collective-permute-done.5), channel_id=1, source_target_pairs={{0,16},{16,0},{1,17},{17,1},{2,18},{18,2},{3,19},{19,3},{4,20},{20... | collective-permute-start | bytes 405512 | tf_op jit(solution)/shard_map/ppermute | solution.py:299
  49.7 1.4 %collective-permute-start.8 = (bf16[16,4224]{1,0:T(8,128)(2,1)S(1)}, bf16[16,4224]{1,0:T(8,128)(2,1)S(1)}, u32[]{:S(2)}, u32[]{:S(2)}) collective-permute-start(bf16[16,4224]{1,0:T(8,128)(2,1)S(1)} %collective-permute-done.7.late_own_ref), channel_id=1, source_target_pairs={{0,1},{1,0},{2,3},{3,2},{4,5},{5,4},{6,7},{7,6},{8,9},{9,8},{10,11... | collective-permute-start | bytes 405512 | tf_op jit(solution)/shard_map/ppermute | solution.py:296
  56.1 2.7 %collective-permute-start.9 = (bf16[128,4096]{1,0:T(8,128)(2,1)S(1)}, bf16[128,4096]{1,0:T(8,128)(2,1)S(1)}, u32[]{:S(2)}, u32[]{:S(2)}) collective-permute-start(bf16[128,4096]{1,0:T(8,128)(2,1)S(1)} %get-tuple-element.29), channel_id=1, source_target_pairs={{0,1},{1,0},{2,3},{3,2},{4,5},{5,4},{6,7},{7,6},{8,9},{9,8},{10,11... | collective-permute-start | bytes 3145736 | tf_op jit(solution)/shard_map/ppermute | solution.py:296
  56.7 8.6 %collective-permute-start.24 = (bf16[32,4096]{1,0:T(8,128)(2,1)S(1)}, bf16[32,4096]{1,0:T(8,128)(2,1)S(1)}, u32[]{:S(2)}, u32[]{:S(2)}) collective-permute-start(bf16[32,4096]{1,0:T(8,128)(2,1)S(1)} %pad_maximum_fusion.1), channel_id=1, source_target_pairs={{0,16},{16,0},{1,17},{17,1},{2,18},{18,2},{3,19},{19,3},{4,20},{20... | collective-permute-start | bytes 786440 | tf_op jit(solution)/shard_map/ppermute | solution.py:299
  58.3 9.3 %collective-permute-start.27 = (bf16[32,4096]{1,0:T(8,128)(2,1)S(1)}, bf16[32,4096]{1,0:T(8,128)(2,1)S(1)}, u32[]{:S(2)}, u32[]{:S(2)}) collective-permute-start(bf16[32,4096]{1,0:T(8,128)(2,1)S(1)} %pad_maximum_fusion.2), channel_id=1, source_target_pairs={{0,2},{1,3},{2,0},{3,1},{4,6},{5,7},{6,4},{7,5},{8,10},{9,11},{10,... | collective-permute-start | bytes 786440 | tf_op jit(solution)/shard_map/ppermute | solution.py:296
  59.2 19.3 %collective-permute-start.10 = (bf16[32,4096]{1,0:T(8,128)(2,1)S(1)}, bf16[32,4096]{1,0:T(8,128)(2,1)S(1)}, u32[]{:S(2)}, u32[]{:S(2)}) collective-permute-start(bf16[32,4096]{1,0:T(8,128)(2,1)S(1)} %concatenate.32), channel_id=1, source_target_pairs={{0,2},{1,3},{2,0},{3,1},{4,6},{5,7},{6,4},{7,5},{8,10},{9,11},{10,... | collective-permute-start | bytes 786440 | tf_op jit(solution)/shard_map/ppermute | solution.py:296
  65.4 9.7 %collective-permute-start.25 = (bf16[16,4096]{1,0:T(8,128)(2,1)S(1)}, bf16[16,4096]{1,0:T(8,128)(2,1)S(1)}, u32[]{:S(2)}, u32[]{:S(2)}) collective-permute-start(bf16[16,4096]{1,0:T(8,128)(2,1)S(1)} %add_convert_fusion.6), channel_id=1, source_target_pairs={{0,2},{1,3},{2,0},{3,1},{4,6},{5,7},{6,4},{7,5},{8,10},{9,11},{10,... | collective-permute-start | bytes 393224 | tf_op jit(solution)/shard_map/ppermute | solution.py:296
  66.7 11.8 %collective-permute-start.12 = (bf16[32,4096]{1,0:T(8,128)(2,1)S(1)}, bf16[32,4096]{1,0:T(8,128)(2,1)S(1)}, u32[]{:S(2)}, u32[]{:S(2)}) collective-permute-start(bf16[32,4096]{1,0:T(8,128)(2,1)S(1)} %pad_maximum_fusion), channel_id=1, source_target_pairs={{0,16},{16,0},{1,17},{17,1},{2,18},{18,2},{3,19},{19,3},{4,20},{20... | collective-permute-start | bytes 786440 | tf_op jit(solution)/shard_map/ppermute | solution.py:299
  75.1 5.5 %collective-permute-start.28 = (bf16[16,4096]{1,0:T(8,128)(2,1)S(1)}, bf16[16,4096]{1,0:T(8,128)(2,1)S(1)}, u32[]{:S(2)}, u32[]{:S(2)}) collective-permute-start(bf16[16,4096]{1,0:T(8,128)(2,1)S(1)} %get-tuple-element.39), channel_id=1, source_target_pairs={{0,16},{16,0},{1,17},{17,1},{2,18},{18,2},{3,19},{19,3},{4,20},{20... | collective-permute-start | bytes 393224 | tf_op jit(solution)/shard_map/ppermute | solution.py:299
  75.7 12.0 %collective-permute-start.26 = (bf16[16,4096]{1,0:T(8,128)(2,1)S(1)}, bf16[16,4096]{1,0:T(8,128)(2,1)S(1)}, u32[]{:S(2)}, u32[]{:S(2)}) collective-permute-start(bf16[16,4096]{1,0:T(8,128)(2,1)S(1)} %get-tuple-element.38), channel_id=1, source_target_pairs={{0,8},{1,9},{2,10},{3,11},{4,12},{5,13},{6,14},{7,15},{8,0},{9,1},... | collective-permute-start | bytes 393224 | tf_op jit(solution)/shard_map/ppermute | solution.py:296
  78.6 5.0 %collective-permute-start.13 = (bf16[16,4096]{1,0:T(8,128)(2,1)S(1)}, bf16[16,4096]{1,0:T(8,128)(2,1)S(1)}, u32[]{:S(2)}, u32[]{:S(2)}) collective-permute-start(bf16[16,4096]{1,0:T(8,128)(2,1)S(1)} %get-tuple-element.35), channel_id=1, source_target_pairs={{0,2},{1,3},{2,0},{3,1},{4,6},{5,7},{6,4},{7,5},{8,10},{9,11},{10,... | collective-permute-start | bytes 393224 | tf_op jit(solution)/shard_map/ppermute | solution.py:296
  79.9 7.9 %collective-permute-start.11 = (bf16[16,4096]{1,0:T(8,128)(2,1)S(1)}, bf16[16,4096]{1,0:T(8,128)(2,1)S(1)}, u32[]{:S(2)}, u32[]{:S(2)}) collective-permute-start(bf16[16,4096]{1,0:T(8,128)(2,1)S(1)} %get-tuple-element.34), channel_id=1, source_target_pairs={{0,16},{16,0},{1,17},{17,1},{2,18},{18,2},{3,19},{19,3},{4,20},{20... | collective-permute-start | bytes 393224 | tf_op jit(solution)/shard_map/ppermute | solution.py:299
  80.7 7.1 %collective-permute-start.29 = (bf16[16,4096]{1,0:T(8,128)(2,1)S(1)}, bf16[16,4096]{1,0:T(8,128)(2,1)S(1)}, u32[]{:S(2)}, u32[]{:S(2)}) collective-permute-start(bf16[16,4096]{1,0:T(8,128)(2,1)S(1)} %add_convert_fusion.3), channel_id=1, source_target_pairs={{0,12},{1,13},{2,14},{3,15},{4,8},{5,9},{6,10},{7,11},{8,4},{9,5},... | collective-permute-start | bytes 393224 | tf_op jit(solution)/shard_map/ppermute | solution.py:296
  83.6 6.1 %collective-permute-start.14 = (bf16[16,4096]{1,0:T(8,128)(2,1)S(1)}, bf16[16,4096]{1,0:T(8,128)(2,1)S(1)}, u32[]{:S(2)}, u32[]{:S(2)}) collective-permute-start(bf16[16,4096]{1,0:T(8,128)(2,1)S(1)} %add_convert_fusion.7), channel_id=1, source_target_pairs={{0,4},{1,5},{2,6},{3,7},{4,0},{5,1},{6,2},{7,3},{8,12},{9,13},{10,... | collective-permute-start | bytes 393224 | tf_op jit(solution)/shard_map/ppermute | solution.py:296
  89.9 5.0 %collective-permute-start.30 = (bf16[16,4096]{1,0:T(8,128)(2,1)S(1)}, bf16[16,4096]{1,0:T(8,128)(2,1)S(1)}, u32[]{:S(2)}, u32[]{:S(2)}) collective-permute-start(bf16[16,4096]{1,0:T(8,128)(2,1)S(1)} %add_convert_fusion.2), channel_id=1, source_target_pairs={{0,16},{16,0},{1,17},{17,1},{2,18},{18,2},{3,19},{19,3},{4,20},{20... | collective-permute-start | bytes 393224 | tf_op jit(solution)/shard_map/ppermute | solution.py:299

commit v3 on v2

--- a/solution.py
+++ b/solution.py
@@ -24,18 +24,24 @@
     new_key_src,
     new_value_src,
     *rest,
+    start,
     chunk,
     together,
 ):
-    weight_srcs, context_ref, weight_refs = rest[:3], rest[3], rest[4:7]
-    queries, keys, values, new_key, new_value, by_token, mixed, sems = rest[7:]
+    staged = (len(rest) - 9) // 2
+    weight_srcs, context_ref, weight_refs = (
+        rest[:staged],
+        rest[staged],
+        rest[staged + 1 : 2 * staged + 1],
+    )
+    queries, keys, values, new_key, new_value, by_token, mixed, sems = rest[2 * staged + 1 :]
     row_count, cache_len, width = keys.shape
     groups = width // HEAD_DIM
     per_group = HEADS // KV_HEADS
     heads = groups * per_group
     score_scale = HEAD_DIM ** (-0.5)
     small = [
-        pltpu.make_async_copy(source, target, sems.at[0, j])
+        pltpu.make_async_copy(source.at[pl.ds(start, row_count)], target, sems.at[0, j])
         for j, (source, target) in enumerate(
             ((query_src, queries), (new_key_src, new_key), (new_value_src, new_value))
         )
@@ -43,7 +49,9 @@
     cached = [
         [
             pltpu.make_async_copy(
-                source.at[pl.ds(low, chunk)], target.at[pl.ds(low, chunk)], sems.at[1 + j, place]
+                source.at[pl.ds(start + low, chunk)],
+                target.at[pl.ds(low, chunk)],
+                sems.at[1 + j, place],
             )
             for j, (source, target) in enumerate(((key_src, keys), (value_src, values)))
         ]
@@ -82,7 +90,7 @@
                     preferred_element_type=jnp.float32,
                 )
                 scores.append(
-                    jnp.where(position < lengths_ref[token], score * score_scale, -1e30)
+                    jnp.where(position < lengths_ref[start + token], score * score_scale, -1e30)
                 )
                 own_score.append(
                     jnp.sum(spread * own_keys[token : token + 1], axis=1, keepdims=True)
@@ -115,27 +123,58 @@
         copy.wait()
 
 
-def attend_and_stage(
-    queries, cache_keys, cache_values, new_key, new_value, cache_lengths, weights
-):
-    row_count, width = queries.shape
+def attend_and_stage(held, cache_lengths, start, row_count, weights):
+    width = held[0].shape[1]
     heads = width // HEAD_DIM
     vmem, hbm = pl.BlockSpec(memory_space=pltpu.VMEM), pl.BlockSpec(memory_space=pltpu.HBM)
-    held = (queries, cache_keys, cache_values, new_key, new_value)
     chunk = 8
     out = pl.pallas_call(
-        functools.partial(attend_kernel, chunk=chunk, together=4),
-        in_specs=[pl.BlockSpec(memory_space=pltpu.SMEM)] + [hbm] * 8,
-        out_specs=[vmem] * 4,
-        out_shape=[jax.ShapeDtypeStruct(queries.shape, queries.dtype)]
+        functools.partial(attend_kernel, start=start, chunk=chunk, together=4),
+        in_specs=[pl.BlockSpec(memory_space=pltpu.SMEM)] + [hbm] * (5 + len(weights)),
+        out_specs=[vmem] * (1 + len(weights)),
+        out_shape=[jax.ShapeDtypeStruct((row_count, width), held[0].dtype)]
         + [pltpu.VMEM(w.shape, w.dtype) for w in weights],
-        scratch_shapes=[pltpu.VMEM(a.shape, a.dtype) for a in held]
+        scratch_shapes=[pltpu.VMEM((row_count,) + a.shape[1:], a.dtype) for a in held]
         + [pltpu.VMEM((row_count * heads, HEAD_DIM), jnp.float32)] * 2
-        + [pltpu.SemaphoreType.DMA((4, max(4, row_count // chunk)))],
-        compiler_params=pltpu.CompilerParams(vmem_limit_bytes=16 * 1024 * 1024),
+        + [pltpu.SemaphoreType.DMA((4, max(4, -(-row_count // chunk))))],
+        compiler_params=pltpu.CompilerParams(vmem_limit_bytes=10 * 1024 * 1024),
+        cost_estimate=pl.CostEstimate(
+            flops=4 * row_count * heads * held[1].shape[1] * held[1].shape[2],
+            bytes_accessed=4 * row_count * held[1].shape[1] * held[1].shape[2]
+            + sum(2 * w.size for w in weights),
+            transcendentals=row_count * heads * held[1].shape[1],
+        ),
         name="attend_and_stage",
     )(cache_lengths, *in_hbm(*held, *weights))
     return out[0], out[1:]
+
+
+def stage_kernel(*refs):
+    count = (len(refs) - 2) // 2
+    refs[-2][...] = jnp.zeros(refs[-2].shape, jnp.float32)
+    copies = [
+        pltpu.make_async_copy(refs[j], refs[count + j], refs[-1].at[j]) for j in range(count)
+    ]
+    for copy in copies:
+        copy.start()
+    for copy in copies:
+        copy.wait()
+
+
+def staged(weights):
+    return pl.pallas_call(
+        stage_kernel,
+        in_specs=[pl.BlockSpec(memory_space=pltpu.HBM)] * len(weights),
+        out_specs=[pl.BlockSpec(memory_space=pltpu.VMEM)] * (len(weights) + 1),
+        out_shape=[pltpu.VMEM(w.shape, w.dtype) for w in weights]
+        + [jax.ShapeDtypeStruct((8, 128), jnp.float32)],
+        scratch_shapes=[pltpu.SemaphoreType.DMA((len(weights),))],
+        compiler_params=pltpu.CompilerParams(vmem_limit_bytes=4 * 1024 * 1024),
+        cost_estimate=pl.CostEstimate(
+            flops=0, bytes_accessed=sum(4 * w.size for w in weights), transcendentals=0
+        ),
+        name="stage_weights",
+    )(*in_hbm(*weights))
 
 
 def norm_kernel(side_ref, *refs):
@@ -202,24 +241,12 @@
     )(side, *in_hbm(*held))
 
 
-def expert_kernel(
-    expert_ref,
-    early_own_ref,
-    early_other_ref,
-    late_own_ref,
-    late_other_ref,
-    gate_ref,
-    up_ref,
-    down_ref,
-    own_out,
-    other_out,
-    activation,
-):
+def expert_kernel(expert_ref, *refs):
+    gate_ref, up_ref, down_ref, own_out, other_out, activation = refs[-6:]
     features = gate_ref.shape[1]
     rows = own_out.shape[0]
-    sources = (early_own_ref, late_own_ref, early_other_ref, late_other_ref)
-    x = jnp.concatenate([ref[:, :features] for ref in sources], axis=0)
-    tail = jnp.concatenate([ref[:, features:] for ref in sources], axis=0)
+    x = jnp.concatenate([ref[:, :features] for ref in refs[:-6]], axis=0)
+    tail = jnp.concatenate([ref[:, features:] for ref in refs[:-6]], axis=0)
     lanes = tail.shape[1]
     lane = lax.broadcasted_iota(jnp.int32, tail.shape, 1)
     mine = (lane == expert_ref[0]) | (lane == expert_ref[0] + lanes // 2)
@@ -239,25 +266,28 @@
         other_out[:, columns] = part[rows:]
 
 
-def expert_rows(early_own, early_other, late_own, late_other, weights):
-    rows = early_own.shape[0] + late_own.shape[0]
+def expert_rows(own, other, weights):
+    rows = sum(a.shape[0] for a in own)
     _, features, hidden_units = weights[0].shape
     expert = lax.axis_index("dev").astype(jnp.int32).reshape(1)
     vmem = pl.BlockSpec(memory_space=pltpu.VMEM)
     return pl.pallas_call(
         expert_kernel,
-        in_specs=[pl.BlockSpec(memory_space=pltpu.SMEM)] + [vmem] * 7,
+        in_specs=[pl.BlockSpec(memory_space=pltpu.SMEM)] + [vmem] * (2 * len(own) + 3),
         out_specs=(vmem, vmem),
         out_shape=(jax.ShapeDtypeStruct((rows, features), jnp.bfloat16),) * 2,
         scratch_shapes=[pltpu.VMEM((2 * rows, hidden_units), jnp.bfloat16)],
-        compiler_params=pltpu.CompilerParams(vmem_limit_bytes=24 * 1024 * 1024),
+        compiler_params=pltpu.CompilerParams(vmem_limit_bytes=16 * 1024 * 1024),
+        cost_estimate=pl.CostEstimate(
+            flops=12 * rows * features * hidden_units,
+            bytes_accessed=6 * features * hidden_units,
+            transcendentals=2 * rows * hidden_units,
+        ),
         name="expert_rows",
     )(
         expert,
-        early_own,
-        early_other,
-        late_own,
-        late_other,
+        *own,
+        *other,
         *(pltpu.with_memory_space_constraint(w, pltpu.VMEM) for w in weights),
     )
 
@@ -298,56 +328,99 @@
     core, across = over(1), over(2)
     sides = lambda a: lax.ppermute(a, "side", [(0, 1), (1, 0)])
 
+    def opposite(a):
+        pairs = [
+            (s * devices + d, (1 - s) * devices + (d ^ 2)) for s in range(2) for d in range(devices)
+        ]
+        return lax.ppermute(a, ("side", "dev"), pairs)
+
     own_rows, own_half = normed_rows(hidden, norm_gain, expert_ids, router_probs, experts)
     half = own_half.shape[0]
-    arrived = {i: over(4 * i)(own_half) for i in range(1, planes)}
+    arrived = {i: over(4 * i)(own_half) for i in range(1, planes) if i != 3}
     beside_own = across(own_rows)
-    context, weights = attend_and_stage(
-        queries,
-        cache_keys,
-        cache_values,
-        new_key,
-        new_value,
-        cache_lengths,
-        (w_gate, w_up, w_down),
-    )
-    far = range(2, planes)
-    context, weights, waited = lax.optimization_barrier(
-        (context, weights, [arrived[i] for i in far])
-    )
-    arrived.update(zip(far, waited))
-
-    blocks = {}
-    for first in range(planes - 2, -1, -2):
-        early, late = [], []
-        for i in (first, first + 1):
-            if i == 0:
-                early += [own_rows, beside_own]
-                continue
-            mine = arrived[i]
-            beside, facing = across(mine), sides(mine)
-            early += [mine, facing, beside]
-            late.append(sides(beside) if i % 4 != 3 else across(facing))
-        early, late = jnp.concatenate(early, axis=0), jnp.concatenate(late, axis=0)
-        blocks[first] = (early, core(early), late, core(late))
+    held = (queries, cache_keys, cache_values, new_key, new_value)
+    part = queries.shape[0] // 2
+    tie = lax.optimization_barrier
+
+    first_context, _ = attend_and_stage(held, cache_lengths, 0, part, ())
+    near, cache_lengths, first_context = tie((arrived[2], cache_lengths, first_context))
+    arrived[3] = over(4)(near)
+    near_rows = [near, opposite(near), across(near), sides(near)]
+
+    far = {}
+    pairs = [(0, 2), (1, 3)] + [(i, i + 1) for i in range(4, planes, 2)]
+    for first, second in pairs[1:]:
+        far[first] = jnp.concatenate([arrived[first], arrived[second]], axis=0)
+    beside_own, far, w_gate = tie((beside_own, far, w_gate))
+    far_beside = {first: across(rows) for first, rows in far.items()}
+    far_facing = {first: sides(rows) for first, rows in far.items()}
+
+    *weights, done = staged((w_gate, w_up, w_down))
+    near_rows, far_beside, far_facing, done = tie((near_rows, far_beside, far_facing, done))
+
+    stack = jnp.concatenate([own_rows, beside_own, *near_rows], axis=0)
+    blocks = {0: ((stack,), (core(stack),))}
+    for first, rows in far.items():
+        beside, facing = far_beside[first], far_facing[first]
+        late = jnp.concatenate([sides(beside[:half]), across(facing[half:])], axis=0)
+        early = jnp.concatenate([rows, facing, beside], axis=0)
+        blocks[first] = ((early, late), (core(early), core(late)))
+
+    def by_plane(first, merged):
+        rows = [merged[j * half : (j + 1) * half] for j in range(8)]
+        if first == 0:
+            return [rows[4], rows[7], rows[6], rows[5]], rows[:4]
+        return rows[0::2], rows[1::2]
+
+    def to_send(first, merged):
+        one, two = by_plane(first, merged)
+        return (
+            jnp.concatenate([one[1], one[3]], axis=0),
+            jnp.concatenate([two[2], two[3]], axis=0),
+        )
 
     reduced = {}
-    for first in range(planes - 2, -1, -2):
+
+    def exchange(sent):
+        return sides(sent[0]), across(sent[1])
+
+    def step(first, second, merged, got):
+        one, two = by_plane(first, merged)
+        by_side, by_row = (second, first) if first == 0 else (first, second)
+        got_side, got_row = got
+        return {
+            by_side: (add(one[0], got_side[:half]), across(add_rounded(one[2], got_side[half:]))),
+            by_row: (add(two[0], got_row[:half]), sides(add_rounded(two[1], got_row[half:]))),
+        }
+
+    def finish(parts):
+        for i, pair in parts.items():
+            reduced[i] = add(*pair) if i == 0 else over(4 * i)(add_rounded(*pair))
+
+    waiting = parts = None
+    for pair in pairs:
+        first = pair[0]
+        if waiting is not None:
+            blocks[first], waiting = tie((blocks[first], waiting))
+            got = exchange(waiting[1])
         own_out, other_out = expert_rows(*blocks[first], weights)
+        if waiting is not None:
+            own_out, other_out, got = tie((own_out, other_out, got))
+            if parts is not None:
+                finish(parts)
+            parts = step(*before, waiting[0], got)
         merged = add_rounded(own_out, core(other_out))
-        rows = [merged[j * half : (j + 1) * half] for j in range(8)]
-        rows = (rows[:4], rows[4:]) if first == 0 else (rows[:3] + rows[6:7], rows[3:6] + rows[7:])
-        for i, (mine, facing, beside, diagonal) in zip((first, first + 1), rows):
-            if i % 4 in (0, 3):
-                got = across(jnp.concatenate([beside, diagonal], axis=0))
-                parts = (add(mine, got[:half]), sides(add_rounded(facing, got[half:])))
-            else:
-                got = sides(jnp.concatenate([facing, diagonal], axis=0))
-                parts = (add(mine, got[:half]), across(add_rounded(beside, got[half:])))
-            if i == 0:
-                reduced[i] = add(*parts)
-            else:
-                reduced[i] = over(4 * i)(add_rounded(*parts))
+        waiting, before = (merged, to_send(first, merged)), pair
+    waiting, cache_lengths = tie((waiting, cache_lengths))
+    second_context, _ = attend_and_stage(
+        held, cache_lengths, part, queries.shape[0] - part, ()
+    )
+    context = jnp.concatenate([first_context, second_context], axis=0)
+    got, parts = tie((exchange(waiting[1]), parts))
+    finish(parts)
+    parts = step(*before, waiting[0], got)
+    parts, reduced = tie((parts, reduced))
+    finish(parts)
     total = add_rounded(*(reduced[i] for i in range(planes)))
     partner = sides(total)
     first = lax.axis_index("side") == 0

time: 95.8 us -> 87.5 us (0.913)
  waiting for transfers between devices: 36 us -> 23.1 us
  Pallas kernels: 21.7 us -> 28.6 us
  starting transfers between devices: 34.4 us -> 31.2 us
    ppermute x10 -> x8, waiting for transfers between devices: 19.1 us -> 11.9 us  [per_device(): sides = lambda a: lax.ppermute(a, 'side', [(0, 1), (1, 0)])]
    pallas_call x1 -> x3, Pallas kernels: 10.3 us -> 17.2 us  [the longest x2 10.2 us: attend_and_stage(): pl.pallas_call(functools.partial(attend_kernel, start=start, chunk=chunk,...]
    ppermute x21 -> x19, waiting for transfers between devices: 17 us -> 11.2 us  [over(): lax.ppermute(a, 'dev', [(d, d ^ bit) for d in range(devices)])]
    ppermute x21 -> x19, starting transfers between devices: 23.7 us -> 21.1 us  [over(): lax.ppermute(a, 'dev', [(d, d ^ bit) for d in range(devices)])]
    ppermute x10 -> x8, starting transfers between devices: 10.7 us -> 8.55 us  [per_device(): sides = lambda a: lax.ppermute(a, 'side', [(0, 1), (1, 0)])]
    ppermute x0 -> x1, starting transfers between devices: none -> 1.56 us  [opposite(): return lax.ppermute(a, ('side', 'dev'), pairs)]
  transfers between devices with their start and end apart: 31 -> 28, of which waited for: 14 -> 14; matrix products, arithmetic and copies ran while one was open for 1% -> 2% of each run, Pallas kernels for 21% -> 31%
where the time goes in v3:
time: 87.5 us; the launch traced here: 87.4 us
  starting transfers between devices  31.2 us (36%)
  Pallas kernels  28.6 us (33%)
  waiting for transfers between devices  23.1 us (26%)
  other arithmetic  2.49 us (3%)
  local copies, waits for them, and re-layouts  0.97 us (1%)
  between operations  0.91 us (1%)
    ppermute x19, starting transfers between devices, over(): lax.ppermute(a, 'dev', [(d, d ^ bit) for d in range(devices)])  21.1 us
    ppermute x8, waiting for transfers between devices, per_device(): sides = lambda a: lax.ppermute(a, 'side', [(0, 1), (1, 0)])  11.9 us
    ppermute x19, waiting for transfers between devices, over(): lax.ppermute(a, 'dev', [(d, d ^ bit) for d in range(devices)])  11.2 us
    pallas_call x2, Pallas kernels, expert_rows(): pl.pallas_call(expert_kernel, in_specs=[pl.BlockSpec(memory_space=pltpu.S...  10.2 us
    pallas_call x2, Pallas kernels, attend_and_stage(): pl.pallas_call(functools.partial(attend_kernel, start=start, chunk=chunk,...  10.2 us
    ppermute x8, starting transfers between devices, per_device(): sides = lambda a: lax.ppermute(a, 'side', [(0, 1), (1, 0)])  8.55 us
    pallas_call x1, Pallas kernels, staged(): pl.pallas_call(stage_kernel, in_specs=[pl.BlockSpec(memory_space=pltpu.HB...  7.02 us
  transfers between devices with their start and end apart: 28, of which 14 were waited for; matrix products, arithmetic and copies ran while one was open for 2% of the time, Pallas kernels for 31%

profile of v3, /device:TPU:0, one launch (start us, length us, event | category | flops | bytes accessed | tf_op | source)
XLA Modules:
  0.0 87.4 jit_solution(17201235484520629653)
XLA Ops:
  0.6 1.2 %norm_and_gates.1 = (bf16[32,4224]{1,0:T(8,128)(2,1)S(1)}, bf16[16,4224]{1,0:T(8,128)(2,1)S(1)}) custom-call(s32[1]{0:T(128)} %bitcast.side_ref, bf16[32,4096]{1,0:T(8,128)(2,1)} %refs_0_.1, bf16[4096]{0:T(1024)(128)(2,1)} %refs_1_.2, s32[8,32]{1,0:T(8,128)} %bitcast.4, f32[8,32]{1,0:T(8,128)} %bitcast.5), custom_call_target="tpu_custom_call" | custom-call | tf_op jit(solution)/shard_map/norm_and_gates/pallas_call | solution.py:229
  1.9 4.1 %collective-permute-start = (bf16[16,4224]{1,0:T(8,128)(2,1)S(1)}, bf16[16,4224]{1,0:T(8,128)(2,1)S(1)}, u32[]{:S(2)}, u32[]{:S(2)}) collective-permute-start(bf16[16,4224]{1,0:T(8,128)(2,1)S(1)} %get-tuple-element.50), channel_id=1, source_target_pairs={{0,8},{1,9},{2,10},{3,11},{4,12},{5,13},{6,14},{7,15},{8,0},{9,1},... | collective-permute-start | bytes 405512 | tf_op jit(solution)/shard_map/ppermute | solution.py:326
  6.0 1.6 %collective-permute-start.2 = (bf16[16,4224]{1,0:T(8,128)(2,1)S(1)}, bf16[16,4224]{1,0:T(8,128)(2,1)S(1)}, u32[]{:S(2)}, u32[]{:S(2)}) collective-permute-start(bf16[16,4224]{1,0:T(8,128)(2,1)S(1)} %get-tuple-element.50), channel_id=1, source_target_pairs={{0,4},{1,5},{2,6},{3,7},{4,0},{5,1},{6,2},{7,3},{8,12},{9,13},{10,... | collective-permute-start | bytes 405512 | tf_op jit(solution)/shard_map/ppermute | solution.py:326
  7.5 1.5 %collective-permute-start.1 = (bf16[32,4224]{1,0:T(8,128)(2,1)S(1)}, bf16[32,4224]{1,0:T(8,128)(2,1)S(1)}, u32[]{:S(2)}, u32[]{:S(2)}) collective-permute-start(bf16[32,4224]{1,0:T(8,128)(2,1)S(1)} %get-tuple-element.52), channel_id=1, source_target_pairs={{0,2},{1,3},{2,0},{3,1},{4,6},{5,7},{6,4},{7,5},{8,10},{9,11},{10,... | collective-permute-start | bytes 811016 | tf_op jit(solution)/shard_map/ppermute | solution.py:326
  9.0 0.7 copy-done
  9.7 5.1 %attend_and_stage.2 = bf16[16,4096]{1,0:T(8,128)(2,1)S(1)} custom-call(s32[32]{0:T(128)S(1)} %copy-done, bf16[32,4096]{1,0:T(8,128)(2,1)} %query_src.3, bf16[32,256,256]{2,1,0:T(8,128)(2,1)} %key_src.3, bf16[32,256,256]{2,1,0:T(8,128)(2,1)} %value_src.3, bf16[32,256]{1,0:T(8,128)(2,1)} %new_key_src.3, bf16[32,256]{1,0:T(8,128)(2,1)} %new_value_src.3), custom_call_target="tpu_custom_call" | custom-call | flops 134217728 | bytes 4194304 | tf_op jit(solution)/shard_map/attend_and_stage/pallas_call | solution.py:131
  14.8 0.5 collective-permute-start.3
  15.3 1.6 %collective-permute-start.4 = (bf16[16,4224]{1,0:T(8,128)(2,1)S(1)}, bf16[16,4224]{1,0:T(8,128)(2,1)S(1)}, u32[]{:S(2)}, u32[]{:S(2)}) collective-permute-start(bf16[16,4224]{1,0:T(8,128)(2,1)S(1)} %collective-permute-done), channel_id=1, source_target_pairs={{0,18},{1,19},{2,16},{3,17},{4,22},{5,23},{6,20},{7,21},{8,26},{9,... | collective-permute-start | bytes 405512 | tf_op jit(solution)/shard_map/ppermute | solution.py:335
  16.9 1.5 %collective-permute-start.5 = (bf16[16,4224]{1,0:T(8,128)(2,1)S(1)}, bf16[16,4224]{1,0:T(8,128)(2,1)S(1)}, u32[]{:S(2)}, u32[]{:S(2)}) collective-permute-start(bf16[16,4224]{1,0:T(8,128)(2,1)S(1)} %collective-permute-done), channel_id=1, source_target_pairs={{0,2},{1,3},{2,0},{3,1},{4,6},{5,7},{6,4},{7,5},{8,10},{9,11},{10,... | collective-permute-start | bytes 405512 | tf_op jit(solution)/shard_map/ppermute | solution.py:326
  18.4 0.5 collective-permute-start.6
  18.9 1.0 %collective-permute-done.3 = bf16[16,4224]{1,0:T(8,128)(2,1)S(1)} collective-permute-done((bf16[16,4224]{1,0:T(8,128)(2,1)S(1)}, bf16[16,4224]{1,0:T(8,128)(2,1)S(1)}, u32[]{:S(2)}, u32[]{:S(2)}) %collective-permute-start.3) | collective-permute-done | bytes 135200 | tf_op jit(solution)/shard_map/ppermute | solution.py:326
  19.9 0.6 collective-permute-start.7
  20.5 1.5 %collective-permute-start.8 = (bf16[32,4224]{1,0:T(8,128)(2,1)S(1)}, bf16[32,4224]{1,0:T(8,128)(2,1)S(1)}, u32[]{:S(2)}, u32[]{:S(2)}) collective-permute-start(bf16[32,4224]{1,0:T(8,128)(2,1)S(1)} %pad_maximum_fusion), channel_id=1, source_target_pairs={{0,16},{16,0},{1,17},{17,1},{2,18},{18,2},{3,19},{19,3},{4,20},{20... | collective-permute-start | bytes 811016 | tf_op jit(solution)/shard_map/ppermute | solution.py:329
  22.1 7.0 %stage_weights.1 = (bf16[1,4096,768]{2,1,0:T(8,128)(2,1)S(1)}, bf16[1,4096,768]{2,1,0:T(8,128)(2,1)S(1)}, bf16[1,768,4096]{2,1,0:T(8,128)(2,1)S(1)}, f32[8,128]{1,0:T(8,128)}) custom-call(bf16[1,4096,768]{2,1,0:T(8,128)(2,1)} %refs_0_.2, bf16[1,4096,768]{2,1,0:T(8,128)(2,1)} %refs_1_.3, bf16[1,768,4096]{2,1,0:T(8,128)(2,1)} %refs_2_.1), custom_call_target="tpu_custom_call" | custom-call | bytes 37748736 | tf_op jit(solution)/shard_map/stage_weights/pallas_call | solution.py:165
  29.5 0.6 collective-permute-start.11
  30.1 1.4 %collective-permute-start.9 = (bf16[16,4224]{1,0:T(8,128)(2,1)S(1)}, bf16[16,4224]{1,0:T(8,128)(2,1)S(1)}, u32[]{:S(2)}, u32[]{:S(2)}) collective-permute-start(bf16[16,4224]{1,0:T(8,128)(2,1)S(1)} %slice.75), channel_id=1, source_target_pairs={{0,16},{16,0},{1,17},{17,1},{2,18},{18,2},{3,19},{19,3},{4,20},{20... | collective-permute-start | bytes 405512 | tf_op jit(solution)/shard_map/ppermute | solution.py:329
  31.5 0.5 collective-permute-start.10
  32.1 5.1 %expert_rows.2 = (bf16[128,4096]{1,0:T(8,128)(2,1)S(1)}, bf16[128,4096]{1,0:T(8,128)(2,1)S(1)}) custom-call(s32[1]{0:T(128)} %bitcast.3.expert_ref, bf16[128,4224]{1,0:T(8,128)(2,1)S(1)} %constant_dynamic-update-slice_fusion.5.refs_0_, bf16[128,4224]{1,0:T(8,128)(2,1)S(1)} %collective-permute-done.13.refs_1_, ...), custom_call_target="tpu_custom_call" | custom-call | flops 4831838208 | bytes 18874368 | tf_op jit(solution)/shard_map/expert_rows/pallas_call | solution.py:274
  37.2 0.2 collective-permute-start.14
  37.5 0.5 collective-permute-start.12
  37.9 2.0 %collective-permute-done.14 = bf16[128,4096]{1,0:T(8,128)(2,1)S(1)} collective-permute-done((bf16[128,4096]{1,0:T(8,128)(2,1)S(1)}, bf16[128,4096]{1,0:T(8,128)(2,1)S(1)}, u32[]{:S(2)}, u32[]{:S(2)}) %collective-permute-start.14) | collective-permute-done | bytes 1048608 | tf_op jit(solution)/shard_map/ppermute | solution.py:326
  40.0 0.2 add_convert_fusion.1
  40.4 1.5 %collective-permute-start.15 = (bf16[32,4096]{1,0:T(8,128)(2,1)S(1)}, bf16[32,4096]{1,0:T(8,128)(2,1)S(1)}, u32[]{:S(2)}, u32[]{:S(2)}) collective-permute-start(bf16[32,4096]{1,0:T(8,128)(2,1)S(1)} %pad_maximum_fusion.1), channel_id=1, source_target_pairs={{0,16},{16,0},{1,17},{17,1},{2,18},{18,2},{3,19},{19,3},{4,20},{20... | collective-permute-start | bytes 786440 | tf_op jit(solution)/shard_map/ppermute | solution.py:329
  41.8 0.6 collective-permute-start.16
  42.4 5.1 %expert_rows.3 = (bf16[128,4096]{1,0:T(8,128)(2,1)S(1)}, bf16[128,4096]{1,0:T(8,128)(2,1)S(1)}) custom-call(s32[1]{0:T(128)} %bitcast.3.expert_ref, bf16[96,4224]{1,0:T(8,128)(2,1)S(1)} %constant_dynamic-update-slice_fusion.refs_0_, bf16[32,4224]{1,0:T(8,128)(2,1)S(1)} %constant_dynamic-update-slice_fusion.3.refs_1_, ...), custom_call_target="tpu_custom_call" | custom-call | flops 4831838208 | bytes 18874368 | tf_op jit(solution)/shard_map/expert_rows/pallas_call | solution.py:274
  47.5 1.2 %collective-permute-done.15 = bf16[32,4096]{1,0:T(8,128)(2,1)S(1)} collective-permute-done((bf16[32,4096]{1,0:T(8,128)(2,1)S(1)}, bf16[32,4096]{1,0:T(8,128)(2,1)S(1)}, u32[]{:S(2)}, u32[]{:S(2)}) %collective-permute-start.15) | collective-permute-done | bytes 262176 | tf_op jit(solution)/shard_map/ppermute | solution.py:329
  48.7 1.2 %collective-permute-done.16 = bf16[32,4096]{1,0:T(8,128)(2,1)S(1)} collective-permute-done((bf16[32,4096]{1,0:T(8,128)(2,1)S(1)}, bf16[32,4096]{1,0:T(8,128)(2,1)S(1)}, u32[]{:S(2)}, u32[]{:S(2)}) %collective-permute-start.16) | collective-permute-done | bytes 262176 | tf_op jit(solution)/shard_map/ppermute | solution.py:326
  49.9 2.7 %collective-permute-done.17 = bf16[128,4096]{1,0:T(8,128)(2,1)S(1)} collective-permute-done((bf16[128,4096]{1,0:T(8,128)(2,1)S(1)}, bf16[128,4096]{1,0:T(8,128)(2,1)S(1)}, u32[]{:S(2)}, u32[]{:S(2)}) %collective-permute-start.17) | collective-permute-done | bytes 1048608 | tf_op jit(solution)/shard_map/ppermute | solution.py:326
  52.5 0.2 add_convert_fusion
  52.9 0.7 collective-permute-start.18
  53.6 1.4 %collective-permute-start.19 = (bf16[32,4096]{1,0:T(8,128)(2,1)S(1)}, bf16[32,4096]{1,0:T(8,128)(2,1)S(1)}, u32[]{:S(2)}, u32[]{:S(2)}) collective-permute-start(bf16[32,4096]{1,0:T(8,128)(2,1)S(1)} %pad_maximum_fusion.3), channel_id=1, source_target_pairs={{0,2},{1,3},{2,0},{3,1},{4,6},{5,7},{6,4},{7,5},{8,10},{9,11},{10,... | collective-permute-start | bytes 786440 | tf_op jit(solution)/shard_map/ppermute | solution.py:326
  55.1 0.7 collective-permute-start.20
  55.8 1.5 %collective-permute-start.21 = (bf16[16,4096]{1,0:T(8,128)(2,1)S(1)}, bf16[16,4096]{1,0:T(8,128)(2,1)S(1)}, u32[]{:S(2)}, u32[]{:S(2)}) collective-permute-start(bf16[16,4096]{1,0:T(8,128)(2,1)S(1)} %get-tuple-element.102), channel_id=1, source_target_pairs={{0,2},{1,3},{2,0},{3,1},{4,6},{5,7},{6,4},{7,5},{8,10},{9,11},{10,... | collective-permute-start | bytes 393224 | tf_op jit(solution)/shard_map/ppermute | solution.py:326
  57.2 6.9 %collective-permute-done.20 = bf16[16,4096]{1,0:T(8,128)(2,1)S(1)} collective-permute-done((bf16[16,4096]{1,0:T(8,128)(2,1)S(1)}, bf16[16,4096]{1,0:T(8,128)(2,1)S(1)}, u32[]{:S(2)}, u32[]{:S(2)}) %collective-permute-start.20) | collective-permute-done | bytes 131104 | tf_op jit(solution)/shard_map/ppermute | solution.py:329
  64.1 0.3 collective-permute-done.21
  64.5 3.2 %collective-permute-start.24 = (bf16[16,4096]{1,0:T(8,128)(2,1)S(1)}, bf16[16,4096]{1,0:T(8,128)(2,1)S(1)}, u32[]{:S(2)}, u32[]{:S(2)}) collective-permute-start(bf16[16,4096]{1,0:T(8,128)(2,1)S(1)} %add_convert_fusion.5), channel_id=1, source_target_pairs={{0,8},{1,9},{2,10},{3,11},{4,12},{5,13},{6,14},{7,15},{8,0},{9,1},... | collective-permute-start | bytes 393224 | tf_op jit(solution)/shard_map/ppermute | solution.py:326
  67.8 0.6 collective-permute-start.22
  68.5 1.5 %collective-permute-start.23 = (bf16[16,4096]{1,0:T(8,128)(2,1)S(1)}, bf16[16,4096]{1,0:T(8,128)(2,1)S(1)}, u32[]{:S(2)}, u32[]{:S(2)}) collective-permute-start(bf16[16,4096]{1,0:T(8,128)(2,1)S(1)} %get-tuple-element.98), channel_id=1, source_target_pairs={{0,16},{16,0},{1,17},{17,1},{2,18},{18,2},{3,19},{19,3},{4,20},{20... | collective-permute-start | bytes 393224 | tf_op jit(solution)/shard_map/ppermute | solution.py:329
  70.0 3.2 %collective-permute-done.24 = bf16[16,4096]{1,0:T(8,128)(2,1)S(1)} collective-permute-done((bf16[16,4096]{1,0:T(8,128)(2,1)S(1)}, bf16[16,4096]{1,0:T(8,128)(2,1)S(1)}, u32[]{:S(2)}, u32[]{:S(2)}) %collective-permute-start.24) | collective-permute-done | bytes 131104 | tf_op jit(solution)/shard_map/ppermute | solution.py:326
  73.2 0.3 collective-permute-done.23
  73.5 0.3 collective-permute-start.25
  73.9 1.9 %collective-permute-start.26 = (bf16[16,4096]{1,0:T(8,128)(2,1)S(1)}, bf16[16,4096]{1,0:T(8,128)(2,1)S(1)}, u32[]{:S(2)}, u32[]{:S(2)}) collective-permute-start(bf16[16,4096]{1,0:T(8,128)(2,1)S(1)} %add_convert_fusion.3), channel_id=1, source_target_pairs={{0,12},{1,13},{2,14},{3,15},{4,8},{5,9},{6,10},{7,11},{8,4},{9,5},... | collective-permute-start | bytes 393224 | tf_op jit(solution)/shard_map/ppermute | solution.py:326
  75.8 5.1 %attend_and_stage.3 = bf16[16,4096]{1,0:T(8,128)(2,1)S(1)} custom-call(s32[32]{0:T(128)S(1)} %copy-done.1, bf16[32,4096]{1,0:T(8,128)(2,1)} %query_src.3, bf16[32,256,256]{2,1,0:T(8,128)(2,1)} %key_src.3, bf16[32,256,256]{2,1,0:T(8,128)(2,1)} %value_src.3, bf16[32,256]{1,0:T(8,128)(2,1)} %new_key_src.3, bf16[32,256]{1,0:T(8,128)(2,1)} %new_value_src.3), custom_call_target="tpu_custom_call" | custom-call | flops 134217728 | bytes 4194304 | tf_op jit(solution)/shard_map/attend_and_stage/pallas_call | solution.py:131
  80.9 0.6 collective-permute-done.26
  81.6 0.8 collective-permute-start.27
  82.4 0.7 pad_maximum_fusion.4
  83.1 3.5 %collective-permute-done.27 = bf16[16,4096]{1,0:T(8,128)(2,1)S(1)} collective-permute-done((bf16[16,4096]{1,0:T(8,128)(2,1)S(1)}, bf16[16,4096]{1,0:T(8,128)(2,1)S(1)}, u32[]{:S(2)}, u32[]{:S(2)}) %collective-permute-start.27) | collective-permute-done | bytes 131104 | tf_op jit(solution)/shard_map/ppermute | solution.py:329
  86.6 0.7 pad_maximum_fusion.5
  (49 shorter events, 1.2 us)
Async XLA Ops:
  1.9 12.9 %collective-permute-start = (bf16[16,4224]{1,0:T(8,128)(2,1)S(1)}, bf16[16,4224]{1,0:T(8,128)(2,1)S(1)}, u32[]{:S(2)}, u32[]{:S(2)}) collective-permute-start(bf16[16,4224]{1,0:T(8,128)(2,1)S(1)} %get-tuple-element.50), channel_id=1, source_target_pairs={{0,8},{1,9},{2,10},{3,11},{4,12},{5,13},{6,14},{7,15},{8,0},{9,1},... | collective-permute-start | bytes 405512 | tf_op jit(solution)/shard_map/ppermute | solution.py:326
  6.0 12.4 %collective-permute-start.2 = (bf16[16,4224]{1,0:T(8,128)(2,1)S(1)}, bf16[16,4224]{1,0:T(8,128)(2,1)S(1)}, u32[]{:S(2)}, u32[]{:S(2)}) collective-permute-start(bf16[16,4224]{1,0:T(8,128)(2,1)S(1)} %get-tuple-element.50), channel_id=1, source_target_pairs={{0,4},{1,5},{2,6},{3,7},{4,0},{5,1},{6,2},{7,3},{8,12},{9,13},{10,... | collective-permute-start | bytes 405512 | tf_op jit(solution)/shard_map/ppermute | solution.py:326
  7.5 12.3 %collective-permute-start.1 = (bf16[32,4224]{1,0:T(8,128)(2,1)S(1)}, bf16[32,4224]{1,0:T(8,128)(2,1)S(1)}, u32[]{:S(2)}, u32[]{:S(2)}) collective-permute-start(bf16[32,4224]{1,0:T(8,128)(2,1)S(1)} %get-tuple-element.52), channel_id=1, source_target_pairs={{0,2},{1,3},{2,0},{3,1},{4,6},{5,7},{6,4},{7,5},{8,10},{9,11},{10,... | collective-permute-start | bytes 811016 | tf_op jit(solution)/shard_map/ppermute | solution.py:326
  9.0 0.7 copy-start
  14.8 5.1 %collective-permute-start.3 = (bf16[16,4224]{1,0:T(8,128)(2,1)S(1)}, bf16[16,4224]{1,0:T(8,128)(2,1)S(1)}, u32[]{:S(2)}, u32[]{:S(2)}) collective-permute-start(bf16[16,4224]{1,0:T(8,128)(2,1)S(1)} %collective-permute-done), channel_id=1, source_target_pairs={{0,4},{1,5},{2,6},{3,7},{4,0},{5,1},{6,2},{7,3},{8,12},{9,13},{10,... | collective-permute-start | bytes 405512 | tf_op jit(solution)/shard_map/ppermute | solution.py:326
  15.3 13.8 %collective-permute-start.4 = (bf16[16,4224]{1,0:T(8,128)(2,1)S(1)}, bf16[16,4224]{1,0:T(8,128)(2,1)S(1)}, u32[]{:S(2)}, u32[]{:S(2)}) collective-permute-start(bf16[16,4224]{1,0:T(8,128)(2,1)S(1)} %collective-permute-done), channel_id=1, source_target_pairs={{0,18},{1,19},{2,16},{3,17},{4,22},{5,23},{6,20},{7,21},{8,26},{9,... | collective-permute-start | bytes 405512 | tf_op jit(solution)/shard_map/ppermute | solution.py:335
  16.9 12.2 %collective-permute-start.5 = (bf16[16,4224]{1,0:T(8,128)(2,1)S(1)}, bf16[16,4224]{1,0:T(8,128)(2,1)S(1)}, u32[]{:S(2)}, u32[]{:S(2)}) collective-permute-start(bf16[16,4224]{1,0:T(8,128)(2,1)S(1)} %collective-permute-done), channel_id=1, source_target_pairs={{0,2},{1,3},{2,0},{3,1},{4,6},{5,7},{6,4},{7,5},{8,10},{9,11},{10,... | collective-permute-start | bytes 405512 | tf_op jit(solution)/shard_map/ppermute | solution.py:326
  18.4 10.7 %collective-permute-start.6 = (bf16[16,4224]{1,0:T(8,128)(2,1)S(1)}, bf16[16,4224]{1,0:T(8,128)(2,1)S(1)}, u32[]{:S(2)}, u32[]{:S(2)}) collective-permute-start(bf16[16,4224]{1,0:T(8,128)(2,1)S(1)} %collective-permute-done), channel_id=1, source_target_pairs={{0,16},{16,0},{1,17},{17,1},{2,18},{18,2},{3,19},{19,3},{4,20},{20... | collective-permute-start | bytes 405512 | tf_op jit(solution)/shard_map/ppermute | solution.py:329
  19.9 9.3 %collective-permute-start.7 = (bf16[32,4224]{1,0:T(8,128)(2,1)S(1)}, bf16[32,4224]{1,0:T(8,128)(2,1)S(1)}, u32[]{:S(2)}, u32[]{:S(2)}) collective-permute-start(bf16[32,4224]{1,0:T(8,128)(2,1)S(1)} %pad_maximum_fusion), channel_id=1, source_target_pairs={{0,2},{1,3},{2,0},{3,1},{4,6},{5,7},{6,4},{7,5},{8,10},{9,11},{10,... | collective-permute-start | bytes 811016 | tf_op jit(solution)/shard_map/ppermute | solution.py:326
  20.5 8.8 %collective-permute-start.8 = (bf16[32,4224]{1,0:T(8,128)(2,1)S(1)}, bf16[32,4224]{1,0:T(8,128)(2,1)S(1)}, u32[]{:S(2)}, u32[]{:S(2)}) collective-permute-start(bf16[32,4224]{1,0:T(8,128)(2,1)S(1)} %pad_maximum_fusion), channel_id=1, source_target_pairs={{0,16},{16,0},{1,17},{17,1},{2,18},{18,2},{3,19},{19,3},{4,20},{20... | collective-permute-start | bytes 811016 | tf_op jit(solution)/shard_map/ppermute | solution.py:329
  29.3 2.8 %collective-permute-start.13 = (bf16[128,4224]{1,0:T(8,128)(2,1)S(1)}, bf16[128,4224]{1,0:T(8,128)(2,1)S(1)}, u32[]{:S(2)}, u32[]{:S(2)}) collective-permute-start(bf16[128,4224]{1,0:T(8,128)(2,1)S(1)} %constant_dynamic-update-slice_fusion.5.refs_0_), channel_id=1, source_target_pairs={{0,1},{1,0},{2,3},{3,2},{4,5},{5,4},{6,7},{7,6},{8,9},{9,8},{10,11... | collective-permute-start | bytes 3244040 | tf_op jit(solution)/shard_map/ppermute | solution.py:326
  29.5 10.8 %collective-permute-start.11 = (bf16[96,4224]{1,0:T(8,128)(2,1)S(1)}, bf16[96,4224]{1,0:T(8,128)(2,1)S(1)}, u32[]{:S(2)}, u32[]{:S(2)}) collective-permute-start(bf16[96,4224]{1,0:T(8,128)(2,1)S(1)} %constant_dynamic-update-slice_fusion.refs_0_), channel_id=1, source_target_pairs={{0,1},{1,0},{2,3},{3,2},{4,5},{5,4},{6,7},{7,6},{8,9},{9,8},{10,11... | collective-permute-start | bytes 2433032 | tf_op jit(solution)/shard_map/ppermute | solution.py:326
  30.1 7.4 %collective-permute-start.9 = (bf16[16,4224]{1,0:T(8,128)(2,1)S(1)}, bf16[16,4224]{1,0:T(8,128)(2,1)S(1)}, u32[]{:S(2)}, u32[]{:S(2)}) collective-permute-start(bf16[16,4224]{1,0:T(8,128)(2,1)S(1)} %slice.75), channel_id=1, source_target_pairs={{0,16},{16,0},{1,17},{17,1},{2,18},{18,2},{3,19},{19,3},{4,20},{20... | collective-permute-start | bytes 405512 | tf_op jit(solution)/shard_map/ppermute | solution.py:329
  31.5 5.9 %collective-permute-start.10 = (bf16[16,4224]{1,0:T(8,128)(2,1)S(1)}, bf16[16,4224]{1,0:T(8,128)(2,1)S(1)}, u32[]{:S(2)}, u32[]{:S(2)}) collective-permute-start(bf16[16,4224]{1,0:T(8,128)(2,1)S(1)} %slice.76), channel_id=1, source_target_pairs={{0,2},{1,3},{2,0},{3,1},{4,6},{5,7},{6,4},{7,5},{8,10},{9,11},{10,... | collective-permute-start | bytes 405512 | tf_op jit(solution)/shard_map/ppermute | solution.py:326
  37.2 2.7 %collective-permute-start.14 = (bf16[128,4096]{1,0:T(8,128)(2,1)S(1)}, bf16[128,4096]{1,0:T(8,128)(2,1)S(1)}, u32[]{:S(2)}, u32[]{:S(2)}) collective-permute-start(bf16[128,4096]{1,0:T(8,128)(2,1)S(1)} %get-tuple-element.67), channel_id=1, source_target_pairs={{0,1},{1,0},{2,3},{3,2},{4,5},{5,4},{6,7},{7,6},{8,9},{9,8},{10,11... | collective-permute-start | bytes 3145736 | tf_op jit(solution)/shard_map/ppermute | solution.py:326
  37.5 2.9 %collective-permute-start.12 = (bf16[32,4224]{1,0:T(8,128)(2,1)S(1)}, bf16[32,4224]{1,0:T(8,128)(2,1)S(1)}, u32[]{:S(2)}, u32[]{:S(2)}) collective-permute-start(bf16[32,4224]{1,0:T(8,128)(2,1)S(1)} %constant_dynamic-update-slice_fusion.3.refs_1_), channel_id=1, source_target_pairs={{0,1},{1,0},{2,3},{3,2},{4,5},{5,4},{6,7},{7,6},{8,9},{9,8},{10,11... | collective-permute-start | bytes 811016 | tf_op jit(solution)/shard_map/ppermute | solution.py:326
  40.4 8.4 %collective-permute-start.15 = (bf16[32,4096]{1,0:T(8,128)(2,1)S(1)}, bf16[32,4096]{1,0:T(8,128)(2,1)S(1)}, u32[]{:S(2)}, u32[]{:S(2)}) collective-permute-start(bf16[32,4096]{1,0:T(8,128)(2,1)S(1)} %pad_maximum_fusion.1), channel_id=1, source_target_pairs={{0,16},{16,0},{1,17},{17,1},{2,18},{18,2},{3,19},{19,3},{4,20},{20... | collective-permute-start | bytes 786440 | tf_op jit(solution)/shard_map/ppermute | solution.py:329
  41.8 8.1 %collective-permute-start.16 = (bf16[32,4096]{1,0:T(8,128)(2,1)S(1)}, bf16[32,4096]{1,0:T(8,128)(2,1)S(1)}, u32[]{:S(2)}, u32[]{:S(2)}) collective-permute-start(bf16[32,4096]{1,0:T(8,128)(2,1)S(1)} %concatenate.40), channel_id=1, source_target_pairs={{0,2},{1,3},{2,0},{3,1},{4,6},{5,7},{6,4},{7,5},{8,10},{9,11},{10,... | collective-permute-start | bytes 786440 | tf_op jit(solution)/shard_map/ppermute | solution.py:326
  49.9 2.7 %collective-permute-start.17 = (bf16[128,4096]{1,0:T(8,128)(2,1)S(1)}, bf16[128,4096]{1,0:T(8,128)(2,1)S(1)}, u32[]{:S(2)}, u32[]{:S(2)}) collective-permute-start(bf16[128,4096]{1,0:T(8,128)(2,1)S(1)} %get-tuple-element.77), channel_id=1, source_target_pairs={{0,1},{1,0},{2,3},{3,2},{4,5},{5,4},{6,7},{7,6},{8,9},{9,8},{10,11... | collective-permute-start | bytes 3145736 | tf_op jit(solution)/shard_map/ppermute | solution.py:326
  52.9 11.5 %collective-permute-start.18 = (bf16[32,4096]{1,0:T(8,128)(2,1)S(1)}, bf16[32,4096]{1,0:T(8,128)(2,1)S(1)}, u32[]{:S(2)}, u32[]{:S(2)}) collective-permute-start(bf16[32,4096]{1,0:T(8,128)(2,1)S(1)} %pad_maximum_fusion.2), channel_id=1, source_target_pairs={{0,16},{16,0},{1,17},{17,1},{2,18},{18,2},{3,19},{19,3},{4,20},{20... | collective-permute-start | bytes 786440 | tf_op jit(solution)/shard_map/ppermute | solution.py:329
  53.6 10.9 %collective-permute-start.19 = (bf16[32,4096]{1,0:T(8,128)(2,1)S(1)}, bf16[32,4096]{1,0:T(8,128)(2,1)S(1)}, u32[]{:S(2)}, u32[]{:S(2)}) collective-permute-start(bf16[32,4096]{1,0:T(8,128)(2,1)S(1)} %pad_maximum_fusion.3), channel_id=1, source_target_pairs={{0,2},{1,3},{2,0},{3,1},{4,6},{5,7},{6,4},{7,5},{8,10},{9,11},{10,... | collective-permute-start | bytes 786440 | tf_op jit(solution)/shard_map/ppermute | solution.py:326
  55.1 9.0 %collective-permute-start.20 = (bf16[16,4096]{1,0:T(8,128)(2,1)S(1)}, bf16[16,4096]{1,0:T(8,128)(2,1)S(1)}, u32[]{:S(2)}, u32[]{:S(2)}) collective-permute-start(bf16[16,4096]{1,0:T(8,128)(2,1)S(1)} %get-tuple-element.109), channel_id=1, source_target_pairs={{0,16},{16,0},{1,17},{17,1},{2,18},{18,2},{3,19},{19,3},{4,20},{20... | collective-permute-start | bytes 393224 | tf_op jit(solution)/shard_map/ppermute | solution.py:329
  55.8 8.7 %collective-permute-start.21 = (bf16[16,4096]{1,0:T(8,128)(2,1)S(1)}, bf16[16,4096]{1,0:T(8,128)(2,1)S(1)}, u32[]{:S(2)}, u32[]{:S(2)}) collective-permute-start(bf16[16,4096]{1,0:T(8,128)(2,1)S(1)} %get-tuple-element.102), channel_id=1, source_target_pairs={{0,2},{1,3},{2,0},{3,1},{4,6},{5,7},{6,4},{7,5},{8,10},{9,11},{10,... | collective-permute-start | bytes 393224 | tf_op jit(solution)/shard_map/ppermute | solution.py:326
  64.5 8.7 %collective-permute-start.24 = (bf16[16,4096]{1,0:T(8,128)(2,1)S(1)}, bf16[16,4096]{1,0:T(8,128)(2,1)S(1)}, u32[]{:S(2)}, u32[]{:S(2)}) collective-permute-start(bf16[16,4096]{1,0:T(8,128)(2,1)S(1)} %add_convert_fusion.5), channel_id=1, source_target_pairs={{0,8},{1,9},{2,10},{3,11},{4,12},{5,13},{6,14},{7,15},{8,0},{9,1},... | collective-permute-start | bytes 393224 | tf_op jit(solution)/shard_map/ppermute | solution.py:326
  67.8 7.9 %copy-start.1 = (s32[32]{0:T(128)S(1)}, s32[32]{0:T(128)}, u32[]{:S(2)}) copy-start(s32[32]{0:T(128)} %lengths_ref.2) | copy-start | bytes 388
  67.8 5.3 %collective-permute-start.22 = (bf16[16,4096]{1,0:T(8,128)(2,1)S(1)}, bf16[16,4096]{1,0:T(8,128)(2,1)S(1)}, u32[]{:S(2)}, u32[]{:S(2)}) collective-permute-start(bf16[16,4096]{1,0:T(8,128)(2,1)S(1)} %get-tuple-element.107), channel_id=1, source_target_pairs={{0,2},{1,3},{2,0},{3,1},{4,6},{5,7},{6,4},{7,5},{8,10},{9,11},{10,... | collective-permute-start | bytes 393224 | tf_op jit(solution)/shard_map/ppermute | solution.py:326
  68.5 5.0 %collective-permute-start.23 = (bf16[16,4096]{1,0:T(8,128)(2,1)S(1)}, bf16[16,4096]{1,0:T(8,128)(2,1)S(1)}, u32[]{:S(2)}, u32[]{:S(2)}) collective-permute-start(bf16[16,4096]{1,0:T(8,128)(2,1)S(1)} %get-tuple-element.98), channel_id=1, source_target_pairs={{0,16},{16,0},{1,17},{17,1},{2,18},{18,2},{3,19},{19,3},{4,20},{20... | collective-permute-start | bytes 393224 | tf_op jit(solution)/shard_map/ppermute | solution.py:329
  73.5 7.4 %collective-permute-start.25 = (bf16[16,4096]{1,0:T(8,128)(2,1)S(1)}, bf16[16,4096]{1,0:T(8,128)(2,1)S(1)}, u32[]{:S(2)}, u32[]{:S(2)}) collective-permute-start(bf16[16,4096]{1,0:T(8,128)(2,1)S(1)} %add_convert_fusion.4), channel_id=1, source_target_pairs={{0,4},{1,5},{2,6},{3,7},{4,0},{5,1},{6,2},{7,3},{8,12},{9,13},{10,... | collective-permute-start | bytes 393224 | tf_op jit(solution)/shard_map/ppermute | solution.py:326
  73.9 7.6 %collective-permute-start.26 = (bf16[16,4096]{1,0:T(8,128)(2,1)S(1)}, bf16[16,4096]{1,0:T(8,128)(2,1)S(1)}, u32[]{:S(2)}, u32[]{:S(2)}) collective-permute-start(bf16[16,4096]{1,0:T(8,128)(2,1)S(1)} %add_convert_fusion.3), channel_id=1, source_target_pairs={{0,12},{1,13},{2,14},{3,15},{4,8},{5,9},{6,10},{7,11},{8,4},{9,5},... | collective-permute-start | bytes 393224 | tf_op jit(solution)/shard_map/ppermute | solution.py:326
  81.6 5.0 %collective-permute-start.27 = (bf16[16,4096]{1,0:T(8,128)(2,1)S(1)}, bf16[16,4096]{1,0:T(8,128)(2,1)S(1)}, u32[]{:S(2)}, u32[]{:S(2)}) collective-permute-start(bf16[16,4096]{1,0:T(8,128)(2,1)S(1)} %add_convert_fusion.2), channel_id=1, source_target_pairs={{0,16},{16,0},{1,17},{17,1},{2,18},{18,2},{3,19},{19,3},{4,20},{20... | collective-permute-start | bytes 393224 | tf_op jit(solution)/shard_map/ppermute | solution.py:329

commit v4 on v3

--- a/solution.py
+++ b/solution.py
@@ -129,7 +129,7 @@
     vmem, hbm = pl.BlockSpec(memory_space=pltpu.VMEM), pl.BlockSpec(memory_space=pltpu.HBM)
     chunk = 8
     out = pl.pallas_call(
-        functools.partial(attend_kernel, start=start, chunk=chunk, together=4),
+        functools.partial(attend_kernel, start=start, chunk=chunk, together=8),
         in_specs=[pl.BlockSpec(memory_space=pltpu.SMEM)] + [hbm] * (5 + len(weights)),
         out_specs=[vmem] * (1 + len(weights)),
         out_shape=[jax.ShapeDtypeStruct((row_count, width), held[0].dtype)]
@@ -267,13 +267,13 @@
 
 
 def expert_rows(own, other, weights):
-    rows = sum(a.shape[0] for a in own)
+    rows = own.shape[0]
     _, features, hidden_units = weights[0].shape
     expert = lax.axis_index("dev").astype(jnp.int32).reshape(1)
     vmem = pl.BlockSpec(memory_space=pltpu.VMEM)
     return pl.pallas_call(
         expert_kernel,
-        in_specs=[pl.BlockSpec(memory_space=pltpu.SMEM)] + [vmem] * (2 * len(own) + 3),
+        in_specs=[pl.BlockSpec(memory_space=pltpu.SMEM)] + [vmem] * 5,
         out_specs=(vmem, vmem),
         out_shape=(jax.ShapeDtypeStruct((rows, features), jnp.bfloat16),) * 2,
         scratch_shapes=[pltpu.VMEM((2 * rows, hidden_units), jnp.bfloat16)],
@@ -286,8 +286,8 @@
         name="expert_rows",
     )(
         expert,
-        *own,
-        *other,
+        own,
+        other,
         *(pltpu.with_memory_space_constraint(w, pltpu.VMEM) for w in weights),
     )
 
@@ -336,44 +336,37 @@
 
     own_rows, own_half = normed_rows(hidden, norm_gain, expert_ids, router_probs, experts)
     half = own_half.shape[0]
-    arrived = {i: over(4 * i)(own_half) for i in range(1, planes) if i != 3}
-    beside_own = across(own_rows)
+    tie = lax.optimization_barrier
     held = (queries, cache_keys, cache_values, new_key, new_value)
     part = queries.shape[0] // 2
-    tie = lax.optimization_barrier
-
-    first_context, _ = attend_and_stage(held, cache_lengths, 0, part, ())
-    near, cache_lengths, first_context = tie((arrived[2], cache_lengths, first_context))
-    arrived[3] = over(4)(near)
-    near_rows = [near, opposite(near), across(near), sides(near)]
-
-    far = {}
-    pairs = [(0, 2), (1, 3)] + [(i, i + 1) for i in range(4, planes, 2)]
-    for first, second in pairs[1:]:
-        far[first] = jnp.concatenate([arrived[first], arrived[second]], axis=0)
-    beside_own, far, w_gate = tie((beside_own, far, w_gate))
-    far_beside = {first: across(rows) for first, rows in far.items()}
-    far_facing = {first: sides(rows) for first, rows in far.items()}
-
+    direct = [i for i in range(1, planes) if i not in (2, 3)]
+    pairs = [(i, i + 2) for i in range(planes) if i % 4 < 2]
+
+    second_half = over(8)(own_half)
+    own_of = {i: over(4 * i)(own_rows) for i in direct}
+    own_of[0], beside_of = own_rows, {0: across(own_rows)}
     *weights, done = staged((w_gate, w_up, w_down))
-    near_rows, far_beside, far_facing, done = tie((near_rows, far_beside, far_facing, done))
-
-    stack = jnp.concatenate([own_rows, beside_own, *near_rows], axis=0)
-    blocks = {0: ((stack,), (core(stack),))}
-    for first, rows in far.items():
-        beside, facing = far_beside[first], far_facing[first]
-        late = jnp.concatenate([sides(beside[:half]), across(facing[half:])], axis=0)
-        early = jnp.concatenate([rows, facing, beside], axis=0)
-        blocks[first] = ((early, late), (core(early), core(late)))
-
-    def by_plane(first, merged):
+    second_half, beside_of[0], done = tie((second_half, beside_of[0], done))
+    third_half = over(4)(second_half)
+
+    around = [sides(second_half), across(second_half), opposite(second_half)]
+    for i in direct:
+        beside_of[i] = over(4 * i)(beside_of[0])
+    around = jnp.concatenate(around, axis=0)
+    blocks = {i: [own_of[i], beside_of[i]] for i in [0] + direct}
+    blocks[2] = [second_half, around]
+    blocks[3] = [third_half, over(4)(around)]
+    stacks = {}
+    for first, second in pairs:
+        stack = jnp.concatenate(blocks[first] + blocks[second], axis=0)
+        stacks[first] = (stack, core(stack))
+
+    def by_plane(merged):
         rows = [merged[j * half : (j + 1) * half] for j in range(8)]
-        if first == 0:
-            return [rows[4], rows[7], rows[6], rows[5]], rows[:4]
-        return rows[0::2], rows[1::2]
-
-    def to_send(first, merged):
-        one, two = by_plane(first, merged)
+        return rows[4:], rows[:4]
+
+    def to_send(merged):
+        one, two = by_plane(merged)
         return (
             jnp.concatenate([one[1], one[3]], axis=0),
             jnp.concatenate([two[2], two[3]], axis=0),
@@ -385,8 +378,8 @@
         return sides(sent[0]), across(sent[1])
 
     def step(first, second, merged, got):
-        one, two = by_plane(first, merged)
-        by_side, by_row = (second, first) if first == 0 else (first, second)
+        one, two = by_plane(merged)
+        by_side, by_row = second, first
         got_side, got_row = got
         return {
             by_side: (add(one[0], got_side[:half]), across(add_rounded(one[2], got_side[half:]))),
@@ -401,26 +394,28 @@
     for pair in pairs:
         first = pair[0]
         if waiting is not None:
-            blocks[first], waiting = tie((blocks[first], waiting))
+            stacks[first], waiting = tie((stacks[first], waiting))
             got = exchange(waiting[1])
-        own_out, other_out = expert_rows(*blocks[first], weights)
+        own_out, other_out = expert_rows(*stacks[first], weights)
         if waiting is not None:
             own_out, other_out, got = tie((own_out, other_out, got))
             if parts is not None:
                 finish(parts)
             parts = step(*before, waiting[0], got)
         merged = add_rounded(own_out, core(other_out))
-        waiting, before = (merged, to_send(first, merged)), pair
+        waiting, before = (merged, to_send(merged)), pair
     waiting, cache_lengths = tie((waiting, cache_lengths))
+    got = exchange(waiting[1])
+    first_context, _ = attend_and_stage(held, cache_lengths, 0, part, ())
+    got, parts, first_context, cache_lengths = tie((got, parts, first_context, cache_lengths))
+    finish(parts)
+    parts = step(*before, waiting[0], got)
+    parts, reduced, cache_lengths = tie((parts, reduced, cache_lengths))
+    finish(parts)
     second_context, _ = attend_and_stage(
         held, cache_lengths, part, queries.shape[0] - part, ()
     )
     context = jnp.concatenate([first_context, second_context], axis=0)
-    got, parts = tie((exchange(waiting[1]), parts))
-    finish(parts)
-    parts = step(*before, waiting[0], got)
-    parts, reduced = tie((parts, reduced))
-    finish(parts)
     total = add_rounded(*(reduced[i] for i in range(planes)))
     partner = sides(total)
     first = lax.axis_index("side") == 0

time: 87.5 us -> 86.9 us (level)
  waiting for transfers between devices: 23.1 us -> 27.2 us
  starting transfers between devices: 31.2 us -> 28.9 us
  Pallas kernels: 28.6 us -> 26.9 us
    ppermute x19 -> x18, waiting for transfers between devices: 11.2 us -> 18.5 us  [over(): lax.ppermute(a, 'dev', [(d, d ^ bit) for d in range(devices)])]
    ppermute x8 -> x6, waiting for transfers between devices: 11.9 us -> 7.41 us  [per_device(): sides = lambda a: lax.ppermute(a, 'side', [(0, 1), (1, 0)])]
    ppermute x19 -> x18, starting transfers between devices: 21.1 us -> 19.2 us  [over(): lax.ppermute(a, 'dev', [(d, d ^ bit) for d in range(devices)])]
    pallas_call x2, Pallas kernels: 10.2 us -> 8.41 us  [attend_and_stage(): pl.pallas_call(functools.partial(attend_kernel, start=start, chunk=chunk,...]
    ppermute x1, waiting for transfers between devices: 0.01 us -> 1.37 us  [opposite(): return lax.ppermute(a, ('side', 'dev'), pairs)]
    ppermute x8 -> x6, starting transfers between devices: 8.55 us -> 8.27 us  [per_device(): sides = lambda a: lax.ppermute(a, 'side', [(0, 1), (1, 0)])]
  transfers between devices with their start and end apart: 28 -> 25, of which waited for: 14 -> 14; matrix products, arithmetic and copies ran while one was open for 2% -> 2% of each run, Pallas kernels for 31% -> 30%
where the time goes in v4:
time: 86.9 us; the launch traced here: 86.8 us
  starting transfers between devices  28.9 us (33%)
  waiting for transfers between devices  27.2 us (31%)
  Pallas kernels  26.9 us (31%)
  other arithmetic  2.45 us (3%)
  between operations  0.91 us (1%)
    ppermute x18, starting transfers between devices, over(): lax.ppermute(a, 'dev', [(d, d ^ bit) for d in range(devices)])  19.2 us
    ppermute x18, waiting for transfers between devices, over(): lax.ppermute(a, 'dev', [(d, d ^ bit) for d in range(devices)])  18.5 us
    pallas_call x2, Pallas kernels, expert_rows(): pl.pallas_call(expert_kernel, in_specs=[pl.BlockSpec(memory_space=pltpu.S...  10.3 us
    pallas_call x2, Pallas kernels, attend_and_stage(): pl.pallas_call(functools.partial(attend_kernel, start=start, chunk=chunk,...  8.41 us
    ppermute x6, starting transfers between devices, per_device(): sides = lambda a: lax.ppermute(a, 'side', [(0, 1), (1, 0)])  8.27 us
    ppermute x6, waiting for transfers between devices, per_device(): sides = lambda a: lax.ppermute(a, 'side', [(0, 1), (1, 0)])  7.41 us
    pallas_call x1, Pallas kernels, staged(): pl.pallas_call(stage_kernel, in_specs=[pl.BlockSpec(memory_space=pltpu.HB...  7.02 us
  transfers between devices with their start and end apart: 25, of which 14 were waited for; matrix products, arithmetic and copies ran while one was open for 2% of the time, Pallas kernels for 30%

profile of v4, /device:TPU:0, one launch (start us, length us, event | category | flops | bytes accessed | tf_op | source)
XLA Modules:
  0.0 86.8 jit_solution(11783428702011435434)
XLA Ops:
  0.6 1.2 %norm_and_gates.1 = (bf16[32,4224]{1,0:T(8,128)(2,1)S(1)}, bf16[16,4224]{1,0:T(8,128)(2,1)S(1)}) custom-call(s32[1]{0:T(128)} %bitcast.1.side_ref, bf16[32,4096]{1,0:T(8,128)(2,1)} %refs_0_.2, bf16[4096]{0:T(1024)(128)(2,1)} %refs_1_.2, s32[8,32]{1,0:T(8,128)} %bitcast.4, f32[8,32]{1,0:T(8,128)} %bitcast.5), custom_call_target="tpu_custom_call" | custom-call | tf_op jit(solution)/shard_map/norm_and_gates/pallas_call | solution.py:229
  1.9 3.0 %collective-permute-start.2 = (bf16[32,4224]{1,0:T(8,128)(2,1)S(1)}, bf16[32,4224]{1,0:T(8,128)(2,1)S(1)}, u32[]{:S(2)}, u32[]{:S(2)}) collective-permute-start(bf16[32,4224]{1,0:T(8,128)(2,1)S(1)} %get-tuple-element.41), channel_id=1, source_target_pairs={{0,2},{1,3},{2,0},{3,1},{4,6},{5,7},{6,4},{7,5},{8,10},{9,11},{10,... | collective-permute-start | bytes 811016 | tf_op jit(solution)/shard_map/ppermute | solution.py:326
  4.9 1.6 %collective-permute-start = (bf16[32,4224]{1,0:T(8,128)(2,1)S(1)}, bf16[32,4224]{1,0:T(8,128)(2,1)S(1)}, u32[]{:S(2)}, u32[]{:S(2)}) collective-permute-start(bf16[32,4224]{1,0:T(8,128)(2,1)S(1)} %get-tuple-element.41), channel_id=1, source_target_pairs={{0,4},{1,5},{2,6},{3,7},{4,0},{5,1},{6,2},{7,3},{8,12},{9,13},{10,... | collective-permute-start | bytes 811016 | tf_op jit(solution)/shard_map/ppermute | solution.py:326
  6.5 2.6 %collective-permute-start.1 = (bf16[16,4224]{1,0:T(8,128)(2,1)S(1)}, bf16[16,4224]{1,0:T(8,128)(2,1)S(1)}, u32[]{:S(2)}, u32[]{:S(2)}) collective-permute-start(bf16[16,4224]{1,0:T(8,128)(2,1)S(1)} %get-tuple-element.42), channel_id=1, source_target_pairs={{0,8},{1,9},{2,10},{3,11},{4,12},{5,13},{6,14},{7,15},{8,0},{9,1},... | collective-permute-start | bytes 405512 | tf_op jit(solution)/shard_map/ppermute | solution.py:326
  9.1 7.0 %stage_weights.1 = (bf16[1,4096,768]{2,1,0:T(8,128)(2,1)S(1)}, bf16[1,4096,768]{2,1,0:T(8,128)(2,1)S(1)}, bf16[1,768,4096]{2,1,0:T(8,128)(2,1)S(1)}, f32[8,128]{1,0:T(8,128)}) custom-call(bf16[1,4096,768]{2,1,0:T(8,128)(2,1)} %refs_0_.3, bf16[1,4096,768]{2,1,0:T(8,128)(2,1)} %refs_1_.3, bf16[1,768,4096]{2,1,0:T(8,128)(2,1)} %refs_2_.1), custom_call_target="tpu_custom_call" | custom-call | bytes 37748736 | tf_op jit(solution)/shard_map/stage_weights/pallas_call | solution.py:165
  16.1 1.6 %collective-permute-start.5 = (bf16[16,4224]{1,0:T(8,128)(2,1)S(1)}, bf16[16,4224]{1,0:T(8,128)(2,1)S(1)}, u32[]{:S(2)}, u32[]{:S(2)}) collective-permute-start(bf16[16,4224]{1,0:T(8,128)(2,1)S(1)} %collective-permute-done.1), channel_id=1, source_target_pairs={{0,16},{16,0},{1,17},{17,1},{2,18},{18,2},{3,19},{19,3},{4,20},{20... | collective-permute-start | bytes 405512 | tf_op jit(solution)/shard_map/ppermute | solution.py:329
  17.7 0.5 collective-permute-start.6
  18.2 1.4 %collective-permute-start.7 = (bf16[16,4224]{1,0:T(8,128)(2,1)S(1)}, bf16[16,4224]{1,0:T(8,128)(2,1)S(1)}, u32[]{:S(2)}, u32[]{:S(2)}) collective-permute-start(bf16[16,4224]{1,0:T(8,128)(2,1)S(1)} %collective-permute-done.1), channel_id=1, source_target_pairs={{0,18},{1,19},{2,16},{3,17},{4,22},{5,23},{6,20},{7,21},{8,26},{9,... | collective-permute-start | bytes 405512 | tf_op jit(solution)/shard_map/ppermute | solution.py:335
  19.7 2.1 %collective-permute-start.3 = (bf16[32,4224]{1,0:T(8,128)(2,1)S(1)}, bf16[32,4224]{1,0:T(8,128)(2,1)S(1)}, u32[]{:S(2)}, u32[]{:S(2)}) collective-permute-start(bf16[32,4224]{1,0:T(8,128)(2,1)S(1)} %collective-permute-done.2), channel_id=1, source_target_pairs={{0,4},{1,5},{2,6},{3,7},{4,0},{5,1},{6,2},{7,3},{8,12},{9,13},{10,... | collective-permute-start | bytes 811016 | tf_op jit(solution)/shard_map/ppermute | solution.py:326
  21.8 0.1 collective-permute-start.4
  22.0 0.7 collective-permute-done.5
  22.7 0.7 collective-permute-done.6
  23.4 1.4 %collective-permute-done.7 = bf16[16,4224]{1,0:T(8,128)(2,1)S(1)} collective-permute-done((bf16[16,4224]{1,0:T(8,128)(2,1)S(1)}, bf16[16,4224]{1,0:T(8,128)(2,1)S(1)}, u32[]{:S(2)}, u32[]{:S(2)}) %collective-permute-start.7) | collective-permute-done | bytes 135200 | tf_op jit(solution)/shard_map/ppermute | solution.py:335
  24.9 1.6 %collective-permute-start.8 = (bf16[48,4224]{1,0:T(8,128)(2,1)S(1)}, bf16[48,4224]{1,0:T(8,128)(2,1)S(1)}, u32[]{:S(2)}, u32[]{:S(2)}) collective-permute-start(bf16[48,4224]{1,0:T(8,128)(2,1)S(1)} %pad_maximum_fusion), channel_id=1, source_target_pairs={{0,4},{1,5},{2,6},{3,7},{4,0},{5,1},{6,2},{7,3},{8,12},{9,13},{10,... | collective-permute-start | bytes 1216520 | tf_op jit(solution)/shard_map/ppermute | solution.py:326
  26.5 1.2 %collective-permute-done.3 = bf16[32,4224]{1,0:T(8,128)(2,1)S(1)} collective-permute-done((bf16[32,4224]{1,0:T(8,128)(2,1)S(1)}, bf16[32,4224]{1,0:T(8,128)(2,1)S(1)}, u32[]{:S(2)}, u32[]{:S(2)}) %collective-permute-start.3) | collective-permute-done | bytes 270368 | tf_op jit(solution)/shard_map/ppermute | solution.py:326
  27.7 5.1 %expert_rows.2 = (bf16[128,4096]{1,0:T(8,128)(2,1)S(1)}, bf16[128,4096]{1,0:T(8,128)(2,1)S(1)}) custom-call(s32[1]{0:T(128)} %bitcast.expert_ref, bf16[128,4224]{1,0:T(8,128)(2,1)S(1)} %constant_dynamic-update-slice_fusion.4.refs_0_, bf16[128,4224]{1,0:T(8,128)(2,1)S(1)} %collective-permute-done.10.refs_1_, ...), custom_call_target="tpu_custom_call" | custom-call | flops 4831838208 | bytes 18874368 | tf_op jit(solution)/shard_map/expert_rows/pallas_call | solution.py:274
  32.8 0.1 collective-permute-start.11
  32.9 4.9 %collective-permute-done.8 = bf16[48,4224]{1,0:T(8,128)(2,1)S(1)} collective-permute-done((bf16[48,4224]{1,0:T(8,128)(2,1)S(1)}, bf16[48,4224]{1,0:T(8,128)(2,1)S(1)}, u32[]{:S(2)}, u32[]{:S(2)}) %collective-permute-start.8) | collective-permute-done | bytes 405536 | tf_op jit(solution)/shard_map/ppermute | solution.py:326
  37.9 0.2 add_convert_fusion.1
  38.3 2.3 %collective-permute-done.9.refs_1_ = bf16[128,4224]{1,0:T(8,128)(2,1)S(1)} collective-permute-done((bf16[128,4224]{1,0:T(8,128)(2,1)S(1)}, bf16[128,4224]{1,0:T(8,128)(2,1)S(1)}, u32[]{:S(2)}, u32[]{:S(2)}) %collective-permute-start.9) | collective-permute-done | bytes 1081376 | tf_op jit(solution)/shard_map/ppermute | solution.py:326
  40.6 1.5 %collective-permute-start.12 = (bf16[32,4096]{1,0:T(8,128)(2,1)S(1)}, bf16[32,4096]{1,0:T(8,128)(2,1)S(1)}, u32[]{:S(2)}, u32[]{:S(2)}) collective-permute-start(bf16[32,4096]{1,0:T(8,128)(2,1)S(1)} %pad_maximum_fusion.1), channel_id=1, source_target_pairs={{0,16},{16,0},{1,17},{17,1},{2,18},{18,2},{3,19},{19,3},{4,20},{20... | collective-permute-start | bytes 786440 | tf_op jit(solution)/shard_map/ppermute | solution.py:329
  42.1 0.5 collective-permute-start.13
  42.7 5.1 %expert_rows.3 = (bf16[128,4096]{1,0:T(8,128)(2,1)S(1)}, bf16[128,4096]{1,0:T(8,128)(2,1)S(1)}) custom-call(s32[1]{0:T(128)} %bitcast.expert_ref, bf16[128,4224]{1,0:T(8,128)(2,1)S(1)} %constant_dynamic-update-slice_fusion.refs_0_, bf16[128,4224]{1,0:T(8,128)(2,1)S(1)} %collective-permute-done.9.refs_1_, ...), custom_call_target="tpu_custom_call" | custom-call | flops 4831838208 | bytes 18874368 | tf_op jit(solution)/shard_map/expert_rows/pallas_call | solution.py:274
  47.8 1.1 %collective-permute-done.12 = bf16[32,4096]{1,0:T(8,128)(2,1)S(1)} collective-permute-done((bf16[32,4096]{1,0:T(8,128)(2,1)S(1)}, bf16[32,4096]{1,0:T(8,128)(2,1)S(1)}, u32[]{:S(2)}, u32[]{:S(2)}) %collective-permute-start.12) | collective-permute-done | bytes 262176 | tf_op jit(solution)/shard_map/ppermute | solution.py:329
  48.9 1.2 %collective-permute-done.13 = bf16[32,4096]{1,0:T(8,128)(2,1)S(1)} collective-permute-done((bf16[32,4096]{1,0:T(8,128)(2,1)S(1)}, bf16[32,4096]{1,0:T(8,128)(2,1)S(1)}, u32[]{:S(2)}, u32[]{:S(2)}) %collective-permute-start.13) | collective-permute-done | bytes 262176 | tf_op jit(solution)/shard_map/ppermute | solution.py:326
  50.2 2.7 %collective-permute-done.14 = bf16[128,4096]{1,0:T(8,128)(2,1)S(1)} collective-permute-done((bf16[128,4096]{1,0:T(8,128)(2,1)S(1)}, bf16[128,4096]{1,0:T(8,128)(2,1)S(1)}, u32[]{:S(2)}, u32[]{:S(2)}) %collective-permute-start.14) | collective-permute-done | bytes 1048608 | tf_op jit(solution)/shard_map/ppermute | solution.py:326
  52.9 0.2 add_convert_fusion
  53.2 0.6 collective-permute-start.15
  53.8 0.5 collective-permute-start.16
  54.3 0.1 add_convert_fusion.8
  54.4 1.6 %collective-permute-start.17 = (bf16[16,4096]{1,0:T(8,128)(2,1)S(1)}, bf16[16,4096]{1,0:T(8,128)(2,1)S(1)}, u32[]{:S(2)}, u32[]{:S(2)}) collective-permute-start(bf16[16,4096]{1,0:T(8,128)(2,1)S(1)} %get-tuple-element.91), channel_id=1, source_target_pairs={{0,16},{16,0},{1,17},{17,1},{2,18},{18,2},{3,19},{19,3},{4,20},{20... | collective-permute-start | bytes 393224 | tf_op jit(solution)/shard_map/ppermute | solution.py:329
  56.0 1.5 %collective-permute-start.18 = (bf16[16,4096]{1,0:T(8,128)(2,1)S(1)}, bf16[16,4096]{1,0:T(8,128)(2,1)S(1)}, u32[]{:S(2)}, u32[]{:S(2)}) collective-permute-start(bf16[16,4096]{1,0:T(8,128)(2,1)S(1)} %get-tuple-element.84), channel_id=1, source_target_pairs={{0,2},{1,3},{2,0},{3,1},{4,6},{5,7},{6,4},{7,5},{8,10},{9,11},{10,... | collective-permute-start | bytes 393224 | tf_op jit(solution)/shard_map/ppermute | solution.py:326
  57.5 4.2 %attend_and_stage.2 = bf16[16,4096]{1,0:T(8,128)(2,1)S(1)} custom-call(s32[32]{0:T(128)S(1)} %copy-done, bf16[32,4096]{1,0:T(8,128)(2,1)} %query_src.3, bf16[32,256,256]{2,1,0:T(8,128)(2,1)} %key_src.3, bf16[32,256,256]{2,1,0:T(8,128)(2,1)} %value_src.3, bf16[32,256]{1,0:T(8,128)(2,1)} %new_key_src.3, bf16[32,256]{1,0:T(8,128)(2,1)} %new_value_src.3), custom_call_target="tpu_custom_call" | custom-call | flops 134217728 | bytes 4194304 | tf_op jit(solution)/shard_map/attend_and_stage/pallas_call | solution.py:131
  61.7 2.7 %collective-permute-done.17 = bf16[16,4096]{1,0:T(8,128)(2,1)S(1)} collective-permute-done((bf16[16,4096]{1,0:T(8,128)(2,1)S(1)}, bf16[16,4096]{1,0:T(8,128)(2,1)S(1)}, u32[]{:S(2)}, u32[]{:S(2)}) %collective-permute-start.17) | collective-permute-done | bytes 131104 | tf_op jit(solution)/shard_map/ppermute | solution.py:329
  64.4 0.2 collective-permute-done.18
  64.7 1.4 %collective-permute-start.21 = (bf16[16,4096]{1,0:T(8,128)(2,1)S(1)}, bf16[16,4096]{1,0:T(8,128)(2,1)S(1)}, u32[]{:S(2)}, u32[]{:S(2)}) collective-permute-start(bf16[16,4096]{1,0:T(8,128)(2,1)S(1)} %add_convert_fusion.5), channel_id=1, source_target_pairs={{0,8},{1,9},{2,10},{3,11},{4,12},{5,13},{6,14},{7,15},{8,0},{9,1},... | collective-permute-start | bytes 393224 | tf_op jit(solution)/shard_map/ppermute | solution.py:326
  66.1 0.1 add_convert_fusion.6
  66.2 1.6 %collective-permute-start.19 = (bf16[16,4096]{1,0:T(8,128)(2,1)S(1)}, bf16[16,4096]{1,0:T(8,128)(2,1)S(1)}, u32[]{:S(2)}, u32[]{:S(2)}) collective-permute-start(bf16[16,4096]{1,0:T(8,128)(2,1)S(1)} %get-tuple-element.89), channel_id=1, source_target_pairs={{0,16},{16,0},{1,17},{17,1},{2,18},{18,2},{3,19},{19,3},{4,20},{20... | collective-permute-start | bytes 393224 | tf_op jit(solution)/shard_map/ppermute | solution.py:329
  67.8 0.5 collective-permute-start.20
  68.4 4.6 %collective-permute-done.21 = bf16[16,4096]{1,0:T(8,128)(2,1)S(1)} collective-permute-done((bf16[16,4096]{1,0:T(8,128)(2,1)S(1)}, bf16[16,4096]{1,0:T(8,128)(2,1)S(1)}, u32[]{:S(2)}, u32[]{:S(2)}) %collective-permute-start.21) | collective-permute-done | bytes 131104 | tf_op jit(solution)/shard_map/ppermute | solution.py:326
  73.0 0.2 collective-permute-start.22
  73.2 2.8 %collective-permute-start.23 = (bf16[16,4096]{1,0:T(8,128)(2,1)S(1)}, bf16[16,4096]{1,0:T(8,128)(2,1)S(1)}, u32[]{:S(2)}, u32[]{:S(2)}) collective-permute-start(bf16[16,4096]{1,0:T(8,128)(2,1)S(1)} %add_convert_fusion.3), channel_id=1, source_target_pairs={{0,12},{1,13},{2,14},{3,15},{4,8},{5,9},{6,10},{7,11},{8,4},{9,5},... | collective-permute-start | bytes 393224 | tf_op jit(solution)/shard_map/ppermute | solution.py:326
  76.0 4.2 %attend_and_stage.3 = bf16[16,4096]{1,0:T(8,128)(2,1)S(1)} custom-call(s32[32]{0:T(128)S(1)} %copy-done, bf16[32,4096]{1,0:T(8,128)(2,1)} %query_src.3, bf16[32,256,256]{2,1,0:T(8,128)(2,1)} %key_src.3, bf16[32,256,256]{2,1,0:T(8,128)(2,1)} %value_src.3, bf16[32,256]{1,0:T(8,128)(2,1)} %new_key_src.3, bf16[32,256]{1,0:T(8,128)(2,1)} %new_value_src.3), custom_call_target="tpu_custom_call" | custom-call | flops 134217728 | bytes 4194304 | tf_op jit(solution)/shard_map/attend_and_stage/pallas_call | solution.py:131
  80.2 0.7 collective-permute-done.23
  81.0 1.4 %collective-permute-start.24 = (bf16[16,4096]{1,0:T(8,128)(2,1)S(1)}, bf16[16,4096]{1,0:T(8,128)(2,1)S(1)}, u32[]{:S(2)}, u32[]{:S(2)}) collective-permute-start(bf16[16,4096]{1,0:T(8,128)(2,1)S(1)} %add_convert_fusion.2), channel_id=1, source_target_pairs={{0,16},{16,0},{1,17},{17,1},{2,18},{18,2},{3,19},{19,3},{4,20},{20... | collective-permute-start | bytes 393224 | tf_op jit(solution)/shard_map/ppermute | solution.py:329
  82.4 0.7 pad_maximum_fusion.3
  83.1 2.9 %collective-permute-done.24 = bf16[16,4096]{1,0:T(8,128)(2,1)S(1)} collective-permute-done((bf16[16,4096]{1,0:T(8,128)(2,1)S(1)}, bf16[16,4096]{1,0:T(8,128)(2,1)S(1)}, u32[]{:S(2)}, u32[]{:S(2)}) %collective-permute-start.24) | collective-permute-done | bytes 131104 | tf_op jit(solution)/shard_map/ppermute | solution.py:329
  86.0 0.7 pad_maximum_fusion.4
  (39 shorter events, 0.7 us)
Async XLA Ops:
  1.9 14.2 %collective-permute-start.2 = (bf16[32,4224]{1,0:T(8,128)(2,1)S(1)}, bf16[32,4224]{1,0:T(8,128)(2,1)S(1)}, u32[]{:S(2)}, u32[]{:S(2)}) collective-permute-start(bf16[32,4224]{1,0:T(8,128)(2,1)S(1)} %get-tuple-element.41), channel_id=1, source_target_pairs={{0,2},{1,3},{2,0},{3,1},{4,6},{5,7},{6,4},{7,5},{8,10},{9,11},{10,... | collective-permute-start | bytes 811016 | tf_op jit(solution)/shard_map/ppermute | solution.py:326
  4.9 16.9 %collective-permute-start = (bf16[32,4224]{1,0:T(8,128)(2,1)S(1)}, bf16[32,4224]{1,0:T(8,128)(2,1)S(1)}, u32[]{:S(2)}, u32[]{:S(2)}) collective-permute-start(bf16[32,4224]{1,0:T(8,128)(2,1)S(1)} %get-tuple-element.41), channel_id=1, source_target_pairs={{0,4},{1,5},{2,6},{3,7},{4,0},{5,1},{6,2},{7,3},{8,12},{9,13},{10,... | collective-permute-start | bytes 811016 | tf_op jit(solution)/shard_map/ppermute | solution.py:326
  6.5 9.6 %collective-permute-start.1 = (bf16[16,4224]{1,0:T(8,128)(2,1)S(1)}, bf16[16,4224]{1,0:T(8,128)(2,1)S(1)}, u32[]{:S(2)}, u32[]{:S(2)}) collective-permute-start(bf16[16,4224]{1,0:T(8,128)(2,1)S(1)} %get-tuple-element.42), channel_id=1, source_target_pairs={{0,8},{1,9},{2,10},{3,11},{4,12},{5,13},{6,14},{7,15},{8,0},{9,1},... | collective-permute-start | bytes 405512 | tf_op jit(solution)/shard_map/ppermute | solution.py:326
  16.1 6.5 %collective-permute-start.5 = (bf16[16,4224]{1,0:T(8,128)(2,1)S(1)}, bf16[16,4224]{1,0:T(8,128)(2,1)S(1)}, u32[]{:S(2)}, u32[]{:S(2)}) collective-permute-start(bf16[16,4224]{1,0:T(8,128)(2,1)S(1)} %collective-permute-done.1), channel_id=1, source_target_pairs={{0,16},{16,0},{1,17},{17,1},{2,18},{18,2},{3,19},{19,3},{4,20},{20... | collective-permute-start | bytes 405512 | tf_op jit(solution)/shard_map/ppermute | solution.py:329
  17.7 5.7 %collective-permute-start.6 = (bf16[16,4224]{1,0:T(8,128)(2,1)S(1)}, bf16[16,4224]{1,0:T(8,128)(2,1)S(1)}, u32[]{:S(2)}, u32[]{:S(2)}) collective-permute-start(bf16[16,4224]{1,0:T(8,128)(2,1)S(1)} %collective-permute-done.1), channel_id=1, source_target_pairs={{0,2},{1,3},{2,0},{3,1},{4,6},{5,7},{6,4},{7,5},{8,10},{9,11},{10,... | collective-permute-start | bytes 405512 | tf_op jit(solution)/shard_map/ppermute | solution.py:326
  18.2 6.5 %collective-permute-start.7 = (bf16[16,4224]{1,0:T(8,128)(2,1)S(1)}, bf16[16,4224]{1,0:T(8,128)(2,1)S(1)}, u32[]{:S(2)}, u32[]{:S(2)}) collective-permute-start(bf16[16,4224]{1,0:T(8,128)(2,1)S(1)} %collective-permute-done.1), channel_id=1, source_target_pairs={{0,18},{1,19},{2,16},{3,17},{4,22},{5,23},{6,20},{7,21},{8,26},{9,... | collective-permute-start | bytes 405512 | tf_op jit(solution)/shard_map/ppermute | solution.py:335
  19.7 8.0 %collective-permute-start.3 = (bf16[32,4224]{1,0:T(8,128)(2,1)S(1)}, bf16[32,4224]{1,0:T(8,128)(2,1)S(1)}, u32[]{:S(2)}, u32[]{:S(2)}) collective-permute-start(bf16[32,4224]{1,0:T(8,128)(2,1)S(1)} %collective-permute-done.2), channel_id=1, source_target_pairs={{0,4},{1,5},{2,6},{3,7},{4,0},{5,1},{6,2},{7,3},{8,12},{9,13},{10,... | collective-permute-start | bytes 811016 | tf_op jit(solution)/shard_map/ppermute | solution.py:326
  21.8 11.1 %collective-permute-start.4 = (bf16[16,4224]{1,0:T(8,128)(2,1)S(1)}, bf16[16,4224]{1,0:T(8,128)(2,1)S(1)}, u32[]{:S(2)}, u32[]{:S(2)}) collective-permute-start(bf16[16,4224]{1,0:T(8,128)(2,1)S(1)} %collective-permute-done.1), channel_id=1, source_target_pairs={{0,4},{1,5},{2,6},{3,7},{4,0},{5,1},{6,2},{7,3},{8,12},{9,13},{10,... | collective-permute-start | bytes 405512 | tf_op jit(solution)/shard_map/ppermute | solution.py:326
  24.8 2.9 %collective-permute-start.10 = (bf16[128,4224]{1,0:T(8,128)(2,1)S(1)}, bf16[128,4224]{1,0:T(8,128)(2,1)S(1)}, u32[]{:S(2)}, u32[]{:S(2)}) collective-permute-start(bf16[128,4224]{1,0:T(8,128)(2,1)S(1)} %constant_dynamic-update-slice_fusion.4.refs_0_), channel_id=1, source_target_pairs={{0,1},{1,0},{2,3},{3,2},{4,5},{5,4},{6,7},{7,6},{8,9},{9,8},{10,11... | collective-permute-start | bytes 3244040 | tf_op jit(solution)/shard_map/ppermute | solution.py:326
  24.9 12.9 %collective-permute-start.8 = (bf16[48,4224]{1,0:T(8,128)(2,1)S(1)}, bf16[48,4224]{1,0:T(8,128)(2,1)S(1)}, u32[]{:S(2)}, u32[]{:S(2)}) collective-permute-start(bf16[48,4224]{1,0:T(8,128)(2,1)S(1)} %pad_maximum_fusion), channel_id=1, source_target_pairs={{0,4},{1,5},{2,6},{3,7},{4,0},{5,1},{6,2},{7,3},{8,12},{9,13},{10,... | collective-permute-start | bytes 1216520 | tf_op jit(solution)/shard_map/ppermute | solution.py:326
  32.8 5.1 %collective-permute-start.11 = (bf16[128,4096]{1,0:T(8,128)(2,1)S(1)}, bf16[128,4096]{1,0:T(8,128)(2,1)S(1)}, u32[]{:S(2)}, u32[]{:S(2)}) collective-permute-start(bf16[128,4096]{1,0:T(8,128)(2,1)S(1)} %get-tuple-element.49), channel_id=1, source_target_pairs={{0,1},{1,0},{2,3},{3,2},{4,5},{5,4},{6,7},{7,6},{8,9},{9,8},{10,11... | collective-permute-start | bytes 3145736 | tf_op jit(solution)/shard_map/ppermute | solution.py:326
  37.8 2.8 %collective-permute-start.9 = (bf16[128,4224]{1,0:T(8,128)(2,1)S(1)}, bf16[128,4224]{1,0:T(8,128)(2,1)S(1)}, u32[]{:S(2)}, u32[]{:S(2)}) collective-permute-start(bf16[128,4224]{1,0:T(8,128)(2,1)S(1)} %constant_dynamic-update-slice_fusion.refs_0_), channel_id=1, source_target_pairs={{0,1},{1,0},{2,3},{3,2},{4,5},{5,4},{6,7},{7,6},{8,9},{9,8},{10,11... | collective-permute-start | bytes 3244040 | tf_op jit(solution)/shard_map/ppermute | solution.py:326
  40.6 8.3 %collective-permute-start.12 = (bf16[32,4096]{1,0:T(8,128)(2,1)S(1)}, bf16[32,4096]{1,0:T(8,128)(2,1)S(1)}, u32[]{:S(2)}, u32[]{:S(2)}) collective-permute-start(bf16[32,4096]{1,0:T(8,128)(2,1)S(1)} %pad_maximum_fusion.1), channel_id=1, source_target_pairs={{0,16},{16,0},{1,17},{17,1},{2,18},{18,2},{3,19},{19,3},{4,20},{20... | collective-permute-start | bytes 786440 | tf_op jit(solution)/shard_map/ppermute | solution.py:329
  42.1 8.1 %collective-permute-start.13 = (bf16[32,4096]{1,0:T(8,128)(2,1)S(1)}, bf16[32,4096]{1,0:T(8,128)(2,1)S(1)}, u32[]{:S(2)}, u32[]{:S(2)}) collective-permute-start(bf16[32,4096]{1,0:T(8,128)(2,1)S(1)} %concatenate.37), channel_id=1, source_target_pairs={{0,2},{1,3},{2,0},{3,1},{4,6},{5,7},{6,4},{7,5},{8,10},{9,11},{10,... | collective-permute-start | bytes 786440 | tf_op jit(solution)/shard_map/ppermute | solution.py:326
  50.2 2.7 %collective-permute-start.14 = (bf16[128,4096]{1,0:T(8,128)(2,1)S(1)}, bf16[128,4096]{1,0:T(8,128)(2,1)S(1)}, u32[]{:S(2)}, u32[]{:S(2)}) collective-permute-start(bf16[128,4096]{1,0:T(8,128)(2,1)S(1)} %get-tuple-element.57), channel_id=1, source_target_pairs={{0,1},{1,0},{2,3},{3,2},{4,5},{5,4},{6,7},{7,6},{8,9},{9,8},{10,11... | collective-permute-start | bytes 3145736 | tf_op jit(solution)/shard_map/ppermute | solution.py:326
  53.2 4.3 %copy-start = (s32[32]{0:T(128)S(1)}, s32[32]{0:T(128)}, u32[]{:S(2)}) copy-start(s32[32]{0:T(128)} %lengths_ref.1) | copy-start | bytes 388
  53.2 11.5 %collective-permute-start.15 = (bf16[32,4096]{1,0:T(8,128)(2,1)S(1)}, bf16[32,4096]{1,0:T(8,128)(2,1)S(1)}, u32[]{:S(2)}, u32[]{:S(2)}) collective-permute-start(bf16[32,4096]{1,0:T(8,128)(2,1)S(1)} %pad_maximum_fusion.2), channel_id=1, source_target_pairs={{0,16},{16,0},{1,17},{17,1},{2,18},{18,2},{3,19},{19,3},{4,20},{20... | collective-permute-start | bytes 786440 | tf_op jit(solution)/shard_map/ppermute | solution.py:329
  53.8 10.9 %collective-permute-start.16 = (bf16[32,4096]{1,0:T(8,128)(2,1)S(1)}, bf16[32,4096]{1,0:T(8,128)(2,1)S(1)}, u32[]{:S(2)}, u32[]{:S(2)}) collective-permute-start(bf16[32,4096]{1,0:T(8,128)(2,1)S(1)} %concatenate.38), channel_id=1, source_target_pairs={{0,2},{1,3},{2,0},{3,1},{4,6},{5,7},{6,4},{7,5},{8,10},{9,11},{10,... | collective-permute-start | bytes 786440 | tf_op jit(solution)/shard_map/ppermute | solution.py:326
  54.4 10.0 %collective-permute-start.17 = (bf16[16,4096]{1,0:T(8,128)(2,1)S(1)}, bf16[16,4096]{1,0:T(8,128)(2,1)S(1)}, u32[]{:S(2)}, u32[]{:S(2)}) collective-permute-start(bf16[16,4096]{1,0:T(8,128)(2,1)S(1)} %get-tuple-element.91), channel_id=1, source_target_pairs={{0,16},{16,0},{1,17},{17,1},{2,18},{18,2},{3,19},{19,3},{4,20},{20... | collective-permute-start | bytes 393224 | tf_op jit(solution)/shard_map/ppermute | solution.py:329
  56.0 8.6 %collective-permute-start.18 = (bf16[16,4096]{1,0:T(8,128)(2,1)S(1)}, bf16[16,4096]{1,0:T(8,128)(2,1)S(1)}, u32[]{:S(2)}, u32[]{:S(2)}) collective-permute-start(bf16[16,4096]{1,0:T(8,128)(2,1)S(1)} %get-tuple-element.84), channel_id=1, source_target_pairs={{0,2},{1,3},{2,0},{3,1},{4,6},{5,7},{6,4},{7,5},{8,10},{9,11},{10,... | collective-permute-start | bytes 393224 | tf_op jit(solution)/shard_map/ppermute | solution.py:326
  64.7 8.3 %collective-permute-start.21 = (bf16[16,4096]{1,0:T(8,128)(2,1)S(1)}, bf16[16,4096]{1,0:T(8,128)(2,1)S(1)}, u32[]{:S(2)}, u32[]{:S(2)}) collective-permute-start(bf16[16,4096]{1,0:T(8,128)(2,1)S(1)} %add_convert_fusion.5), channel_id=1, source_target_pairs={{0,8},{1,9},{2,10},{3,11},{4,12},{5,13},{6,14},{7,15},{8,0},{9,1},... | collective-permute-start | bytes 393224 | tf_op jit(solution)/shard_map/ppermute | solution.py:326
  66.2 6.7 %collective-permute-start.19 = (bf16[16,4096]{1,0:T(8,128)(2,1)S(1)}, bf16[16,4096]{1,0:T(8,128)(2,1)S(1)}, u32[]{:S(2)}, u32[]{:S(2)}) collective-permute-start(bf16[16,4096]{1,0:T(8,128)(2,1)S(1)} %get-tuple-element.89), channel_id=1, source_target_pairs={{0,16},{16,0},{1,17},{17,1},{2,18},{18,2},{3,19},{19,3},{4,20},{20... | collective-permute-start | bytes 393224 | tf_op jit(solution)/shard_map/ppermute | solution.py:329
  67.8 5.1 %collective-permute-start.20 = (bf16[16,4096]{1,0:T(8,128)(2,1)S(1)}, bf16[16,4096]{1,0:T(8,128)(2,1)S(1)}, u32[]{:S(2)}, u32[]{:S(2)}) collective-permute-start(bf16[16,4096]{1,0:T(8,128)(2,1)S(1)} %get-tuple-element.80), channel_id=1, source_target_pairs={{0,2},{1,3},{2,0},{3,1},{4,6},{5,7},{6,4},{7,5},{8,10},{9,11},{10,... | collective-permute-start | bytes 393224 | tf_op jit(solution)/shard_map/ppermute | solution.py:326
  73.0 7.2 %collective-permute-start.22 = (bf16[16,4096]{1,0:T(8,128)(2,1)S(1)}, bf16[16,4096]{1,0:T(8,128)(2,1)S(1)}, u32[]{:S(2)}, u32[]{:S(2)}) collective-permute-start(bf16[16,4096]{1,0:T(8,128)(2,1)S(1)} %add_convert_fusion.4), channel_id=1, source_target_pairs={{0,4},{1,5},{2,6},{3,7},{4,0},{5,1},{6,2},{7,3},{8,12},{9,13},{10,... | collective-permute-start | bytes 393224 | tf_op jit(solution)/shard_map/ppermute | solution.py:326
  73.2 7.7 %collective-permute-start.23 = (bf16[16,4096]{1,0:T(8,128)(2,1)S(1)}, bf16[16,4096]{1,0:T(8,128)(2,1)S(1)}, u32[]{:S(2)}, u32[]{:S(2)}) collective-permute-start(bf16[16,4096]{1,0:T(8,128)(2,1)S(1)} %add_convert_fusion.3), channel_id=1, source_target_pairs={{0,12},{1,13},{2,14},{3,15},{4,8},{5,9},{6,10},{7,11},{8,4},{9,5},... | collective-permute-start | bytes 393224 | tf_op jit(solution)/shard_map/ppermute | solution.py:326
  81.0 5.0 %collective-permute-start.24 = (bf16[16,4096]{1,0:T(8,128)(2,1)S(1)}, bf16[16,4096]{1,0:T(8,128)(2,1)S(1)}, u32[]{:S(2)}, u32[]{:S(2)}) collective-permute-start(bf16[16,4096]{1,0:T(8,128)(2,1)S(1)} %add_convert_fusion.2), channel_id=1, source_target_pairs={{0,16},{16,0},{1,17},{17,1},{2,18},{18,2},{3,19},{19,3},{4,20},{20... | collective-permute-start | bytes 393224 | tf_op jit(solution)/shard_map/ppermute | solution.py:329

commit v5 on v4

--- a/solution.py
+++ b/solution.py
@@ -135,7 +135,7 @@
         out_shape=[jax.ShapeDtypeStruct((row_count, width), held[0].dtype)]
         + [pltpu.VMEM(w.shape, w.dtype) for w in weights],
         scratch_shapes=[pltpu.VMEM((row_count,) + a.shape[1:], a.dtype) for a in held]
-        + [pltpu.VMEM((row_count * heads, HEAD_DIM), jnp.float32)] * 2
+        + [pltpu.VMEM(((row_count + 1) * heads, HEAD_DIM), jnp.float32)] * 2
         + [pltpu.SemaphoreType.DMA((4, max(4, -(-row_count // chunk))))],
         compiler_params=pltpu.CompilerParams(vmem_limit_bytes=10 * 1024 * 1024),
         cost_estimate=pl.CostEstimate(

time: 86.9 us -> 86.9 us (level)
  no operation moved by 1% of the time
where the time goes in v5:
time: 86.9 us; the launch traced here: 86.8 us
  starting transfers between devices  28.9 us (33%)
  waiting for transfers between devices  27.2 us (31%)
  Pallas kernels  26.9 us (31%)
  other arithmetic  2.45 us (3%)
  between operations  0.91 us (1%)
    ppermute x18, starting transfers between devices, over(): lax.ppermute(a, 'dev', [(d, d ^ bit) for d in range(devices)])  19.2 us
    ppermute x18, waiting for transfers between devices, over(): lax.ppermute(a, 'dev', [(d, d ^ bit) for d in range(devices)])  18.5 us
    pallas_call x2, Pallas kernels, expert_rows(): pl.pallas_call(expert_kernel, in_specs=[pl.BlockSpec(memory_space=pltpu.S...  10.3 us
    pallas_call x2, Pallas kernels, attend_and_stage(): pl.pallas_call(functools.partial(attend_kernel, start=start, chunk=chunk,...  8.41 us
    ppermute x6, starting transfers between devices, per_device(): sides = lambda a: lax.ppermute(a, 'side', [(0, 1), (1, 0)])  8.27 us
    ppermute x6, waiting for transfers between devices, per_device(): sides = lambda a: lax.ppermute(a, 'side', [(0, 1), (1, 0)])  7.41 us
    pallas_call x1, Pallas kernels, staged(): pl.pallas_call(stage_kernel, in_specs=[pl.BlockSpec(memory_space=pltpu.HB...  7.02 us
  transfers between devices with their start and end apart: 25, of which 14 were waited for; matrix products, arithmetic and copies ran while one was open for 2% of the time, Pallas kernels for 30%

profile of v5, /device:TPU:0, one launch (start us, length us, event | category | flops | bytes accessed | tf_op | source)
XLA Modules:
  0.0 86.8 jit_solution(4351224547367696873)
XLA Ops:
  0.6 1.2 %norm_and_gates.1 = (bf16[32,4224]{1,0:T(8,128)(2,1)S(1)}, bf16[16,4224]{1,0:T(8,128)(2,1)S(1)}) custom-call(s32[1]{0:T(128)} %bitcast.1.side_ref, bf16[32,4096]{1,0:T(8,128)(2,1)} %refs_0_.2, bf16[4096]{0:T(1024)(128)(2,1)} %refs_1_.2, s32[8,32]{1,0:T(8,128)} %bitcast.4, f32[8,32]{1,0:T(8,128)} %bitcast.5), custom_call_target="tpu_custom_call" | custom-call | tf_op jit(solution)/shard_map/norm_and_gates/pallas_call | solution.py:229
  1.9 3.0 %collective-permute-start.2 = (bf16[32,4224]{1,0:T(8,128)(2,1)S(1)}, bf16[32,4224]{1,0:T(8,128)(2,1)S(1)}, u32[]{:S(2)}, u32[]{:S(2)}) collective-permute-start(bf16[32,4224]{1,0:T(8,128)(2,1)S(1)} %get-tuple-element.41), channel_id=1, source_target_pairs={{0,2},{1,3},{2,0},{3,1},{4,6},{5,7},{6,4},{7,5},{8,10},{9,11},{10,... | collective-permute-start | bytes 811016 | tf_op jit(solution)/shard_map/ppermute | solution.py:326
  4.9 1.6 %collective-permute-start = (bf16[32,4224]{1,0:T(8,128)(2,1)S(1)}, bf16[32,4224]{1,0:T(8,128)(2,1)S(1)}, u32[]{:S(2)}, u32[]{:S(2)}) collective-permute-start(bf16[32,4224]{1,0:T(8,128)(2,1)S(1)} %get-tuple-element.41), channel_id=1, source_target_pairs={{0,4},{1,5},{2,6},{3,7},{4,0},{5,1},{6,2},{7,3},{8,12},{9,13},{10,... | collective-permute-start | bytes 811016 | tf_op jit(solution)/shard_map/ppermute | solution.py:326
  6.5 2.6 %collective-permute-start.1 = (bf16[16,4224]{1,0:T(8,128)(2,1)S(1)}, bf16[16,4224]{1,0:T(8,128)(2,1)S(1)}, u32[]{:S(2)}, u32[]{:S(2)}) collective-permute-start(bf16[16,4224]{1,0:T(8,128)(2,1)S(1)} %get-tuple-element.42), channel_id=1, source_target_pairs={{0,8},{1,9},{2,10},{3,11},{4,12},{5,13},{6,14},{7,15},{8,0},{9,1},... | collective-permute-start | bytes 405512 | tf_op jit(solution)/shard_map/ppermute | solution.py:326
  9.1 7.0 %stage_weights.1 = (bf16[1,4096,768]{2,1,0:T(8,128)(2,1)S(1)}, bf16[1,4096,768]{2,1,0:T(8,128)(2,1)S(1)}, bf16[1,768,4096]{2,1,0:T(8,128)(2,1)S(1)}, f32[8,128]{1,0:T(8,128)}) custom-call(bf16[1,4096,768]{2,1,0:T(8,128)(2,1)} %refs_0_.3, bf16[1,4096,768]{2,1,0:T(8,128)(2,1)} %refs_1_.3, bf16[1,768,4096]{2,1,0:T(8,128)(2,1)} %refs_2_.1), custom_call_target="tpu_custom_call" | custom-call | bytes 37748736 | tf_op jit(solution)/shard_map/stage_weights/pallas_call | solution.py:165
  16.1 1.6 %collective-permute-start.5 = (bf16[16,4224]{1,0:T(8,128)(2,1)S(1)}, bf16[16,4224]{1,0:T(8,128)(2,1)S(1)}, u32[]{:S(2)}, u32[]{:S(2)}) collective-permute-start(bf16[16,4224]{1,0:T(8,128)(2,1)S(1)} %collective-permute-done.1), channel_id=1, source_target_pairs={{0,16},{16,0},{1,17},{17,1},{2,18},{18,2},{3,19},{19,3},{4,20},{20... | collective-permute-start | bytes 405512 | tf_op jit(solution)/shard_map/ppermute | solution.py:329
  17.7 0.5 collective-permute-start.6
  18.2 1.4 %collective-permute-start.7 = (bf16[16,4224]{1,0:T(8,128)(2,1)S(1)}, bf16[16,4224]{1,0:T(8,128)(2,1)S(1)}, u32[]{:S(2)}, u32[]{:S(2)}) collective-permute-start(bf16[16,4224]{1,0:T(8,128)(2,1)S(1)} %collective-permute-done.1), channel_id=1, source_target_pairs={{0,18},{1,19},{2,16},{3,17},{4,22},{5,23},{6,20},{7,21},{8,26},{9,... | collective-permute-start | bytes 405512 | tf_op jit(solution)/shard_map/ppermute | solution.py:335
  19.7 2.1 %collective-permute-start.3 = (bf16[32,4224]{1,0:T(8,128)(2,1)S(1)}, bf16[32,4224]{1,0:T(8,128)(2,1)S(1)}, u32[]{:S(2)}, u32[]{:S(2)}) collective-permute-start(bf16[32,4224]{1,0:T(8,128)(2,1)S(1)} %collective-permute-done.2), channel_id=1, source_target_pairs={{0,4},{1,5},{2,6},{3,7},{4,0},{5,1},{6,2},{7,3},{8,12},{9,13},{10,... | collective-permute-start | bytes 811016 | tf_op jit(solution)/shard_map/ppermute | solution.py:326
  21.8 0.1 collective-permute-start.4
  22.0 0.7 collective-permute-done.5
  22.7 0.7 collective-permute-done.6
  23.4 1.4 %collective-permute-done.7 = bf16[16,4224]{1,0:T(8,128)(2,1)S(1)} collective-permute-done((bf16[16,4224]{1,0:T(8,128)(2,1)S(1)}, bf16[16,4224]{1,0:T(8,128)(2,1)S(1)}, u32[]{:S(2)}, u32[]{:S(2)}) %collective-permute-start.7) | collective-permute-done | bytes 135200 | tf_op jit(solution)/shard_map/ppermute | solution.py:335
  24.9 1.6 %collective-permute-start.8 = (bf16[48,4224]{1,0:T(8,128)(2,1)S(1)}, bf16[48,4224]{1,0:T(8,128)(2,1)S(1)}, u32[]{:S(2)}, u32[]{:S(2)}) collective-permute-start(bf16[48,4224]{1,0:T(8,128)(2,1)S(1)} %pad_maximum_fusion), channel_id=1, source_target_pairs={{0,4},{1,5},{2,6},{3,7},{4,0},{5,1},{6,2},{7,3},{8,12},{9,13},{10,... | collective-permute-start | bytes 1216520 | tf_op jit(solution)/shard_map/ppermute | solution.py:326
  26.5 1.2 %collective-permute-done.3 = bf16[32,4224]{1,0:T(8,128)(2,1)S(1)} collective-permute-done((bf16[32,4224]{1,0:T(8,128)(2,1)S(1)}, bf16[32,4224]{1,0:T(8,128)(2,1)S(1)}, u32[]{:S(2)}, u32[]{:S(2)}) %collective-permute-start.3) | collective-permute-done | bytes 270368 | tf_op jit(solution)/shard_map/ppermute | solution.py:326
  27.7 5.1 %expert_rows.2 = (bf16[128,4096]{1,0:T(8,128)(2,1)S(1)}, bf16[128,4096]{1,0:T(8,128)(2,1)S(1)}) custom-call(s32[1]{0:T(128)} %bitcast.expert_ref, bf16[128,4224]{1,0:T(8,128)(2,1)S(1)} %constant_dynamic-update-slice_fusion.4.refs_0_, bf16[128,4224]{1,0:T(8,128)(2,1)S(1)} %collective-permute-done.10.refs_1_, ...), custom_call_target="tpu_custom_call" | custom-call | flops 4831838208 | bytes 18874368 | tf_op jit(solution)/shard_map/expert_rows/pallas_call | solution.py:274
  32.8 0.1 collective-permute-start.11
  32.9 4.9 %collective-permute-done.8 = bf16[48,4224]{1,0:T(8,128)(2,1)S(1)} collective-permute-done((bf16[48,4224]{1,0:T(8,128)(2,1)S(1)}, bf16[48,4224]{1,0:T(8,128)(2,1)S(1)}, u32[]{:S(2)}, u32[]{:S(2)}) %collective-permute-start.8) | collective-permute-done | bytes 405536 | tf_op jit(solution)/shard_map/ppermute | solution.py:326
  37.9 0.2 add_convert_fusion.1
  38.3 2.3 %collective-permute-done.9.refs_1_ = bf16[128,4224]{1,0:T(8,128)(2,1)S(1)} collective-permute-done((bf16[128,4224]{1,0:T(8,128)(2,1)S(1)}, bf16[128,4224]{1,0:T(8,128)(2,1)S(1)}, u32[]{:S(2)}, u32[]{:S(2)}) %collective-permute-start.9) | collective-permute-done | bytes 1081376 | tf_op jit(solution)/shard_map/ppermute | solution.py:326
  40.6 1.5 %collective-permute-start.12 = (bf16[32,4096]{1,0:T(8,128)(2,1)S(1)}, bf16[32,4096]{1,0:T(8,128)(2,1)S(1)}, u32[]{:S(2)}, u32[]{:S(2)}) collective-permute-start(bf16[32,4096]{1,0:T(8,128)(2,1)S(1)} %pad_maximum_fusion.1), channel_id=1, source_target_pairs={{0,16},{16,0},{1,17},{17,1},{2,18},{18,2},{3,19},{19,3},{4,20},{20... | collective-permute-start | bytes 786440 | tf_op jit(solution)/shard_map/ppermute | solution.py:329
  42.1 0.5 collective-permute-start.13
  42.7 5.1 %expert_rows.3 = (bf16[128,4096]{1,0:T(8,128)(2,1)S(1)}, bf16[128,4096]{1,0:T(8,128)(2,1)S(1)}) custom-call(s32[1]{0:T(128)} %bitcast.expert_ref, bf16[128,4224]{1,0:T(8,128)(2,1)S(1)} %constant_dynamic-update-slice_fusion.refs_0_, bf16[128,4224]{1,0:T(8,128)(2,1)S(1)} %collective-permute-done.9.refs_1_, ...), custom_call_target="tpu_custom_call" | custom-call | flops 4831838208 | bytes 18874368 | tf_op jit(solution)/shard_map/expert_rows/pallas_call | solution.py:274
  47.8 1.1 %collective-permute-done.12 = bf16[32,4096]{1,0:T(8,128)(2,1)S(1)} collective-permute-done((bf16[32,4096]{1,0:T(8,128)(2,1)S(1)}, bf16[32,4096]{1,0:T(8,128)(2,1)S(1)}, u32[]{:S(2)}, u32[]{:S(2)}) %collective-permute-start.12) | collective-permute-done | bytes 262176 | tf_op jit(solution)/shard_map/ppermute | solution.py:329
  48.9 1.2 %collective-permute-done.13 = bf16[32,4096]{1,0:T(8,128)(2,1)S(1)} collective-permute-done((bf16[32,4096]{1,0:T(8,128)(2,1)S(1)}, bf16[32,4096]{1,0:T(8,128)(2,1)S(1)}, u32[]{:S(2)}, u32[]{:S(2)}) %collective-permute-start.13) | collective-permute-done | bytes 262176 | tf_op jit(solution)/shard_map/ppermute | solution.py:326
  50.2 2.7 %collective-permute-done.14 = bf16[128,4096]{1,0:T(8,128)(2,1)S(1)} collective-permute-done((bf16[128,4096]{1,0:T(8,128)(2,1)S(1)}, bf16[128,4096]{1,0:T(8,128)(2,1)S(1)}, u32[]{:S(2)}, u32[]{:S(2)}) %collective-permute-start.14) | collective-permute-done | bytes 1048608 | tf_op jit(solution)/shard_map/ppermute | solution.py:326
  52.9 0.2 add_convert_fusion
  53.2 0.6 collective-permute-start.15
  53.8 0.5 collective-permute-start.16
  54.3 0.1 add_convert_fusion.8
  54.4 1.6 %collective-permute-start.17 = (bf16[16,4096]{1,0:T(8,128)(2,1)S(1)}, bf16[16,4096]{1,0:T(8,128)(2,1)S(1)}, u32[]{:S(2)}, u32[]{:S(2)}) collective-permute-start(bf16[16,4096]{1,0:T(8,128)(2,1)S(1)} %get-tuple-element.91), channel_id=1, source_target_pairs={{0,16},{16,0},{1,17},{17,1},{2,18},{18,2},{3,19},{19,3},{4,20},{20... | collective-permute-start | bytes 393224 | tf_op jit(solution)/shard_map/ppermute | solution.py:329
  56.0 1.5 %collective-permute-start.18 = (bf16[16,4096]{1,0:T(8,128)(2,1)S(1)}, bf16[16,4096]{1,0:T(8,128)(2,1)S(1)}, u32[]{:S(2)}, u32[]{:S(2)}) collective-permute-start(bf16[16,4096]{1,0:T(8,128)(2,1)S(1)} %get-tuple-element.84), channel_id=1, source_target_pairs={{0,2},{1,3},{2,0},{3,1},{4,6},{5,7},{6,4},{7,5},{8,10},{9,11},{10,... | collective-permute-start | bytes 393224 | tf_op jit(solution)/shard_map/ppermute | solution.py:326
  57.5 4.2 %attend_and_stage.2 = bf16[16,4096]{1,0:T(8,128)(2,1)S(1)} custom-call(s32[32]{0:T(128)S(1)} %copy-done, bf16[32,4096]{1,0:T(8,128)(2,1)} %query_src.3, bf16[32,256,256]{2,1,0:T(8,128)(2,1)} %key_src.3, bf16[32,256,256]{2,1,0:T(8,128)(2,1)} %value_src.3, bf16[32,256]{1,0:T(8,128)(2,1)} %new_key_src.3, bf16[32,256]{1,0:T(8,128)(2,1)} %new_value_src.3), custom_call_target="tpu_custom_call" | custom-call | flops 134217728 | bytes 4194304 | tf_op jit(solution)/shard_map/attend_and_stage/pallas_call | solution.py:131
  61.7 2.7 %collective-permute-done.17 = bf16[16,4096]{1,0:T(8,128)(2,1)S(1)} collective-permute-done((bf16[16,4096]{1,0:T(8,128)(2,1)S(1)}, bf16[16,4096]{1,0:T(8,128)(2,1)S(1)}, u32[]{:S(2)}, u32[]{:S(2)}) %collective-permute-start.17) | collective-permute-done | bytes 131104 | tf_op jit(solution)/shard_map/ppermute | solution.py:329
  64.4 0.2 collective-permute-done.18
  64.7 1.4 %collective-permute-start.21 = (bf16[16,4096]{1,0:T(8,128)(2,1)S(1)}, bf16[16,4096]{1,0:T(8,128)(2,1)S(1)}, u32[]{:S(2)}, u32[]{:S(2)}) collective-permute-start(bf16[16,4096]{1,0:T(8,128)(2,1)S(1)} %add_convert_fusion.5), channel_id=1, source_target_pairs={{0,8},{1,9},{2,10},{3,11},{4,12},{5,13},{6,14},{7,15},{8,0},{9,1},... | collective-permute-start | bytes 393224 | tf_op jit(solution)/shard_map/ppermute | solution.py:326
  66.1 0.1 add_convert_fusion.6
  66.2 1.6 %collective-permute-start.19 = (bf16[16,4096]{1,0:T(8,128)(2,1)S(1)}, bf16[16,4096]{1,0:T(8,128)(2,1)S(1)}, u32[]{:S(2)}, u32[]{:S(2)}) collective-permute-start(bf16[16,4096]{1,0:T(8,128)(2,1)S(1)} %get-tuple-element.89), channel_id=1, source_target_pairs={{0,16},{16,0},{1,17},{17,1},{2,18},{18,2},{3,19},{19,3},{4,20},{20... | collective-permute-start | bytes 393224 | tf_op jit(solution)/shard_map/ppermute | solution.py:329
  67.8 0.5 collective-permute-start.20
  68.4 4.6 %collective-permute-done.21 = bf16[16,4096]{1,0:T(8,128)(2,1)S(1)} collective-permute-done((bf16[16,4096]{1,0:T(8,128)(2,1)S(1)}, bf16[16,4096]{1,0:T(8,128)(2,1)S(1)}, u32[]{:S(2)}, u32[]{:S(2)}) %collective-permute-start.21) | collective-permute-done | bytes 131104 | tf_op jit(solution)/shard_map/ppermute | solution.py:326
  73.0 0.2 collective-permute-start.22
  73.2 2.8 %collective-permute-start.23 = (bf16[16,4096]{1,0:T(8,128)(2,1)S(1)}, bf16[16,4096]{1,0:T(8,128)(2,1)S(1)}, u32[]{:S(2)}, u32[]{:S(2)}) collective-permute-start(bf16[16,4096]{1,0:T(8,128)(2,1)S(1)} %add_convert_fusion.3), channel_id=1, source_target_pairs={{0,12},{1,13},{2,14},{3,15},{4,8},{5,9},{6,10},{7,11},{8,4},{9,5},... | collective-permute-start | bytes 393224 | tf_op jit(solution)/shard_map/ppermute | solution.py:326
  76.0 4.2 %attend_and_stage.3 = bf16[16,4096]{1,0:T(8,128)(2,1)S(1)} custom-call(s32[32]{0:T(128)S(1)} %copy-done, bf16[32,4096]{1,0:T(8,128)(2,1)} %query_src.3, bf16[32,256,256]{2,1,0:T(8,128)(2,1)} %key_src.3, bf16[32,256,256]{2,1,0:T(8,128)(2,1)} %value_src.3, bf16[32,256]{1,0:T(8,128)(2,1)} %new_key_src.3, bf16[32,256]{1,0:T(8,128)(2,1)} %new_value_src.3), custom_call_target="tpu_custom_call" | custom-call | flops 134217728 | bytes 4194304 | tf_op jit(solution)/shard_map/attend_and_stage/pallas_call | solution.py:131
  80.2 0.7 collective-permute-done.23
  81.0 1.4 %collective-permute-start.24 = (bf16[16,4096]{1,0:T(8,128)(2,1)S(1)}, bf16[16,4096]{1,0:T(8,128)(2,1)S(1)}, u32[]{:S(2)}, u32[]{:S(2)}) collective-permute-start(bf16[16,4096]{1,0:T(8,128)(2,1)S(1)} %add_convert_fusion.2), channel_id=1, source_target_pairs={{0,16},{16,0},{1,17},{17,1},{2,18},{18,2},{3,19},{19,3},{4,20},{20... | collective-permute-start | bytes 393224 | tf_op jit(solution)/shard_map/ppermute | solution.py:329
  82.4 0.7 pad_maximum_fusion.3
  83.1 2.9 %collective-permute-done.24 = bf16[16,4096]{1,0:T(8,128)(2,1)S(1)} collective-permute-done((bf16[16,4096]{1,0:T(8,128)(2,1)S(1)}, bf16[16,4096]{1,0:T(8,128)(2,1)S(1)}, u32[]{:S(2)}, u32[]{:S(2)}) %collective-permute-start.24) | collective-permute-done | bytes 131104 | tf_op jit(solution)/shard_map/ppermute | solution.py:329
  86.0 0.7 pad_maximum_fusion.4
  (39 shorter events, 0.7 us)
Async XLA Ops:
  1.9 14.2 %collective-permute-start.2 = (bf16[32,4224]{1,0:T(8,128)(2,1)S(1)}, bf16[32,4224]{1,0:T(8,128)(2,1)S(1)}, u32[]{:S(2)}, u32[]{:S(2)}) collective-permute-start(bf16[32,4224]{1,0:T(8,128)(2,1)S(1)} %get-tuple-element.41), channel_id=1, source_target_pairs={{0,2},{1,3},{2,0},{3,1},{4,6},{5,7},{6,4},{7,5},{8,10},{9,11},{10,... | collective-permute-start | bytes 811016 | tf_op jit(solution)/shard_map/ppermute | solution.py:326
  4.9 16.9 %collective-permute-start = (bf16[32,4224]{1,0:T(8,128)(2,1)S(1)}, bf16[32,4224]{1,0:T(8,128)(2,1)S(1)}, u32[]{:S(2)}, u32[]{:S(2)}) collective-permute-start(bf16[32,4224]{1,0:T(8,128)(2,1)S(1)} %get-tuple-element.41), channel_id=1, source_target_pairs={{0,4},{1,5},{2,6},{3,7},{4,0},{5,1},{6,2},{7,3},{8,12},{9,13},{10,... | collective-permute-start | bytes 811016 | tf_op jit(solution)/shard_map/ppermute | solution.py:326
  6.5 9.6 %collective-permute-start.1 = (bf16[16,4224]{1,0:T(8,128)(2,1)S(1)}, bf16[16,4224]{1,0:T(8,128)(2,1)S(1)}, u32[]{:S(2)}, u32[]{:S(2)}) collective-permute-start(bf16[16,4224]{1,0:T(8,128)(2,1)S(1)} %get-tuple-element.42), channel_id=1, source_target_pairs={{0,8},{1,9},{2,10},{3,11},{4,12},{5,13},{6,14},{7,15},{8,0},{9,1},... | collective-permute-start | bytes 405512 | tf_op jit(solution)/shard_map/ppermute | solution.py:326
  16.1 6.5 %collective-permute-start.5 = (bf16[16,4224]{1,0:T(8,128)(2,1)S(1)}, bf16[16,4224]{1,0:T(8,128)(2,1)S(1)}, u32[]{:S(2)}, u32[]{:S(2)}) collective-permute-start(bf16[16,4224]{1,0:T(8,128)(2,1)S(1)} %collective-permute-done.1), channel_id=1, source_target_pairs={{0,16},{16,0},{1,17},{17,1},{2,18},{18,2},{3,19},{19,3},{4,20},{20... | collective-permute-start | bytes 405512 | tf_op jit(solution)/shard_map/ppermute | solution.py:329
  17.7 5.7 %collective-permute-start.6 = (bf16[16,4224]{1,0:T(8,128)(2,1)S(1)}, bf16[16,4224]{1,0:T(8,128)(2,1)S(1)}, u32[]{:S(2)}, u32[]{:S(2)}) collective-permute-start(bf16[16,4224]{1,0:T(8,128)(2,1)S(1)} %collective-permute-done.1), channel_id=1, source_target_pairs={{0,2},{1,3},{2,0},{3,1},{4,6},{5,7},{6,4},{7,5},{8,10},{9,11},{10,... | collective-permute-start | bytes 405512 | tf_op jit(solution)/shard_map/ppermute | solution.py:326
  18.2 6.5 %collective-permute-start.7 = (bf16[16,4224]{1,0:T(8,128)(2,1)S(1)}, bf16[16,4224]{1,0:T(8,128)(2,1)S(1)}, u32[]{:S(2)}, u32[]{:S(2)}) collective-permute-start(bf16[16,4224]{1,0:T(8,128)(2,1)S(1)} %collective-permute-done.1), channel_id=1, source_target_pairs={{0,18},{1,19},{2,16},{3,17},{4,22},{5,23},{6,20},{7,21},{8,26},{9,... | collective-permute-start | bytes 405512 | tf_op jit(solution)/shard_map/ppermute | solution.py:335
  19.7 8.0 %collective-permute-start.3 = (bf16[32,4224]{1,0:T(8,128)(2,1)S(1)}, bf16[32,4224]{1,0:T(8,128)(2,1)S(1)}, u32[]{:S(2)}, u32[]{:S(2)}) collective-permute-start(bf16[32,4224]{1,0:T(8,128)(2,1)S(1)} %collective-permute-done.2), channel_id=1, source_target_pairs={{0,4},{1,5},{2,6},{3,7},{4,0},{5,1},{6,2},{7,3},{8,12},{9,13},{10,... | collective-permute-start | bytes 811016 | tf_op jit(solution)/shard_map/ppermute | solution.py:326
  21.8 11.1 %collective-permute-start.4 = (bf16[16,4224]{1,0:T(8,128)(2,1)S(1)}, bf16[16,4224]{1,0:T(8,128)(2,1)S(1)}, u32[]{:S(2)}, u32[]{:S(2)}) collective-permute-start(bf16[16,4224]{1,0:T(8,128)(2,1)S(1)} %collective-permute-done.1), channel_id=1, source_target_pairs={{0,4},{1,5},{2,6},{3,7},{4,0},{5,1},{6,2},{7,3},{8,12},{9,13},{10,... | collective-permute-start | bytes 405512 | tf_op jit(solution)/shard_map/ppermute | solution.py:326
  24.8 2.9 %collective-permute-start.10 = (bf16[128,4224]{1,0:T(8,128)(2,1)S(1)}, bf16[128,4224]{1,0:T(8,128)(2,1)S(1)}, u32[]{:S(2)}, u32[]{:S(2)}) collective-permute-start(bf16[128,4224]{1,0:T(8,128)(2,1)S(1)} %constant_dynamic-update-slice_fusion.4.refs_0_), channel_id=1, source_target_pairs={{0,1},{1,0},{2,3},{3,2},{4,5},{5,4},{6,7},{7,6},{8,9},{9,8},{10,11... | collective-permute-start | bytes 3244040 | tf_op jit(solution)/shard_map/ppermute | solution.py:326
  24.9 12.9 %collective-permute-start.8 = (bf16[48,4224]{1,0:T(8,128)(2,1)S(1)}, bf16[48,4224]{1,0:T(8,128)(2,1)S(1)}, u32[]{:S(2)}, u32[]{:S(2)}) collective-permute-start(bf16[48,4224]{1,0:T(8,128)(2,1)S(1)} %pad_maximum_fusion), channel_id=1, source_target_pairs={{0,4},{1,5},{2,6},{3,7},{4,0},{5,1},{6,2},{7,3},{8,12},{9,13},{10,... | collective-permute-start | bytes 1216520 | tf_op jit(solution)/shard_map/ppermute | solution.py:326
  32.8 5.1 %collective-permute-start.11 = (bf16[128,4096]{1,0:T(8,128)(2,1)S(1)}, bf16[128,4096]{1,0:T(8,128)(2,1)S(1)}, u32[]{:S(2)}, u32[]{:S(2)}) collective-permute-start(bf16[128,4096]{1,0:T(8,128)(2,1)S(1)} %get-tuple-element.49), channel_id=1, source_target_pairs={{0,1},{1,0},{2,3},{3,2},{4,5},{5,4},{6,7},{7,6},{8,9},{9,8},{10,11... | collective-permute-start | bytes 3145736 | tf_op jit(solution)/shard_map/ppermute | solution.py:326
  37.8 2.8 %collective-permute-start.9 = (bf16[128,4224]{1,0:T(8,128)(2,1)S(1)}, bf16[128,4224]{1,0:T(8,128)(2,1)S(1)}, u32[]{:S(2)}, u32[]{:S(2)}) collective-permute-start(bf16[128,4224]{1,0:T(8,128)(2,1)S(1)} %constant_dynamic-update-slice_fusion.refs_0_), channel_id=1, source_target_pairs={{0,1},{1,0},{2,3},{3,2},{4,5},{5,4},{6,7},{7,6},{8,9},{9,8},{10,11... | collective-permute-start | bytes 3244040 | tf_op jit(solution)/shard_map/ppermute | solution.py:326
  40.6 8.3 %collective-permute-start.12 = (bf16[32,4096]{1,0:T(8,128)(2,1)S(1)}, bf16[32,4096]{1,0:T(8,128)(2,1)S(1)}, u32[]{:S(2)}, u32[]{:S(2)}) collective-permute-start(bf16[32,4096]{1,0:T(8,128)(2,1)S(1)} %pad_maximum_fusion.1), channel_id=1, source_target_pairs={{0,16},{16,0},{1,17},{17,1},{2,18},{18,2},{3,19},{19,3},{4,20},{20... | collective-permute-start | bytes 786440 | tf_op jit(solution)/shard_map/ppermute | solution.py:329
  42.1 8.1 %collective-permute-start.13 = (bf16[32,4096]{1,0:T(8,128)(2,1)S(1)}, bf16[32,4096]{1,0:T(8,128)(2,1)S(1)}, u32[]{:S(2)}, u32[]{:S(2)}) collective-permute-start(bf16[32,4096]{1,0:T(8,128)(2,1)S(1)} %concatenate.37), channel_id=1, source_target_pairs={{0,2},{1,3},{2,0},{3,1},{4,6},{5,7},{6,4},{7,5},{8,10},{9,11},{10,... | collective-permute-start | bytes 786440 | tf_op jit(solution)/shard_map/ppermute | solution.py:326
  50.2 2.7 %collective-permute-start.14 = (bf16[128,4096]{1,0:T(8,128)(2,1)S(1)}, bf16[128,4096]{1,0:T(8,128)(2,1)S(1)}, u32[]{:S(2)}, u32[]{:S(2)}) collective-permute-start(bf16[128,4096]{1,0:T(8,128)(2,1)S(1)} %get-tuple-element.57), channel_id=1, source_target_pairs={{0,1},{1,0},{2,3},{3,2},{4,5},{5,4},{6,7},{7,6},{8,9},{9,8},{10,11... | collective-permute-start | bytes 3145736 | tf_op jit(solution)/shard_map/ppermute | solution.py:326
  53.2 4.3 %copy-start = (s32[32]{0:T(128)S(1)}, s32[32]{0:T(128)}, u32[]{:S(2)}) copy-start(s32[32]{0:T(128)} %lengths_ref.1) | copy-start | bytes 388
  53.2 11.5 %collective-permute-start.15 = (bf16[32,4096]{1,0:T(8,128)(2,1)S(1)}, bf16[32,4096]{1,0:T(8,128)(2,1)S(1)}, u32[]{:S(2)}, u32[]{:S(2)}) collective-permute-start(bf16[32,4096]{1,0:T(8,128)(2,1)S(1)} %pad_maximum_fusion.2), channel_id=1, source_target_pairs={{0,16},{16,0},{1,17},{17,1},{2,18},{18,2},{3,19},{19,3},{4,20},{20... | collective-permute-start | bytes 786440 | tf_op jit(solution)/shard_map/ppermute | solution.py:329
  53.8 10.9 %collective-permute-start.16 = (bf16[32,4096]{1,0:T(8,128)(2,1)S(1)}, bf16[32,4096]{1,0:T(8,128)(2,1)S(1)}, u32[]{:S(2)}, u32[]{:S(2)}) collective-permute-start(bf16[32,4096]{1,0:T(8,128)(2,1)S(1)} %concatenate.38), channel_id=1, source_target_pairs={{0,2},{1,3},{2,0},{3,1},{4,6},{5,7},{6,4},{7,5},{8,10},{9,11},{10,... | collective-permute-start | bytes 786440 | tf_op jit(solution)/shard_map/ppermute | solution.py:326
  54.4 10.0 %collective-permute-start.17 = (bf16[16,4096]{1,0:T(8,128)(2,1)S(1)}, bf16[16,4096]{1,0:T(8,128)(2,1)S(1)}, u32[]{:S(2)}, u32[]{:S(2)}) collective-permute-start(bf16[16,4096]{1,0:T(8,128)(2,1)S(1)} %get-tuple-element.91), channel_id=1, source_target_pairs={{0,16},{16,0},{1,17},{17,1},{2,18},{18,2},{3,19},{19,3},{4,20},{20... | collective-permute-start | bytes 393224 | tf_op jit(solution)/shard_map/ppermute | solution.py:329
  56.0 8.6 %collective-permute-start.18 = (bf16[16,4096]{1,0:T(8,128)(2,1)S(1)}, bf16[16,4096]{1,0:T(8,128)(2,1)S(1)}, u32[]{:S(2)}, u32[]{:S(2)}) collective-permute-start(bf16[16,4096]{1,0:T(8,128)(2,1)S(1)} %get-tuple-element.84), channel_id=1, source_target_pairs={{0,2},{1,3},{2,0},{3,1},{4,6},{5,7},{6,4},{7,5},{8,10},{9,11},{10,... | collective-permute-start | bytes 393224 | tf_op jit(solution)/shard_map/ppermute | solution.py:326
  64.7 8.3 %collective-permute-start.21 = (bf16[16,4096]{1,0:T(8,128)(2,1)S(1)}, bf16[16,4096]{1,0:T(8,128)(2,1)S(1)}, u32[]{:S(2)}, u32[]{:S(2)}) collective-permute-start(bf16[16,4096]{1,0:T(8,128)(2,1)S(1)} %add_convert_fusion.5), channel_id=1, source_target_pairs={{0,8},{1,9},{2,10},{3,11},{4,12},{5,13},{6,14},{7,15},{8,0},{9,1},... | collective-permute-start | bytes 393224 | tf_op jit(solution)/shard_map/ppermute | solution.py:326
  66.2 6.7 %collective-permute-start.19 = (bf16[16,4096]{1,0:T(8,128)(2,1)S(1)}, bf16[16,4096]{1,0:T(8,128)(2,1)S(1)}, u32[]{:S(2)}, u32[]{:S(2)}) collective-permute-start(bf16[16,4096]{1,0:T(8,128)(2,1)S(1)} %get-tuple-element.89), channel_id=1, source_target_pairs={{0,16},{16,0},{1,17},{17,1},{2,18},{18,2},{3,19},{19,3},{4,20},{20... | collective-permute-start | bytes 393224 | tf_op jit(solution)/shard_map/ppermute | solution.py:329
  67.8 5.1 %collective-permute-start.20 = (bf16[16,4096]{1,0:T(8,128)(2,1)S(1)}, bf16[16,4096]{1,0:T(8,128)(2,1)S(1)}, u32[]{:S(2)}, u32[]{:S(2)}) collective-permute-start(bf16[16,4096]{1,0:T(8,128)(2,1)S(1)} %get-tuple-element.80), channel_id=1, source_target_pairs={{0,2},{1,3},{2,0},{3,1},{4,6},{5,7},{6,4},{7,5},{8,10},{9,11},{10,... | collective-permute-start | bytes 393224 | tf_op jit(solution)/shard_map/ppermute | solution.py:326
  73.0 7.2 %collective-permute-start.22 = (bf16[16,4096]{1,0:T(8,128)(2,1)S(1)}, bf16[16,4096]{1,0:T(8,128)(2,1)S(1)}, u32[]{:S(2)}, u32[]{:S(2)}) collective-permute-start(bf16[16,4096]{1,0:T(8,128)(2,1)S(1)} %add_convert_fusion.4), channel_id=1, source_target_pairs={{0,4},{1,5},{2,6},{3,7},{4,0},{5,1},{6,2},{7,3},{8,12},{9,13},{10,... | collective-permute-start | bytes 393224 | tf_op jit(solution)/shard_map/ppermute | solution.py:326
  73.2 7.7 %collective-permute-start.23 = (bf16[16,4096]{1,0:T(8,128)(2,1)S(1)}, bf16[16,4096]{1,0:T(8,128)(2,1)S(1)}, u32[]{:S(2)}, u32[]{:S(2)}) collective-permute-start(bf16[16,4096]{1,0:T(8,128)(2,1)S(1)} %add_convert_fusion.3), channel_id=1, source_target_pairs={{0,12},{1,13},{2,14},{3,15},{4,8},{5,9},{6,10},{7,11},{8,4},{9,5},... | collective-permute-start | bytes 393224 | tf_op jit(solution)/shard_map/ppermute | solution.py:326
  81.0 5.0 %collective-permute-start.24 = (bf16[16,4096]{1,0:T(8,128)(2,1)S(1)}, bf16[16,4096]{1,0:T(8,128)(2,1)S(1)}, u32[]{:S(2)}, u32[]{:S(2)}) collective-permute-start(bf16[16,4096]{1,0:T(8,128)(2,1)S(1)} %add_convert_fusion.2), channel_id=1, source_target_pairs={{0,16},{16,0},{1,17},{17,1},{2,18},{18,2},{3,19},{19,3},{4,20},{20... | collective-permute-start | bytes 393224 | tf_op jit(solution)/shard_map/ppermute | solution.py:329

commit v6 on v5

--- a/solution.py
+++ b/solution.py
@@ -418,10 +418,10 @@
     context = jnp.concatenate([first_context, second_context], axis=0)
     total = add_rounded(*(reduced[i] for i in range(planes)))
     partner = sides(total)
-    first = lax.axis_index("side") == 0
-    moe_out = jnp.concatenate(
-        [jnp.where(first, total, partner), jnp.where(first, partner, total)], axis=0
-    )
+    low = lax.axis_index("side") * half
+    moe_out = jnp.zeros((2 * half, total.shape[1]), total.dtype)
+    moe_out = lax.dynamic_update_slice(moe_out, total, (low, 0))
+    moe_out = lax.dynamic_update_slice(moe_out, partner, (half - low, 0))
     return (context, moe_out)
 
 

time: 86.9 us -> 86.9 us (level)
  no operation moved by 1% of the time
where the time goes in v6:
time: 86.9 us; the launch traced here: 86.8 us
  starting transfers between devices  28.9 us (33%)
  waiting for transfers between devices  27.2 us (31%)
  Pallas kernels  26.9 us (31%)
  other arithmetic  1.71 us (2%)
  local copies, waits for them, and re-layouts  1.02 us (1%)
  between operations  0.93 us (1%)
    ppermute x18, starting transfers between devices, over(): lax.ppermute(a, 'dev', [(d, d ^ bit) for d in range(devices)])  19.2 us
    ppermute x18, waiting for transfers between devices, over(): lax.ppermute(a, 'dev', [(d, d ^ bit) for d in range(devices)])  18.5 us
    pallas_call x2, Pallas kernels, expert_rows(): pl.pallas_call(expert_kernel, in_specs=[pl.BlockSpec(memory_space=pltpu.S...  10.3 us
    pallas_call x2, Pallas kernels, attend_and_stage(): pl.pallas_call(functools.partial(attend_kernel, start=start, chunk=chunk,...  8.41 us
    ppermute x6, starting transfers between devices, per_device(): sides = lambda a: lax.ppermute(a, 'side', [(0, 1), (1, 0)])  8.27 us
    ppermute x6, waiting for transfers between devices, per_device(): sides = lambda a: lax.ppermute(a, 'side', [(0, 1), (1, 0)])  7.41 us
    pallas_call x1, Pallas kernels, staged(): pl.pallas_call(stage_kernel, in_specs=[pl.BlockSpec(memory_space=pltpu.HB...  7.02 us
  transfers between devices with their start and end apart: 25, of which 14 were waited for; matrix products, arithmetic and copies ran while one was open for 2% of the time, Pallas kernels for 30%

profile of v6, /device:TPU:0, one launch (start us, length us, event | category | flops | bytes accessed | tf_op | source)
XLA Modules:
  0.0 86.8 jit_solution(1965132726076143327)
XLA Ops:
  0.6 1.2 %norm_and_gates.1 = (bf16[32,4224]{1,0:T(8,128)(2,1)S(1)}, bf16[16,4224]{1,0:T(8,128)(2,1)S(1)}) custom-call(s32[1]{0:T(128)} %bitcast.1.side_ref, bf16[32,4096]{1,0:T(8,128)(2,1)} %refs_0_.2, bf16[4096]{0:T(1024)(128)(2,1)} %refs_1_.2, s32[8,32]{1,0:T(8,128)} %bitcast.4, f32[8,32]{1,0:T(8,128)} %bitcast.5), custom_call_target="tpu_custom_call" | custom-call | tf_op jit(solution)/shard_map/norm_and_gates/pallas_call | solution.py:229
  1.9 3.0 %collective-permute-start.2 = (bf16[32,4224]{1,0:T(8,128)(2,1)S(1)}, bf16[32,4224]{1,0:T(8,128)(2,1)S(1)}, u32[]{:S(2)}, u32[]{:S(2)}) collective-permute-start(bf16[32,4224]{1,0:T(8,128)(2,1)S(1)} %get-tuple-element.41), channel_id=1, source_target_pairs={{0,2},{1,3},{2,0},{3,1},{4,6},{5,7},{6,4},{7,5},{8,10},{9,11},{10,... | collective-permute-start | bytes 811016 | tf_op jit(solution)/shard_map/ppermute | solution.py:326
  4.9 1.6 %collective-permute-start = (bf16[32,4224]{1,0:T(8,128)(2,1)S(1)}, bf16[32,4224]{1,0:T(8,128)(2,1)S(1)}, u32[]{:S(2)}, u32[]{:S(2)}) collective-permute-start(bf16[32,4224]{1,0:T(8,128)(2,1)S(1)} %get-tuple-element.41), channel_id=1, source_target_pairs={{0,4},{1,5},{2,6},{3,7},{4,0},{5,1},{6,2},{7,3},{8,12},{9,13},{10,... | collective-permute-start | bytes 811016 | tf_op jit(solution)/shard_map/ppermute | solution.py:326
  6.5 2.6 %collective-permute-start.1 = (bf16[16,4224]{1,0:T(8,128)(2,1)S(1)}, bf16[16,4224]{1,0:T(8,128)(2,1)S(1)}, u32[]{:S(2)}, u32[]{:S(2)}) collective-permute-start(bf16[16,4224]{1,0:T(8,128)(2,1)S(1)} %get-tuple-element.42), channel_id=1, source_target_pairs={{0,8},{1,9},{2,10},{3,11},{4,12},{5,13},{6,14},{7,15},{8,0},{9,1},... | collective-permute-start | bytes 405512 | tf_op jit(solution)/shard_map/ppermute | solution.py:326
  9.1 7.0 %stage_weights.1 = (bf16[1,4096,768]{2,1,0:T(8,128)(2,1)S(1)}, bf16[1,4096,768]{2,1,0:T(8,128)(2,1)S(1)}, bf16[1,768,4096]{2,1,0:T(8,128)(2,1)S(1)}, f32[8,128]{1,0:T(8,128)}) custom-call(bf16[1,4096,768]{2,1,0:T(8,128)(2,1)} %refs_0_.3, bf16[1,4096,768]{2,1,0:T(8,128)(2,1)} %refs_1_.3, bf16[1,768,4096]{2,1,0:T(8,128)(2,1)} %refs_2_.1), custom_call_target="tpu_custom_call" | custom-call | bytes 37748736 | tf_op jit(solution)/shard_map/stage_weights/pallas_call | solution.py:165
  16.1 1.6 %collective-permute-start.5 = (bf16[16,4224]{1,0:T(8,128)(2,1)S(1)}, bf16[16,4224]{1,0:T(8,128)(2,1)S(1)}, u32[]{:S(2)}, u32[]{:S(2)}) collective-permute-start(bf16[16,4224]{1,0:T(8,128)(2,1)S(1)} %collective-permute-done.1), channel_id=1, source_target_pairs={{0,16},{16,0},{1,17},{17,1},{2,18},{18,2},{3,19},{19,3},{4,20},{20... | collective-permute-start | bytes 405512 | tf_op jit(solution)/shard_map/ppermute | solution.py:329
  17.7 0.5 collective-permute-start.6
  18.2 1.4 %collective-permute-start.7 = (bf16[16,4224]{1,0:T(8,128)(2,1)S(1)}, bf16[16,4224]{1,0:T(8,128)(2,1)S(1)}, u32[]{:S(2)}, u32[]{:S(2)}) collective-permute-start(bf16[16,4224]{1,0:T(8,128)(2,1)S(1)} %collective-permute-done.1), channel_id=1, source_target_pairs={{0,18},{1,19},{2,16},{3,17},{4,22},{5,23},{6,20},{7,21},{8,26},{9,... | collective-permute-start | bytes 405512 | tf_op jit(solution)/shard_map/ppermute | solution.py:335
  19.7 2.1 %collective-permute-start.3 = (bf16[32,4224]{1,0:T(8,128)(2,1)S(1)}, bf16[32,4224]{1,0:T(8,128)(2,1)S(1)}, u32[]{:S(2)}, u32[]{:S(2)}) collective-permute-start(bf16[32,4224]{1,0:T(8,128)(2,1)S(1)} %collective-permute-done.2), channel_id=1, source_target_pairs={{0,4},{1,5},{2,6},{3,7},{4,0},{5,1},{6,2},{7,3},{8,12},{9,13},{10,... | collective-permute-start | bytes 811016 | tf_op jit(solution)/shard_map/ppermute | solution.py:326
  21.8 0.1 collective-permute-start.4
  22.0 0.7 collective-permute-done.5
  22.7 0.7 collective-permute-done.6
  23.4 1.4 %collective-permute-done.7 = bf16[16,4224]{1,0:T(8,128)(2,1)S(1)} collective-permute-done((bf16[16,4224]{1,0:T(8,128)(2,1)S(1)}, bf16[16,4224]{1,0:T(8,128)(2,1)S(1)}, u32[]{:S(2)}, u32[]{:S(2)}) %collective-permute-start.7) | collective-permute-done | bytes 135200 | tf_op jit(solution)/shard_map/ppermute | solution.py:335
  24.9 1.6 %collective-permute-start.8 = (bf16[48,4224]{1,0:T(8,128)(2,1)S(1)}, bf16[48,4224]{1,0:T(8,128)(2,1)S(1)}, u32[]{:S(2)}, u32[]{:S(2)}) collective-permute-start(bf16[48,4224]{1,0:T(8,128)(2,1)S(1)} %pad_maximum_fusion), channel_id=1, source_target_pairs={{0,4},{1,5},{2,6},{3,7},{4,0},{5,1},{6,2},{7,3},{8,12},{9,13},{10,... | collective-permute-start | bytes 1216520 | tf_op jit(solution)/shard_map/ppermute | solution.py:326
  26.5 1.2 %collective-permute-done.3 = bf16[32,4224]{1,0:T(8,128)(2,1)S(1)} collective-permute-done((bf16[32,4224]{1,0:T(8,128)(2,1)S(1)}, bf16[32,4224]{1,0:T(8,128)(2,1)S(1)}, u32[]{:S(2)}, u32[]{:S(2)}) %collective-permute-start.3) | collective-permute-done | bytes 270368 | tf_op jit(solution)/shard_map/ppermute | solution.py:326
  27.7 5.1 %expert_rows.2 = (bf16[128,4096]{1,0:T(8,128)(2,1)S(1)}, bf16[128,4096]{1,0:T(8,128)(2,1)S(1)}) custom-call(s32[1]{0:T(128)} %bitcast.expert_ref, bf16[128,4224]{1,0:T(8,128)(2,1)S(1)} %constant_dynamic-update-slice_fusion.4.refs_0_, bf16[128,4224]{1,0:T(8,128)(2,1)S(1)} %collective-permute-done.10.refs_1_, ...), custom_call_target="tpu_custom_call" | custom-call | flops 4831838208 | bytes 18874368 | tf_op jit(solution)/shard_map/expert_rows/pallas_call | solution.py:274
  32.8 0.1 collective-permute-start.11
  32.9 4.9 %collective-permute-done.8 = bf16[48,4224]{1,0:T(8,128)(2,1)S(1)} collective-permute-done((bf16[48,4224]{1,0:T(8,128)(2,1)S(1)}, bf16[48,4224]{1,0:T(8,128)(2,1)S(1)}, u32[]{:S(2)}, u32[]{:S(2)}) %collective-permute-start.8) | collective-permute-done | bytes 405536 | tf_op jit(solution)/shard_map/ppermute | solution.py:326
  37.9 0.2 add_convert_fusion.1
  38.3 2.3 %collective-permute-done.9.refs_1_ = bf16[128,4224]{1,0:T(8,128)(2,1)S(1)} collective-permute-done((bf16[128,4224]{1,0:T(8,128)(2,1)S(1)}, bf16[128,4224]{1,0:T(8,128)(2,1)S(1)}, u32[]{:S(2)}, u32[]{:S(2)}) %collective-permute-start.9) | collective-permute-done | bytes 1081376 | tf_op jit(solution)/shard_map/ppermute | solution.py:326
  40.6 1.5 %collective-permute-start.12 = (bf16[32,4096]{1,0:T(8,128)(2,1)S(1)}, bf16[32,4096]{1,0:T(8,128)(2,1)S(1)}, u32[]{:S(2)}, u32[]{:S(2)}) collective-permute-start(bf16[32,4096]{1,0:T(8,128)(2,1)S(1)} %pad_maximum_fusion.1), channel_id=1, source_target_pairs={{0,16},{16,0},{1,17},{17,1},{2,18},{18,2},{3,19},{19,3},{4,20},{20... | collective-permute-start | bytes 786440 | tf_op jit(solution)/shard_map/ppermute | solution.py:329
  42.1 0.5 collective-permute-start.13
  42.7 5.1 %expert_rows.3 = (bf16[128,4096]{1,0:T(8,128)(2,1)S(1)}, bf16[128,4096]{1,0:T(8,128)(2,1)S(1)}) custom-call(s32[1]{0:T(128)} %bitcast.expert_ref, bf16[128,4224]{1,0:T(8,128)(2,1)S(1)} %constant_dynamic-update-slice_fusion.refs_0_, bf16[128,4224]{1,0:T(8,128)(2,1)S(1)} %collective-permute-done.9.refs_1_, ...), custom_call_target="tpu_custom_call" | custom-call | flops 4831838208 | bytes 18874368 | tf_op jit(solution)/shard_map/expert_rows/pallas_call | solution.py:274
  47.8 1.1 %collective-permute-done.12 = bf16[32,4096]{1,0:T(8,128)(2,1)S(1)} collective-permute-done((bf16[32,4096]{1,0:T(8,128)(2,1)S(1)}, bf16[32,4096]{1,0:T(8,128)(2,1)S(1)}, u32[]{:S(2)}, u32[]{:S(2)}) %collective-permute-start.12) | collective-permute-done | bytes 262176 | tf_op jit(solution)/shard_map/ppermute | solution.py:329
  48.9 1.2 %collective-permute-done.13 = bf16[32,4096]{1,0:T(8,128)(2,1)S(1)} collective-permute-done((bf16[32,4096]{1,0:T(8,128)(2,1)S(1)}, bf16[32,4096]{1,0:T(8,128)(2,1)S(1)}, u32[]{:S(2)}, u32[]{:S(2)}) %collective-permute-start.13) | collective-permute-done | bytes 262176 | tf_op jit(solution)/shard_map/ppermute | solution.py:326
  50.2 2.7 %collective-permute-done.14 = bf16[128,4096]{1,0:T(8,128)(2,1)S(1)} collective-permute-done((bf16[128,4096]{1,0:T(8,128)(2,1)S(1)}, bf16[128,4096]{1,0:T(8,128)(2,1)S(1)}, u32[]{:S(2)}, u32[]{:S(2)}) %collective-permute-start.14) | collective-permute-done | bytes 1048608 | tf_op jit(solution)/shard_map/ppermute | solution.py:326
  52.9 0.2 add_convert_fusion
  53.2 0.6 collective-permute-start.15
  53.8 0.5 collective-permute-start.16
  54.3 0.1 add_convert_fusion.8
  54.4 1.6 %collective-permute-start.17 = (bf16[16,4096]{1,0:T(8,128)(2,1)S(1)}, bf16[16,4096]{1,0:T(8,128)(2,1)S(1)}, u32[]{:S(2)}, u32[]{:S(2)}) collective-permute-start(bf16[16,4096]{1,0:T(8,128)(2,1)S(1)} %get-tuple-element.93), channel_id=1, source_target_pairs={{0,16},{16,0},{1,17},{17,1},{2,18},{18,2},{3,19},{19,3},{4,20},{20... | collective-permute-start | bytes 393224 | tf_op jit(solution)/shard_map/ppermute | solution.py:329
  56.0 1.5 %collective-permute-start.18 = (bf16[16,4096]{1,0:T(8,128)(2,1)S(1)}, bf16[16,4096]{1,0:T(8,128)(2,1)S(1)}, u32[]{:S(2)}, u32[]{:S(2)}) collective-permute-start(bf16[16,4096]{1,0:T(8,128)(2,1)S(1)} %get-tuple-element.86), channel_id=1, source_target_pairs={{0,2},{1,3},{2,0},{3,1},{4,6},{5,7},{6,4},{7,5},{8,10},{9,11},{10,... | collective-permute-start | bytes 393224 | tf_op jit(solution)/shard_map/ppermute | solution.py:326
  57.5 4.2 %attend_and_stage.2 = bf16[16,4096]{1,0:T(8,128)(2,1)S(1)} custom-call(s32[32]{0:T(128)S(1)} %copy-done, bf16[32,4096]{1,0:T(8,128)(2,1)} %query_src.3, bf16[32,256,256]{2,1,0:T(8,128)(2,1)} %key_src.3, bf16[32,256,256]{2,1,0:T(8,128)(2,1)} %value_src.3, bf16[32,256]{1,0:T(8,128)(2,1)} %new_key_src.3, bf16[32,256]{1,0:T(8,128)(2,1)} %new_value_src.3), custom_call_target="tpu_custom_call" | custom-call | flops 134217728 | bytes 4194304 | tf_op jit(solution)/shard_map/attend_and_stage/pallas_call | solution.py:131
  61.7 2.7 %collective-permute-done.17 = bf16[16,4096]{1,0:T(8,128)(2,1)S(1)} collective-permute-done((bf16[16,4096]{1,0:T(8,128)(2,1)S(1)}, bf16[16,4096]{1,0:T(8,128)(2,1)S(1)}, u32[]{:S(2)}, u32[]{:S(2)}) %collective-permute-start.17) | collective-permute-done | bytes 131104 | tf_op jit(solution)/shard_map/ppermute | solution.py:329
  64.4 0.2 collective-permute-done.18
  64.7 1.4 %collective-permute-start.21 = (bf16[16,4096]{1,0:T(8,128)(2,1)S(1)}, bf16[16,4096]{1,0:T(8,128)(2,1)S(1)}, u32[]{:S(2)}, u32[]{:S(2)}) collective-permute-start(bf16[16,4096]{1,0:T(8,128)(2,1)S(1)} %add_convert_fusion.5), channel_id=1, source_target_pairs={{0,8},{1,9},{2,10},{3,11},{4,12},{5,13},{6,14},{7,15},{8,0},{9,1},... | collective-permute-start | bytes 393224 | tf_op jit(solution)/shard_map/ppermute | solution.py:326
  66.1 0.1 add_convert_fusion.6
  66.2 1.6 %collective-permute-start.19 = (bf16[16,4096]{1,0:T(8,128)(2,1)S(1)}, bf16[16,4096]{1,0:T(8,128)(2,1)S(1)}, u32[]{:S(2)}, u32[]{:S(2)}) collective-permute-start(bf16[16,4096]{1,0:T(8,128)(2,1)S(1)} %get-tuple-element.91), channel_id=1, source_target_pairs={{0,16},{16,0},{1,17},{17,1},{2,18},{18,2},{3,19},{19,3},{4,20},{20... | collective-permute-start | bytes 393224 | tf_op jit(solution)/shard_map/ppermute | solution.py:329
  67.8 0.5 collective-permute-start.20
  68.4 4.6 %collective-permute-done.21 = bf16[16,4096]{1,0:T(8,128)(2,1)S(1)} collective-permute-done((bf16[16,4096]{1,0:T(8,128)(2,1)S(1)}, bf16[16,4096]{1,0:T(8,128)(2,1)S(1)}, u32[]{:S(2)}, u32[]{:S(2)}) %collective-permute-start.21) | collective-permute-done | bytes 131104 | tf_op jit(solution)/shard_map/ppermute | solution.py:326
  73.0 0.2 collective-permute-start.22
  73.2 2.8 %collective-permute-start.23 = (bf16[16,4096]{1,0:T(8,128)(2,1)S(1)}, bf16[16,4096]{1,0:T(8,128)(2,1)S(1)}, u32[]{:S(2)}, u32[]{:S(2)}) collective-permute-start(bf16[16,4096]{1,0:T(8,128)(2,1)S(1)} %add_convert_fusion.3), channel_id=1, source_target_pairs={{0,12},{1,13},{2,14},{3,15},{4,8},{5,9},{6,10},{7,11},{8,4},{9,5},... | collective-permute-start | bytes 393224 | tf_op jit(solution)/shard_map/ppermute | solution.py:326
  76.0 4.2 %attend_and_stage.3 = bf16[16,4096]{1,0:T(8,128)(2,1)S(1)} custom-call(s32[32]{0:T(128)S(1)} %copy-done, bf16[32,4096]{1,0:T(8,128)(2,1)} %query_src.3, bf16[32,256,256]{2,1,0:T(8,128)(2,1)} %key_src.3, bf16[32,256,256]{2,1,0:T(8,128)(2,1)} %value_src.3, bf16[32,256]{1,0:T(8,128)(2,1)} %new_key_src.3, bf16[32,256]{1,0:T(8,128)(2,1)} %new_value_src.3), custom_call_target="tpu_custom_call" | custom-call | flops 134217728 | bytes 4194304 | tf_op jit(solution)/shard_map/attend_and_stage/pallas_call | solution.py:131
  80.2 0.7 collective-permute-done.23
  81.0 1.4 %collective-permute-start.24 = (bf16[16,4096]{1,0:T(8,128)(2,1)S(1)}, bf16[16,4096]{1,0:T(8,128)(2,1)S(1)}, u32[]{:S(2)}, u32[]{:S(2)}) collective-permute-start(bf16[16,4096]{1,0:T(8,128)(2,1)S(1)} %get-tuple-element.81), channel_id=1, source_target_pairs={{0,16},{16,0},{1,17},{17,1},{2,18},{18,2},{3,19},{19,3},{4,20},{20... | collective-permute-start | bytes 393224 | tf_op jit(solution)/shard_map/ppermute | solution.py:329
  82.4 0.7 pad_maximum_fusion.3
  83.2 2.9 %collective-permute-done.24 = bf16[16,4096]{1,0:T(8,128)(2,1)S(1)} collective-permute-done((bf16[16,4096]{1,0:T(8,128)(2,1)S(1)}, bf16[16,4096]{1,0:T(8,128)(2,1)S(1)}, u32[]{:S(2)}, u32[]{:S(2)}) %collective-permute-start.24) | collective-permute-done | bytes 131104 | tf_op jit(solution)/shard_map/ppermute | solution.py:329
  86.1 0.7 copy-done.1
  (41 shorter events, 0.8 us)
Async XLA Ops:
  1.9 14.2 %collective-permute-start.2 = (bf16[32,4224]{1,0:T(8,128)(2,1)S(1)}, bf16[32,4224]{1,0:T(8,128)(2,1)S(1)}, u32[]{:S(2)}, u32[]{:S(2)}) collective-permute-start(bf16[32,4224]{1,0:T(8,128)(2,1)S(1)} %get-tuple-element.41), channel_id=1, source_target_pairs={{0,2},{1,3},{2,0},{3,1},{4,6},{5,7},{6,4},{7,5},{8,10},{9,11},{10,... | collective-permute-start | bytes 811016 | tf_op jit(solution)/shard_map/ppermute | solution.py:326
  4.9 16.9 %collective-permute-start = (bf16[32,4224]{1,0:T(8,128)(2,1)S(1)}, bf16[32,4224]{1,0:T(8,128)(2,1)S(1)}, u32[]{:S(2)}, u32[]{:S(2)}) collective-permute-start(bf16[32,4224]{1,0:T(8,128)(2,1)S(1)} %get-tuple-element.41), channel_id=1, source_target_pairs={{0,4},{1,5},{2,6},{3,7},{4,0},{5,1},{6,2},{7,3},{8,12},{9,13},{10,... | collective-permute-start | bytes 811016 | tf_op jit(solution)/shard_map/ppermute | solution.py:326
  6.5 9.6 %collective-permute-start.1 = (bf16[16,4224]{1,0:T(8,128)(2,1)S(1)}, bf16[16,4224]{1,0:T(8,128)(2,1)S(1)}, u32[]{:S(2)}, u32[]{:S(2)}) collective-permute-start(bf16[16,4224]{1,0:T(8,128)(2,1)S(1)} %get-tuple-element.42), channel_id=1, source_target_pairs={{0,8},{1,9},{2,10},{3,11},{4,12},{5,13},{6,14},{7,15},{8,0},{9,1},... | collective-permute-start | bytes 405512 | tf_op jit(solution)/shard_map/ppermute | solution.py:326
  16.1 6.5 %collective-permute-start.5 = (bf16[16,4224]{1,0:T(8,128)(2,1)S(1)}, bf16[16,4224]{1,0:T(8,128)(2,1)S(1)}, u32[]{:S(2)}, u32[]{:S(2)}) collective-permute-start(bf16[16,4224]{1,0:T(8,128)(2,1)S(1)} %collective-permute-done.1), channel_id=1, source_target_pairs={{0,16},{16,0},{1,17},{17,1},{2,18},{18,2},{3,19},{19,3},{4,20},{20... | collective-permute-start | bytes 405512 | tf_op jit(solution)/shard_map/ppermute | solution.py:329
  17.7 5.7 %collective-permute-start.6 = (bf16[16,4224]{1,0:T(8,128)(2,1)S(1)}, bf16[16,4224]{1,0:T(8,128)(2,1)S(1)}, u32[]{:S(2)}, u32[]{:S(2)}) collective-permute-start(bf16[16,4224]{1,0:T(8,128)(2,1)S(1)} %collective-permute-done.1), channel_id=1, source_target_pairs={{0,2},{1,3},{2,0},{3,1},{4,6},{5,7},{6,4},{7,5},{8,10},{9,11},{10,... | collective-permute-start | bytes 405512 | tf_op jit(solution)/shard_map/ppermute | solution.py:326
  18.2 6.5 %collective-permute-start.7 = (bf16[16,4224]{1,0:T(8,128)(2,1)S(1)}, bf16[16,4224]{1,0:T(8,128)(2,1)S(1)}, u32[]{:S(2)}, u32[]{:S(2)}) collective-permute-start(bf16[16,4224]{1,0:T(8,128)(2,1)S(1)} %collective-permute-done.1), channel_id=1, source_target_pairs={{0,18},{1,19},{2,16},{3,17},{4,22},{5,23},{6,20},{7,21},{8,26},{9,... | collective-permute-start | bytes 405512 | tf_op jit(solution)/shard_map/ppermute | solution.py:335
  19.7 8.0 %collective-permute-start.3 = (bf16[32,4224]{1,0:T(8,128)(2,1)S(1)}, bf16[32,4224]{1,0:T(8,128)(2,1)S(1)}, u32[]{:S(2)}, u32[]{:S(2)}) collective-permute-start(bf16[32,4224]{1,0:T(8,128)(2,1)S(1)} %collective-permute-done.2), channel_id=1, source_target_pairs={{0,4},{1,5},{2,6},{3,7},{4,0},{5,1},{6,2},{7,3},{8,12},{9,13},{10,... | collective-permute-start | bytes 811016 | tf_op jit(solution)/shard_map/ppermute | solution.py:326
  21.8 11.1 %collective-permute-start.4 = (bf16[16,4224]{1,0:T(8,128)(2,1)S(1)}, bf16[16,4224]{1,0:T(8,128)(2,1)S(1)}, u32[]{:S(2)}, u32[]{:S(2)}) collective-permute-start(bf16[16,4224]{1,0:T(8,128)(2,1)S(1)} %collective-permute-done.1), channel_id=1, source_target_pairs={{0,4},{1,5},{2,6},{3,7},{4,0},{5,1},{6,2},{7,3},{8,12},{9,13},{10,... | collective-permute-start | bytes 405512 | tf_op jit(solution)/shard_map/ppermute | solution.py:326
  24.8 2.9 %collective-permute-start.10 = (bf16[128,4224]{1,0:T(8,128)(2,1)S(1)}, bf16[128,4224]{1,0:T(8,128)(2,1)S(1)}, u32[]{:S(2)}, u32[]{:S(2)}) collective-permute-start(bf16[128,4224]{1,0:T(8,128)(2,1)S(1)} %constant_dynamic-update-slice_fusion.4.refs_0_), channel_id=1, source_target_pairs={{0,1},{1,0},{2,3},{3,2},{4,5},{5,4},{6,7},{7,6},{8,9},{9,8},{10,11... | collective-permute-start | bytes 3244040 | tf_op jit(solution)/shard_map/ppermute | solution.py:326
  24.9 12.9 %collective-permute-start.8 = (bf16[48,4224]{1,0:T(8,128)(2,1)S(1)}, bf16[48,4224]{1,0:T(8,128)(2,1)S(1)}, u32[]{:S(2)}, u32[]{:S(2)}) collective-permute-start(bf16[48,4224]{1,0:T(8,128)(2,1)S(1)} %pad_maximum_fusion), channel_id=1, source_target_pairs={{0,4},{1,5},{2,6},{3,7},{4,0},{5,1},{6,2},{7,3},{8,12},{9,13},{10,... | collective-permute-start | bytes 1216520 | tf_op jit(solution)/shard_map/ppermute | solution.py:326
  32.8 5.1 %collective-permute-start.11 = (bf16[128,4096]{1,0:T(8,128)(2,1)S(1)}, bf16[128,4096]{1,0:T(8,128)(2,1)S(1)}, u32[]{:S(2)}, u32[]{:S(2)}) collective-permute-start(bf16[128,4096]{1,0:T(8,128)(2,1)S(1)} %get-tuple-element.49), channel_id=1, source_target_pairs={{0,1},{1,0},{2,3},{3,2},{4,5},{5,4},{6,7},{7,6},{8,9},{9,8},{10,11... | collective-permute-start | bytes 3145736 | tf_op jit(solution)/shard_map/ppermute | solution.py:326
  37.8 2.8 %collective-permute-start.9 = (bf16[128,4224]{1,0:T(8,128)(2,1)S(1)}, bf16[128,4224]{1,0:T(8,128)(2,1)S(1)}, u32[]{:S(2)}, u32[]{:S(2)}) collective-permute-start(bf16[128,4224]{1,0:T(8,128)(2,1)S(1)} %constant_dynamic-update-slice_fusion.refs_0_), channel_id=1, source_target_pairs={{0,1},{1,0},{2,3},{3,2},{4,5},{5,4},{6,7},{7,6},{8,9},{9,8},{10,11... | collective-permute-start | bytes 3244040 | tf_op jit(solution)/shard_map/ppermute | solution.py:326
  40.6 8.3 %collective-permute-start.12 = (bf16[32,4096]{1,0:T(8,128)(2,1)S(1)}, bf16[32,4096]{1,0:T(8,128)(2,1)S(1)}, u32[]{:S(2)}, u32[]{:S(2)}) collective-permute-start(bf16[32,4096]{1,0:T(8,128)(2,1)S(1)} %pad_maximum_fusion.1), channel_id=1, source_target_pairs={{0,16},{16,0},{1,17},{17,1},{2,18},{18,2},{3,19},{19,3},{4,20},{20... | collective-permute-start | bytes 786440 | tf_op jit(solution)/shard_map/ppermute | solution.py:329
  42.1 8.1 %collective-permute-start.13 = (bf16[32,4096]{1,0:T(8,128)(2,1)S(1)}, bf16[32,4096]{1,0:T(8,128)(2,1)S(1)}, u32[]{:S(2)}, u32[]{:S(2)}) collective-permute-start(bf16[32,4096]{1,0:T(8,128)(2,1)S(1)} %concatenate.33), channel_id=1, source_target_pairs={{0,2},{1,3},{2,0},{3,1},{4,6},{5,7},{6,4},{7,5},{8,10},{9,11},{10,... | collective-permute-start | bytes 786440 | tf_op jit(solution)/shard_map/ppermute | solution.py:326
  50.2 2.7 %collective-permute-start.14 = (bf16[128,4096]{1,0:T(8,128)(2,1)S(1)}, bf16[128,4096]{1,0:T(8,128)(2,1)S(1)}, u32[]{:S(2)}, u32[]{:S(2)}) collective-permute-start(bf16[128,4096]{1,0:T(8,128)(2,1)S(1)} %get-tuple-element.57), channel_id=1, source_target_pairs={{0,1},{1,0},{2,3},{3,2},{4,5},{5,4},{6,7},{7,6},{8,9},{9,8},{10,11... | collective-permute-start | bytes 3145736 | tf_op jit(solution)/shard_map/ppermute | solution.py:326
  53.2 4.3 %copy-start = (s32[32]{0:T(128)S(1)}, s32[32]{0:T(128)}, u32[]{:S(2)}) copy-start(s32[32]{0:T(128)} %lengths_ref.1) | copy-start | bytes 388
  53.2 11.5 %collective-permute-start.15 = (bf16[32,4096]{1,0:T(8,128)(2,1)S(1)}, bf16[32,4096]{1,0:T(8,128)(2,1)S(1)}, u32[]{:S(2)}, u32[]{:S(2)}) collective-permute-start(bf16[32,4096]{1,0:T(8,128)(2,1)S(1)} %pad_maximum_fusion.2), channel_id=1, source_target_pairs={{0,16},{16,0},{1,17},{17,1},{2,18},{18,2},{3,19},{19,3},{4,20},{20... | collective-permute-start | bytes 786440 | tf_op jit(solution)/shard_map/ppermute | solution.py:329
  53.8 10.9 %collective-permute-start.16 = (bf16[32,4096]{1,0:T(8,128)(2,1)S(1)}, bf16[32,4096]{1,0:T(8,128)(2,1)S(1)}, u32[]{:S(2)}, u32[]{:S(2)}) collective-permute-start(bf16[32,4096]{1,0:T(8,128)(2,1)S(1)} %concatenate.34), channel_id=1, source_target_pairs={{0,2},{1,3},{2,0},{3,1},{4,6},{5,7},{6,4},{7,5},{8,10},{9,11},{10,... | collective-permute-start | bytes 786440 | tf_op jit(solution)/shard_map/ppermute | solution.py:326
  54.4 10.0 %collective-permute-start.17 = (bf16[16,4096]{1,0:T(8,128)(2,1)S(1)}, bf16[16,4096]{1,0:T(8,128)(2,1)S(1)}, u32[]{:S(2)}, u32[]{:S(2)}) collective-permute-start(bf16[16,4096]{1,0:T(8,128)(2,1)S(1)} %get-tuple-element.93), channel_id=1, source_target_pairs={{0,16},{16,0},{1,17},{17,1},{2,18},{18,2},{3,19},{19,3},{4,20},{20... | collective-permute-start | bytes 393224 | tf_op jit(solution)/shard_map/ppermute | solution.py:329
  56.0 8.6 %collective-permute-start.18 = (bf16[16,4096]{1,0:T(8,128)(2,1)S(1)}, bf16[16,4096]{1,0:T(8,128)(2,1)S(1)}, u32[]{:S(2)}, u32[]{:S(2)}) collective-permute-start(bf16[16,4096]{1,0:T(8,128)(2,1)S(1)} %get-tuple-element.86), channel_id=1, source_target_pairs={{0,2},{1,3},{2,0},{3,1},{4,6},{5,7},{6,4},{7,5},{8,10},{9,11},{10,... | collective-permute-start | bytes 393224 | tf_op jit(solution)/shard_map/ppermute | solution.py:326
  64.7 8.3 %collective-permute-start.21 = (bf16[16,4096]{1,0:T(8,128)(2,1)S(1)}, bf16[16,4096]{1,0:T(8,128)(2,1)S(1)}, u32[]{:S(2)}, u32[]{:S(2)}) collective-permute-start(bf16[16,4096]{1,0:T(8,128)(2,1)S(1)} %add_convert_fusion.5), channel_id=1, source_target_pairs={{0,8},{1,9},{2,10},{3,11},{4,12},{5,13},{6,14},{7,15},{8,0},{9,1},... | collective-permute-start | bytes 393224 | tf_op jit(solution)/shard_map/ppermute | solution.py:326
  66.2 6.7 %collective-permute-start.19 = (bf16[16,4096]{1,0:T(8,128)(2,1)S(1)}, bf16[16,4096]{1,0:T(8,128)(2,1)S(1)}, u32[]{:S(2)}, u32[]{:S(2)}) collective-permute-start(bf16[16,4096]{1,0:T(8,128)(2,1)S(1)} %get-tuple-element.91), channel_id=1, source_target_pairs={{0,16},{16,0},{1,17},{17,1},{2,18},{18,2},{3,19},{19,3},{4,20},{20... | collective-permute-start | bytes 393224 | tf_op jit(solution)/shard_map/ppermute | solution.py:329
  67.8 5.1 %collective-permute-start.20 = (bf16[16,4096]{1,0:T(8,128)(2,1)S(1)}, bf16[16,4096]{1,0:T(8,128)(2,1)S(1)}, u32[]{:S(2)}, u32[]{:S(2)}) collective-permute-start(bf16[16,4096]{1,0:T(8,128)(2,1)S(1)} %get-tuple-element.82), channel_id=1, source_target_pairs={{0,2},{1,3},{2,0},{3,1},{4,6},{5,7},{6,4},{7,5},{8,10},{9,11},{10,... | collective-permute-start | bytes 393224 | tf_op jit(solution)/shard_map/ppermute | solution.py:326
  73.0 7.2 %collective-permute-start.22 = (bf16[16,4096]{1,0:T(8,128)(2,1)S(1)}, bf16[16,4096]{1,0:T(8,128)(2,1)S(1)}, u32[]{:S(2)}, u32[]{:S(2)}) collective-permute-start(bf16[16,4096]{1,0:T(8,128)(2,1)S(1)} %add_convert_fusion.4), channel_id=1, source_target_pairs={{0,4},{1,5},{2,6},{3,7},{4,0},{5,1},{6,2},{7,3},{8,12},{9,13},{10,... | collective-permute-start | bytes 393224 | tf_op jit(solution)/shard_map/ppermute | solution.py:326
  73.2 7.7 %collective-permute-start.23 = (bf16[16,4096]{1,0:T(8,128)(2,1)S(1)}, bf16[16,4096]{1,0:T(8,128)(2,1)S(1)}, u32[]{:S(2)}, u32[]{:S(2)}) collective-permute-start(bf16[16,4096]{1,0:T(8,128)(2,1)S(1)} %add_convert_fusion.3), channel_id=1, source_target_pairs={{0,12},{1,13},{2,14},{3,15},{4,8},{5,9},{6,10},{7,11},{8,4},{9,5},... | collective-permute-start | bytes 393224 | tf_op jit(solution)/shard_map/ppermute | solution.py:326
  81.0 5.0 %collective-permute-start.24 = (bf16[16,4096]{1,0:T(8,128)(2,1)S(1)}, bf16[16,4096]{1,0:T(8,128)(2,1)S(1)}, u32[]{:S(2)}, u32[]{:S(2)}) collective-permute-start(bf16[16,4096]{1,0:T(8,128)(2,1)S(1)} %get-tuple-element.81), channel_id=1, source_target_pairs={{0,16},{16,0},{1,17},{17,1},{2,18},{18,2},{3,19},{19,3},{4,20},{20... | collective-permute-start | bytes 393224 | tf_op jit(solution)/shard_map/ppermute | solution.py:329
  86.1 0.7 copy-start.1
